TPU v7x, 32 devices: a whole 2x2x4 slice. The times are simulated.
32 devices in a mesh: seq: 2 (over y), fsdp: 16 (over z, x, core).
Axes of the slice: x: 2, y: 2, z: 4, core: 2. Of those that a mesh axis runs over, the one named last changes fastest.
Arguments:
- tokens: bfloat16 [8192, 2048], P(('fsdp', 'seq')), may hold values from -6 to 6
- attn_gain: bfloat16 [2048], P(('seq', 'fsdp')), may hold values from 0.5 to 1.5
- w_query: bfloat16 [2048, 1024], P(('seq', 'fsdp')), may hold values from -0.125 to 0.125
- w_key: bfloat16 [2048, 1024], P(('seq', 'fsdp')), may hold values from -0.125 to 0.125
- w_value: bfloat16 [2048, 2048], P(('seq', 'fsdp')), may hold values from -0.125 to 0.125
- w_down_rank: bfloat16 [2048, 16], P(('seq', 'fsdp')), may hold values from -0.125 to 0.125
- w_up_rank: bfloat16 [16, 1024], P(None, ('seq', 'fsdp')), may hold values from -1.5 to 1.5
- gate_bias: bfloat16 [1024], P(('seq', 'fsdp')), may hold values from -1 to 11
- w_outgate: bfloat16 [2048, 2048], P(('seq', 'fsdp')), may hold values from -0.125 to 0.125
- head_gain: bfloat16 [512], P(('seq', 'fsdp')), may hold values from 0.5 to 1.5
- w_output: bfloat16 [2048, 2048], P(('seq', 'fsdp')), may hold values from -0.25 to 0.25
- ffn_gain: bfloat16 [2048], P(('seq', 'fsdp')), may hold values from 0.5 to 1.5
- w_gate: bfloat16 [2048, 5632], P(('seq', 'fsdp')), may hold values from -0.125 to 0.125
- w_up: bfloat16 [2048, 5632], P(('seq', 'fsdp')), may hold values from -0.125 to 0.125
- w_down: bfloat16 [5632, 2048], P(('seq', 'fsdp')), may hold values from -0.15625 to 0.15625
- doc_starts: int32 [32], P('fsdp'), may hold values from 0 to 256, as said below
- cotangent: bfloat16 [8192, 2048], P(('fsdp', 'seq')), may hold values from -6 to 6
Outputs:
- layer_output: bfloat16 [8192, 2048], P(('fsdp', 'seq'))
- input_grad: bfloat16 [8192, 2048], P(('fsdp', 'seq'))
- attn_gain_grad: float32 [2048], P(('seq', 'fsdp'))
- w_query_grad: float32 [2048, 1024], P(('seq', 'fsdp'))
- w_key_grad: float32 [2048, 1024], P(('seq', 'fsdp'))
- w_value_grad: float32 [2048, 2048], P(('seq', 'fsdp'))
- w_down_rank_grad: float32 [2048, 16], P(('seq', 'fsdp'))
- w_up_rank_grad: float32 [16, 1024], P(None, ('seq', 'fsdp'))
- gate_bias_grad: float32 [1024], P(('seq', 'fsdp'))
- w_outgate_grad: float32 [2048, 2048], P(('seq', 'fsdp'))
- head_gain_grad: float32 [512], P(('seq', 'fsdp'))
- w_output_grad: float32 [2048, 2048], P(('seq', 'fsdp'))
- ffn_gain_grad: float32 [2048], P(('seq', 'fsdp'))
- w_gate_grad: float32 [2048, 5632], P(('seq', 'fsdp'))
- w_up_grad: float32 [2048, 5632], P(('seq', 'fsdp'))
- w_down_grad: float32 [5632, 2048], P(('seq', 'fsdp'))
Inputs may be any that keep to these rules, and one draw needn't show every extreme that they name: `doc_starts`: segment 0 holds a document start after its first token, segment 32 - 1 holds one, no other segment holds one.
All inputs are finite; a program needn't handle non-finite values.
Results may differ from a plain program's by a relative error of at most 0.025.
The roundings to bfloat16 on the way count: a program that leaves them out, or rounds other values in their place, can miss the bound.
Values may be sent and summed in bfloat16 or wider, within the bound.
No kernel may reach another device: no remote copies, remote signals or barrier semaphores. Data moves between devices by JAX's collectives and lax.ppermute only.
A program may use at most 448 MiB of HBM per device.

v0:
```python
from functools import partial

import jax
import jax.numpy as jnp
from jax import lax
from jax.sharding import PartitionSpec as P

SPAN = 64
HK = 256
HV = 512


epsilon = 1e-06
gate_scale = 16.0


def entering(shard, axis, combine, identity, reverse):
    count, position = (lax.axis_size(axis), lax.axis_index(axis))
    everything = jax.tree.map(lambda part: lax.all_gather(part, axis), shard)
    start = jax.tree.map(
        lambda part, zero: jnp.broadcast_to(jnp.asarray(zero, part.dtype), part.shape),
        shard,
        identity,
    )

    def step(k, before):
        at = count - 1 - k if reverse else k
        reached = at > position if reverse else at < position
        new = combine(before, jax.tree.map(lambda part: part[at], everything))
        return jax.tree.map(lambda a, b: jnp.where(reached, a, b), new, before)

    return lax.fori_loop(0, count, step, start)


def exact_dot(left, right):
    return jnp.dot(left, right, precision=lax.Precision.HIGHEST)


def precise_einsum(form, left, right):
    return jnp.einsum(form, left, right, precision=lax.Precision.HIGHEST)


def plain_dot(left, right):
    return jnp.dot(left, right, preferred_element_type=jnp.float32)


def inner_rows(left, right):
    return lax.dot_general(
        left, right, (((0,), (0,)), ((), ())), preferred_element_type=jnp.float32
    )


def outer_cols(left, right):
    return lax.dot_general(
        left, right, (((1,), (1,)), ((), ())), preferred_element_type=jnp.float32
    )


def norm_rows(value_rows, gain):
    return (
        value_rows
        * lax.rsqrt(jnp.mean(value_rows * value_rows, axis=-1, keepdims=True) + epsilon)
        * gain
    )


def head_norm(value_rows, gain):
    shaped = value_rows.reshape(value_rows.shape[0], -1, HV)
    scaled = shaped * lax.rsqrt(jnp.mean(shaped * shaped, axis=-1, keepdims=True) + epsilon) * gain
    return scaled.reshape(value_rows.shape)


def span_step(carried_in, pieces):
    carried_state, offset, reset_seen = carried_in
    queries, keys_in, value_rows, decays, starts_flag = pieces
    length = starts_flag.shape[0]
    causal = (
        lax.broadcasted_iota(jnp.int32, (length, length), 0)
        >= lax.broadcasted_iota(jnp.int32, (length, length), 1)
    ).astype(jnp.float32)
    running = precise_einsum("ts,hsk->htk", causal, decays)
    doc_count = exact_dot(causal, starts_flag)
    expanded_rows = queries * jnp.exp(running)
    shrunk = keys_in * jnp.exp(-running)
    score_matrix = precise_einsum("htk,hsk->hts", expanded_rows, shrunk)
    same_doc = (doc_count[:, None] == doc_count[None, :]) & (causal > 0)
    score_matrix = jnp.where(same_doc[None, :, :], score_matrix, 0.0)
    unfinished_rows = doc_count == 0.0
    output_rows = precise_einsum("xbe,xeg->xbg", score_matrix, value_rows) + jnp.where(
        unfinished_rows[None, :, None],
        precise_einsum("cze,cer->czr", expanded_rows, carried_state),
        0.0,
    )
    closing_sum = running[:, -1, :]
    tail_rows = doc_count == doc_count[-1]
    ending_flags = jnp.where(
        tail_rows[None, :, None], keys_in * jnp.exp(closing_sum[:, None, :] - running), 0.0
    )
    unbroken_mask = doc_count[-1] == 0.0
    next_carried_state = jnp.where(
        unbroken_mask, jnp.exp(closing_sum)[:, :, None] * carried_state, 0.0
    ) + precise_einsum("deo,dew->dow", ending_flags, value_rows)
    reach_rows = unfinished_rows & (reset_seen == 0.0)
    reach_decay = jnp.where(
        reach_rows[None, :, None], queries * jnp.exp(offset[:, None, :] + running), 0.0
    )
    seen_next = jnp.maximum(reset_seen, jnp.where(unbroken_mask, 0.0, 1.0))
    return ((next_carried_state, offset + closing_sum, seen_next), (output_rows, reach_decay))


def mixer_parts(queries, keys_in, value_rows, logits, starts_flag):
    group_length = queries.shape[0]
    heads_here = queries.shape[1] // HK
    spans = group_length // SPAN

    def to_blocks(array, width):
        return array.reshape(spans, SPAN, heads_here, width).transpose(0, 2, 1, 3)

    decays = jax.nn.log_sigmoid(logits) / gate_scale
    initial = (
        jnp.zeros((heads_here, HK, HV), jnp.float32),
        jnp.zeros((heads_here, HK), jnp.float32),
        jnp.zeros((), jnp.float32),
    )
    pieces = (
        to_blocks(queries, HK) * HK ** (-0.5),
        to_blocks(keys_in, HK),
        to_blocks(value_rows, HV),
        to_blocks(decays, HK),
        starts_flag.reshape(spans, SPAN),
    )
    final_carry, (output_rows, reach_decay) = lax.scan(span_step, initial, pieces)
    local_end, offset, reset_seen = final_carry
    through = jnp.exp(offset) * (1.0 - reset_seen)
    local_output = output_rows.transpose(0, 2, 1, 3).reshape(group_length, heads_here * HV)
    reach_decay = reach_decay.transpose(1, 0, 2, 3).reshape(heads_here, group_length, HK)
    return (local_output, reach_decay, local_end, through)


def carry_combine(earlier, later):
    return (earlier[0] * later[0], later[0][:, :, None] * earlier[1] + later[1])


def return_combine(earlier, later):
    return (earlier[0] * later[0], later[1] + later[0][:, :, None] * earlier[1])


def on_device(
    tokens,
    attn_gain,
    w_query,
    w_key,
    w_value,
    w_down_rank,
    w_up_rank,
    gate_bias,
    w_outgate,
    head_gain,
    w_output,
    ffn_gain,
    w_gate,
    w_up,
    w_down,
    doc_starts,
    cotangent,
):
    gathered = (
        lax.all_gather(attn_gain, ("seq", "fsdp"), axis=0, tiled=True),
        lax.all_gather(w_query, ("seq", "fsdp"), axis=0, tiled=True),
        lax.all_gather(w_key, ("seq", "fsdp"), axis=0, tiled=True),
        lax.all_gather(w_value, ("seq", "fsdp"), axis=0, tiled=True),
        lax.all_gather(w_down_rank, ("seq", "fsdp"), axis=0, tiled=True),
        lax.all_gather(w_up_rank, ("seq", "fsdp"), axis=1, tiled=True),
        lax.all_gather(gate_bias, ("seq", "fsdp"), axis=0, tiled=True),
        lax.all_gather(w_outgate, ("seq", "fsdp"), axis=0, tiled=True),
        lax.all_gather(head_gain, ("seq", "fsdp"), axis=0, tiled=True),
        lax.all_gather(w_output, ("seq", "fsdp"), axis=0, tiled=True),
        lax.all_gather(ffn_gain, ("seq", "fsdp"), axis=0, tiled=True),
        lax.all_gather(w_gate, ("seq", "fsdp"), axis=0, tiled=True),
        lax.all_gather(w_up, ("seq", "fsdp"), axis=0, tiled=True),
        lax.all_gather(w_down, ("seq", "fsdp"), axis=0, tiled=True),
    )
    (
        full_attn_gain,
        full_query,
        full_key,
        full_value,
        full_down_rank,
        full_up_rank,
        full_bias,
        full_outgate,
        full_head_gain,
        full_output,
        full_ffn_gain,
        full_gate,
        full_up,
        full_down,
    ) = gathered
    inputs = tokens.astype(jnp.float32)
    normed_in, input_pull = jax.vjp(norm_rows, inputs, full_attn_gain.astype(jnp.float32))
    normed_low = normed_in.astype(jnp.bfloat16)
    queries = plain_dot(normed_low, full_query).astype(jnp.bfloat16)
    keys_in = plain_dot(normed_low, full_key).astype(jnp.bfloat16)
    value_rows = plain_dot(normed_low, full_value).astype(jnp.bfloat16)
    rank_low = plain_dot(normed_low, full_down_rank).astype(jnp.bfloat16)
    logits = (plain_dot(rank_low, full_up_rank) + full_bias.astype(jnp.float32)).astype(
        jnp.bfloat16
    )
    outgate = plain_dot(normed_low, full_outgate)
    head_query, head_key, head_value, head_logit = (
        lax.all_to_all(queries, "seq", split_axis=1, concat_axis=0, tiled=True),
        lax.all_to_all(keys_in, "seq", split_axis=1, concat_axis=0, tiled=True),
        lax.all_to_all(value_rows, "seq", split_axis=1, concat_axis=0, tiled=True),
        lax.all_to_all(logits, "seq", split_axis=1, concat_axis=0, tiled=True),
    )
    group_length = head_query.shape[0]
    seg_len = tokens.shape[0]
    starts_flag = (
        (jnp.arange(seg_len, dtype=jnp.int32)[None, :] == doc_starts[:, None])
        .astype(jnp.float32)
        .reshape(group_length)
    )
    parts, mixer_pull = jax.vjp(
        partial(mixer_parts, starts_flag=starts_flag),
        head_query.astype(jnp.float32),
        head_key.astype(jnp.float32),
        head_value.astype(jnp.float32),
        head_logit.astype(jnp.float32),
    )
    local_output, reach_decay, local_end, through = parts
    prefix_decay, incoming_state = entering(
        (through, local_end),
        "fsdp",
        carry_combine,
        (jnp.ones_like(through), jnp.zeros_like(local_end)),
        False,
    )
    mixed_tokens = local_output + precise_einsum(
        "led,ldf->elf", reach_decay, incoming_state
    ).reshape(group_length, -1)
    mixed_tok = lax.all_to_all(
        mixed_tokens.astype(jnp.bfloat16), "seq", split_axis=0, concat_axis=1, tiled=True
    )
    normed_mix, head_pull = jax.vjp(
        head_norm, mixed_tok.astype(jnp.float32), full_head_gain.astype(jnp.float32)
    )
    gate_act = jax.nn.silu(outgate)
    gated_low = (normed_mix * gate_act).astype(jnp.bfloat16)
    resid = inputs + plain_dot(gated_low, full_output)
    normed_mid, mid_pull = jax.vjp(norm_rows, resid, full_ffn_gain.astype(jnp.float32))
    mid_low = normed_mid.astype(jnp.bfloat16)
    gate_pre = plain_dot(mid_low, full_gate)
    up_pre = plain_dot(mid_low, full_up)
    gate_sig = jax.nn.sigmoid(gate_pre)
    silu_gate = gate_pre * gate_sig
    hidden_low = (silu_gate * up_pre).astype(jnp.bfloat16)
    layer_output = (resid + plain_dot(hidden_low, full_down)).astype(jnp.bfloat16)
    (
        back_query,
        back_key,
        back_value,
        back_down_rank,
        back_up_rank,
        back_outgate,
        back_output,
        back_gate,
        back_up,
        back_down,
    ) = (
        lax.all_gather(w_query, ("seq", "fsdp"), axis=0, tiled=True),
        lax.all_gather(w_key, ("seq", "fsdp"), axis=0, tiled=True),
        lax.all_gather(w_value, ("seq", "fsdp"), axis=0, tiled=True),
        lax.all_gather(w_down_rank, ("seq", "fsdp"), axis=0, tiled=True),
        lax.all_gather(w_up_rank, ("seq", "fsdp"), axis=1, tiled=True),
        lax.all_gather(w_outgate, ("seq", "fsdp"), axis=0, tiled=True),
        lax.all_gather(w_output, ("seq", "fsdp"), axis=0, tiled=True),
        lax.all_gather(w_gate, ("seq", "fsdp"), axis=0, tiled=True),
        lax.all_gather(w_up, ("seq", "fsdp"), axis=0, tiled=True),
        lax.all_gather(w_down, ("seq", "fsdp"), axis=0, tiled=True),
    )
    down_term = inner_rows(hidden_low, cotangent)
    hidden_grad = outer_cols(cotangent, back_down)
    gate_grad = (hidden_grad * up_pre * (gate_sig * (1.0 + gate_pre * (1.0 - gate_sig)))).astype(
        jnp.bfloat16
    )
    up_grad = (hidden_grad * silu_gate).astype(jnp.bfloat16)
    gate_term = inner_rows(mid_low, gate_grad)
    up_term = inner_rows(mid_low, up_grad)
    mid_grad = outer_cols(gate_grad, back_gate) + outer_cols(up_grad, back_up)
    resid_part, ffn_gain_term = mid_pull(mid_grad)
    resid_grad = cotangent.astype(jnp.float32) + resid_part
    ffn_grads = (
        lax.psum_scatter(ffn_gain_term, ("seq", "fsdp"), scatter_dimension=0, tiled=True),
        lax.psum_scatter(gate_term, ("seq", "fsdp"), scatter_dimension=0, tiled=True),
        lax.psum_scatter(up_term, ("seq", "fsdp"), scatter_dimension=0, tiled=True),
        lax.psum_scatter(down_term, ("seq", "fsdp"), scatter_dimension=0, tiled=True),
    )
    branch_low = resid_grad.astype(jnp.bfloat16)
    output_term = inner_rows(gated_low, branch_low)
    gated_grad = outer_cols(branch_low, back_output)
    outgate_sig = jax.nn.sigmoid(outgate)
    outgate_grad = (
        gated_grad * normed_mix * outgate_sig * (1.0 + outgate * (1.0 - outgate_sig))
    ).astype(jnp.bfloat16)
    mixed_grad, head_gain_term = head_pull(gated_grad * gate_act)
    head_grad = lax.all_to_all(
        mixed_grad.astype(jnp.bfloat16), "seq", split_axis=1, concat_axis=0, tiled=True
    ).astype(jnp.float32)
    heads_here = reach_decay.shape[0]
    reshaped_gradient = head_grad.reshape(group_length, heads_here, HV)
    state_gradient = precise_einsum("swi,wsa->sia", reach_decay, reshaped_gradient)
    reach_decay_gradient = precise_einsum("urx,rox->ruo", reshaped_gradient, incoming_state)
    prefix_back, later_grad = entering(
        (through, state_gradient),
        "fsdp",
        return_combine,
        (jnp.ones_like(through), jnp.zeros_like(state_gradient)),
        True,
    )
    through_grad = jnp.sum(later_grad * incoming_state, axis=-1)
    query_grad, key_grad, value_grad, logit_grad = mixer_pull(
        (head_grad, reach_decay_gradient, later_grad, through_grad)
    )
    query_back, key_back, value_back, logit_back = (
        lax.all_to_all(
            query_grad.astype(jnp.bfloat16), "seq", split_axis=0, concat_axis=1, tiled=True
        ),
        lax.all_to_all(
            key_grad.astype(jnp.bfloat16), "seq", split_axis=0, concat_axis=1, tiled=True
        ),
        lax.all_to_all(
            value_grad.astype(jnp.bfloat16), "seq", split_axis=0, concat_axis=1, tiled=True
        ),
        lax.all_to_all(
            logit_grad.astype(jnp.bfloat16), "seq", split_axis=0, concat_axis=1, tiled=True
        ),
    )
    bias_term = jnp.sum(logit_back.astype(jnp.float32), axis=0)
    up_rank_term = inner_rows(rank_low, logit_back)
    rank_grad = outer_cols(logit_back, back_up_rank).astype(jnp.bfloat16)
    down_rank_term = inner_rows(normed_low, rank_grad)
    query_term = inner_rows(normed_low, query_back)
    key_term = inner_rows(normed_low, key_back)
    value_term = inner_rows(normed_low, value_back)
    outgate_term = inner_rows(normed_low, outgate_grad)
    in_grad = (
        outer_cols(query_back, back_query)
        + outer_cols(key_back, back_key)
        + outer_cols(value_back, back_value)
    )
    in_grad = (
        in_grad + outer_cols(rank_grad, back_down_rank) + outer_cols(outgate_grad, back_outgate)
    )
    input_part, attn_gain_term = input_pull(in_grad)
    input_grad = (resid_grad + input_part).astype(jnp.bfloat16)
    mixer_grads = (
        lax.psum_scatter(attn_gain_term, ("seq", "fsdp"), scatter_dimension=0, tiled=True),
        lax.psum_scatter(query_term, ("seq", "fsdp"), scatter_dimension=0, tiled=True),
        lax.psum_scatter(key_term, ("seq", "fsdp"), scatter_dimension=0, tiled=True),
        lax.psum_scatter(value_term, ("seq", "fsdp"), scatter_dimension=0, tiled=True),
        lax.psum_scatter(down_rank_term, ("seq", "fsdp"), scatter_dimension=0, tiled=True),
        lax.psum_scatter(up_rank_term, ("seq", "fsdp"), scatter_dimension=1, tiled=True),
        lax.psum_scatter(bias_term, ("seq", "fsdp"), scatter_dimension=0, tiled=True),
        lax.psum_scatter(outgate_term, ("seq", "fsdp"), scatter_dimension=0, tiled=True),
        lax.psum_scatter(head_gain_term, ("seq", "fsdp"), scatter_dimension=0, tiled=True),
        lax.psum_scatter(output_term, ("seq", "fsdp"), scatter_dimension=0, tiled=True),
    )
    return (
        layer_output,
        input_grad,
        mixer_grads[0],
        mixer_grads[1],
        mixer_grads[2],
        mixer_grads[3],
        mixer_grads[4],
        mixer_grads[5],
        mixer_grads[6],
        mixer_grads[7],
        mixer_grads[8],
        mixer_grads[9],
        ffn_grads[0],
        ffn_grads[1],
        ffn_grads[2],
        ffn_grads[3],
    )


def solution(mesh):
    in_specs = (
        P(("fsdp", "seq"), None),
        P(("seq", "fsdp")),
        P(("seq", "fsdp"), None),
        P(("seq", "fsdp"), None),
        P(("seq", "fsdp"), None),
        P(("seq", "fsdp"), None),
        P(None, ("seq", "fsdp")),
        P(("seq", "fsdp")),
        P(("seq", "fsdp"), None),
        P(("seq", "fsdp")),
        P(("seq", "fsdp"), None),
        P(("seq", "fsdp")),
        P(("seq", "fsdp"), None),
        P(("seq", "fsdp"), None),
        P(("seq", "fsdp"), None),
        P("fsdp"),
        P(("fsdp", "seq"), None),
    )
    out_specs = (
        P(("fsdp", "seq"), None),
        P(("fsdp", "seq"), None),
        P(("seq", "fsdp")),
        P(("seq", "fsdp"), None),
        P(("seq", "fsdp"), None),
        P(("seq", "fsdp"), None),
        P(("seq", "fsdp"), None),
        P(None, ("seq", "fsdp")),
        P(("seq", "fsdp")),
        P(("seq", "fsdp"), None),
        P(("seq", "fsdp")),
        P(("seq", "fsdp"), None),
        P(("seq", "fsdp")),
        P(("seq", "fsdp"), None),
        P(("seq", "fsdp"), None),
        P(("seq", "fsdp"), None),
    )
    return jax.shard_map(
        on_device, mesh=mesh, in_specs=in_specs, out_specs=out_specs, check_vma=False
    )
```

profile of v0, /device:TPU:0, one launch (start us, length us, event | category | flops | bytes accessed | tf_op | source)
XLA Modules:
  0.0 4250.1 jit_solution(7449455289546220834)
XLA Ops:
  9.4 44.1 %all-gather.3 = bf16[32,64,16]{1,2,0:T(8,128)(2,1)S(1)} all-gather(bf16[1,64,16]{1,2,0:T(8,128)(2,1)} %bitcast.665), channel_id=1, replica_groups=mesh['seq'=2,'fsdp'=16] {'seq','fsdp'}, dimensions={0}, use_global_device_ids=true | all-gather | bytes 67584 | tf_op jit(solution)/shard_map/all_gather | solution.py:172
  57.2 37.4 all-reduce.10
  94.6 42.1 all-gather.4
  183.1 36.1 all-gather.19.cloned.1.call-done
  262.7 210.8 %while.116 = (s32[]{:T(128)}, f32[2,256,512]{2,1,0:T(8,128)S(1)}, f32[2,256]{1,0:T(2,128)}, f32[]{:T(128)}, f32[8,2,64,512]{3,2,1,0:T(8,128)}, /*index=5*/f32[8,...) while((s32[]{:T(128)}, f32[2,256,512]{2,1,0:T(8,128)S(1)}, ...), condition=%wide.region_2.3_spmd.clone.clone.clone, body=%wide.region_1.2_spmd.clone.clone.sunk.clone | while | flops 505672896 | bytes 10185855 | solution.py:132
  486.7 20.5 all-gather.5
  507.2 93.2 %all-gather.33.cloned.1.call-done = f32[32,256,512]{2,1,0:T(8,128)} async-done(((f32[2,256,512]{2,1,0:T(8,128)}), f32[32,256,512]{2,1,0:T(8,128)}) %all-gather.33.cloned.1.call-update) | async-done | bytes 16777232 | tf_op jit(solution)/shard_map/all_gather | solution.py:19
  600.3 24.6 while.114
  645.1 22.6 all-to-all-done.4
  695.7 67.7 %all-gather.25.cloned.1.call-done = bf16[2048,2048]{1,0:T(8,128)(2,1)} async-done(((bf16[64,2048]{1,0:T(8,128)(2,1)}), bf16[2048,2048]{1,0:T(8,128)(2,1)}) %all-gather.25.cloned.1.call-update) | async-done | bytes 8388624 | tf_op jit(solution)/shard_map/all_gather | solution.py:177
  770.9 138.7 %all-gather.27.cloned.1.call-done = bf16[2048,5632]{1,0:T(8,128)(2,1)} async-done(((bf16[64,5632]{1,0:T(8,128)(2,1)}), bf16[2048,5632]{1,0:T(8,128)(2,1)}) %all-gather.27.cloned.1.call-update) | async-done | bytes 23068688 | tf_op jit(solution)/shard_map/all_gather | solution.py:179
  922.7 132.6 %all-gather.29.cloned.1.call-done = bf16[2048,5632]{1,0:T(8,128)(2,1)} async-done(((bf16[64,5632]{1,0:T(8,128)(2,1)}), bf16[2048,5632]{1,0:T(8,128)(2,1)}) %all-gather.29.cloned.1.call-update) | async-done | bytes 23068688 | tf_op jit(solution)/shard_map/all_gather | solution.py:180
  1068.4 132.6 %all-gather.31.cloned.1.call-done = bf16[5632,2048]{1,0:T(8,128)(2,1)} async-done(((bf16[176,2048]{1,0:T(8,128)(2,1)}), bf16[5632,2048]{1,0:T(8,128)(2,1)}) %all-gather.31.cloned.1.call-update) | async-done | bytes 23068688 | tf_op jit(solution)/shard_map/all_gather | solution.py:181
  1201.0 18.9 multiply_convert_fusion
  1269.3 17.6 all_to_all.142
  1303.5 113.8 %all-gather.35.cloned.1.call-done = f32[32,256,512]{2,1,0:T(8,128)} async-done(((f32[2,256,512]{2,1,0:T(8,128)}), f32[32,256,512]{2,1,0:T(8,128)}) %all-gather.35.cloned.1.call-update) | async-done | bytes 16777232 | tf_op jit(solution)/shard_map/all_gather | solution.py:19
  1417.3 24.6 while.115
  1443.3 191.6 %while.113 = (s32[]{:T(128)}, f32[2,256,512]{2,1,0:T(8,128)S(1)}, f32[2,256]{1,0:T(2,128)S(1)}, f32[8,2,64,256]{3,2,1,0:T(8,128)S(1)}, bf16[8,2,64,256]{3,2,1,0:...) while((s32[]{:T(128)}, f32[2,256,512]{2,1,0:T(8,128)S(1)}, ...), condition=%wide.region_16.17_spmd.clone.clone, body=%wide.region_12.16_spmd.clone.sunk.clone | while | flops 984171008 | bytes 15041320 | solution.py:132
  1714.0 15.5 all_to_all.146
  1740.6 19.7 fusion.151
  1760.3 19.7 fusion.152
  1781.3 19.7 fusion.153
  1828.2 91.7 %reduce-scatter.31.cloned.1.call-done = f32[64,16]{1,0:T(8,128)} async-done(((f32[2048,16]{1,0:T(8,128)}), f32[64,16]{1,0:T(8,128)}) %reduce-scatter.31.cloned.1.call-update) | async-done | bytes 4112
  1930.4 40.8 all-reduce.9
  1976.7 127.8 %reduce-scatter.21.cloned.1.call-done = f32[64,2048]{1,0:T(8,128)} async-done(((f32[2048,2048]{1,0:T(8,128)}), f32[64,2048]{1,0:T(8,128)}) %reduce-scatter.21.cloned.1.call-update) | async-done | bytes 524304 | tf_op jit(solution)/shard_map/reduce_scatter | solution.py:364
  2104.5 184.2 %reduce-scatter.23.cloned.1.call-done = f32[64,2048]{1,0:T(8,128)} async-done(((f32[2048,2048]{1,0:T(8,128)}), f32[64,2048]{1,0:T(8,128)}) %reduce-scatter.23.cloned.1.call-update) | async-done | bytes 524304 | tf_op jit(solution)/shard_map/reduce_scatter | solution.py:366
  2288.7 154.3 %reduce-scatter.15.cloned.1.call-done = f32[64,1024]{1,0:T(8,128)} async-done(((f32[2048,1024]{1,0:T(8,128)}), f32[64,1024]{1,0:T(8,128)}) %reduce-scatter.15.cloned.1.call-update) | async-done | bytes 262160 | tf_op jit(solution)/shard_map/reduce_scatter | solution.py:358
  2442.9 148.2 %reduce-scatter.17.cloned.1.call-done = f32[64,1024]{1,0:T(8,128)} async-done(((f32[2048,1024]{1,0:T(8,128)}), f32[64,1024]{1,0:T(8,128)}) %reduce-scatter.17.cloned.1.call-update) | async-done | bytes 262160 | tf_op jit(solution)/shard_map/reduce_scatter | solution.py:359
  2591.1 180.4 %reduce-scatter.19.cloned.1.call-done = f32[64,2048]{1,0:T(8,128)} async-done(((f32[2048,2048]{1,0:T(8,128)}), f32[64,2048]{1,0:T(8,128)}) %reduce-scatter.19.cloned.1.call-update) | async-done | bytes 524304 | tf_op jit(solution)/shard_map/reduce_scatter | solution.py:360
  2771.5 488.9 %reduce-scatter.25.cloned.1.call-done = f32[64,5632]{1,0:T(8,128)} async-done(((f32[2048,5632]{1,0:T(8,128)}), f32[64,5632]{1,0:T(8,128)}) %reduce-scatter.25.cloned.1.call-update) | async-done | bytes 1441808 | tf_op jit(solution)/shard_map/reduce_scatter | solution.py:294
  3260.4 491.4 %reduce-scatter.27.cloned.1.call-done = f32[64,5632]{1,0:T(8,128)} async-done(((f32[2048,5632]{1,0:T(8,128)}), f32[64,5632]{1,0:T(8,128)}) %reduce-scatter.27.cloned.1.call-update) | async-done | bytes 1441808 | tf_op jit(solution)/shard_map/reduce_scatter | solution.py:295
  3751.8 491.2 %reduce-scatter.29.cloned.1.call-done = f32[176,2048]{1,0:T(8,128)} async-done(((f32[5632,2048]{1,0:T(8,128)}), f32[176,2048]{1,0:T(8,128)}) %reduce-scatter.29.cloned.1.call-update) | async-done | bytes 1441808 | tf_op jit(solution)/shard_map/reduce_scatter | solution.py:296
  (758 shorter events, 836.3 us)
Async XLA Ops:
  7.2 129.8 %copy-start.1 = (bf16[256,2048]{1,0:T(8,128)(2,1)S(1)}, bf16[256,2048]{1,0:T(8,128)(2,1)}, u32[]{:S(2)}) copy-start(bf16[256,2048]{1,0:T(8,128)(2,1)} %param.25) | copy-start | bytes 3145732
  7.2 153.0 %all-gather.17.cloned.1.call-start = ((), (), s32[]{:S(2)}) async-start(), calls=%async_computation.20 | async-start | bytes 4325376 | tf_op jit(solution)/shard_map/all_gather | solution.py:170
  7.9 160.1 %all-gather.21.cloned.1.call-start = ((), (), s32[]{:S(2)}) async-start(), calls=%async_computation.22 | async-start | bytes 4325376 | tf_op jit(solution)/shard_map/all_gather | solution.py:169
  8.7 210.5 %all-gather.19.cloned.1.call-start = ((), (), s32[]{:S(2)}) async-start(), calls=%async_computation.21 | async-start | bytes 8650752 | tf_op jit(solution)/shard_map/all_gather | solution.py:171
  53.7 84.9 %copy-start.39 = (bf16[2048,16]{0,1:T(8,128)(2,1)}, bf16[2048,16]{0,1:T(8,128)(2,1)S(1)}, u32[]{:S(2)}) copy-start(bf16[2048,16]{0,1:T(8,128)(2,1)S(1)} %reshape.309) | copy-start | bytes 196612
  137.8 81.3 %copy-start.41 = (f32[256]{0:T(256)}, f32[256]{0:T(256)S(1)}, u32[]{:S(2)}) copy-start(f32[256]{0:T(256)S(1)} %fusion.126) | copy-start | bytes 3076
  139.5 12.2 all-to-all-start
  164.5 15.0 all-to-all-start.1
  179.6 45.3 %copy-start.29 = (bf16[256,2,512]{2,0,1:T(8,128)(2,1)}, bf16[256,2,512]{2,0,1:T(8,128)(2,1)S(1)}, u32[]{:S(2)}) copy-start(bf16[256,2,512]{2,0,1:T(8,128)(2,1)S(1)} %all-to-all-done.1) | copy-start | bytes 1572868
  179.6 46.4 %all-to-all-start.3 = ((bf16[256,2,512]{2,0,1:T(8,128)(2,1)}), bf16[256,2,512]{2,0,1:T(8,128)(2,1)S(1)}, u32[]{:S(2)}, u32[]{:S(2)}) async-start(bf16[256,2,512]{2,0,1:T(8,128)(2,1)} %bitcast.646), calls=%async_computation.3 | async-start | bytes 1048576 | tf_op jit(solution)/shard_map/all_to_all | solution.py:211
  226.0 18.8 all-to-all-start.2
  230.4 369.9 %all-gather.33.cloned.1.call-start = ((), (), s32[]{:S(2)}) async-start(), calls=%async_computation.36 | async-start | bytes 17825792 | tf_op jit(solution)/shard_map/all_gather | solution.py:19
  474.5 211.8 %all-gather.23.cloned.1.call-start = ((), (), s32[]{:S(2)}) async-start(), calls=%async_computation.23 | async-start | bytes 8650752 | tf_op jit(solution)/shard_map/all_gather | solution.py:175
  475.1 288.3 %all-gather.25.cloned.1.call-start = ((), (), s32[]{:S(2)}) async-start(), calls=%async_computation.24 | async-start | bytes 8650752 | tf_op jit(solution)/shard_map/all_gather | solution.py:177
  475.7 433.9 %all-gather.27.cloned.1.call-start = ((), (), s32[]{:S(2)}) async-start(), calls=%async_computation.25 | async-start | bytes 23789568 | tf_op jit(solution)/shard_map/all_gather | solution.py:179
  476.4 578.9 %all-gather.29.cloned.1.call-start = ((), (), s32[]{:S(2)}) async-start(), calls=%async_computation.26 | async-start | bytes 23789568 | tf_op jit(solution)/shard_map/all_gather | solution.py:180
  477.2 723.8 %all-gather.31.cloned.1.call-start = ((), (), s32[]{:S(2)}) async-start(), calls=%async_computation.27 | async-start | bytes 23789568 | tf_op jit(solution)/shard_map/all_gather | solution.py:181
  641.0 26.6 all-to-all-start.4
  644.8 772.6 %all-gather.35.cloned.1.call-start = ((), (), s32[]{:S(2)}) async-start(), calls=%async_computation.37 | async-start | bytes 17825792 | tf_op jit(solution)/shard_map/all_gather | solution.py:19
  695.7 73.6 %copy-start.35 = (bf16[256,2048]{1,0:T(8,128)(2,1)}, bf16[256,2048]{1,0:T(8,128)(2,1)S(1)}, u32[]{:S(2)}) copy-start(bf16[256,2048]{1,0:T(8,128)(2,1)S(1)} %get-tuple-element.1817) | copy-start | bytes 3145732
  770.9 284.4 %copy-start.6 = (bf16[256,2048]{1,0:T(8,128)(2,1)}, bf16[256,2048]{1,0:T(8,128)(2,1)S(1)}, u32[]{:S(2)}) copy-start(bf16[256,2048]{1,0:T(8,128)(2,1)S(1)} %multiply_convert_fusion.4) | copy-start | bytes 3145732
  1292.4 534.5 %reduce-scatter.33.cloned.1.call-start = ((), (), s32[]{:S(2)}) async-start(), calls=%async_computation.39 | async-start | bytes 540672
  1654.6 265.3 %reduce-scatter.31.cloned.1.call-start = ((), (), s32[]{:S(2)}) async-start(), calls=%async_computation.38 | async-start | bytes 1081344
  1656.3 448.2 %reduce-scatter.21.cloned.1.call-start = ((), (), s32[]{:S(2)}) async-start(), calls=%async_computation.31 | async-start | bytes 17301504 | tf_op jit(solution)/shard_map/reduce_scatter | solution.py:364
  1664.8 623.8 %reduce-scatter.23.cloned.1.call-start = ((), (), s32[]{:S(2)}) async-start(), calls=%async_computation.32 | async-start | bytes 17301504 | tf_op jit(solution)/shard_map/reduce_scatter | solution.py:366
  1675.8 767.1 %reduce-scatter.15.cloned.1.call-start = ((), (), s32[]{:S(2)}) async-start(), calls=%async_computation.28 | async-start | bytes 8650752 | tf_op jit(solution)/shard_map/reduce_scatter | solution.py:358
  1692.8 898.3 %reduce-scatter.17.cloned.1.call-start = ((), (), s32[]{:S(2)}) async-start(), calls=%async_computation.29 | async-start | bytes 8650752 | tf_op jit(solution)/shard_map/reduce_scatter | solution.py:359
  1709.0 1062.5 %reduce-scatter.19.cloned.1.call-start = ((), (), s32[]{:S(2)}) async-start(), calls=%async_computation.30 | async-start | bytes 17301504 | tf_op jit(solution)/shard_map/reduce_scatter | solution.py:360
  1739.3 1521.1 %reduce-scatter.25.cloned.1.call-start = ((), (), s32[]{:S(2)}) async-start(), calls=%async_computation.33 | async-start | bytes 47579136 | tf_op jit(solution)/shard_map/reduce_scatter | solution.py:294
  1760.2 1991.6 %reduce-scatter.27.cloned.1.call-start = ((), (), s32[]{:S(2)}) async-start(), calls=%async_computation.34 | async-start | bytes 47579136 | tf_op jit(solution)/shard_map/reduce_scatter | solution.py:295
  1780.1 2462.9 %reduce-scatter.29.cloned.1.call-start = ((), (), s32[]{:S(2)}) async-start(), calls=%async_computation.35 | async-start | bytes 47579136 | tf_op jit(solution)/shard_map/reduce_scatter | solution.py:296
  1824.2 97.1 %copy-start.21 = (bf16[256,2,1024]{0,2,1:T(8,128)(2,1)S(1)}, bf16[256,2,1024]{0,2,1:T(8,128)(2,1)}, u32[]{:S(2)}) copy-start(bf16[256,2,1024]{0,2,1:T(8,128)(2,1)} %copy-done.20) | copy-start | bytes 3145732
  (75 other events, 389.8 us)
Sparse Core Ops, SparseCore 0:
  10.9 65.4 all-gather.16
  79.2 60.7 all-gather.20
  142.9 76.1 all-gather.18
  474.7 125.6 all-gather.32
  603.0 83.2 all-gather.22
  689.0 74.3 all-gather.24
  766.3 143.1 all-gather.26
  912.5 142.7 all-gather.28
  1058.2 142.7 all-gather.30
  1292.5 124.8 all-gather.34
  1654.7 131.8 reduce-scatter.32
  1788.8 131.0 reduce-scatter.30
  1922.8 181.6 reduce-scatter.20
  2107.2 181.4 reduce-scatter.22
  2291.4 151.5 reduce-scatter.14
  2445.7 145.4 reduce-scatter.16
  2593.8 177.6 reduce-scatter.18
  2774.2 486.1 reduce-scatter.24
  3263.3 488.4 reduce-scatter.26
  3754.5 488.4 reduce-scatter.28
where the time goes:
time: 4270 us; the launch traced here: 4250 us
  waiting for transfers between devices  3130 us (73%)
  matrix products  458 us (11%)
  blocking collectives  248 us (6%)
  local copies, waits for them, and re-layouts  204 us (5%)
  other arithmetic  167 us (4%)
    reduce_scatter x1, waiting for transfers between devices, on_device(): lax.psum_scatter(up_term, ('seq', 'fsdp'), scatter_dimension=0, tiled=True)  491 us
    reduce_scatter x1, waiting for transfers between devices, on_device(): lax.psum_scatter(down_term, ('seq', 'fsdp'), scatter_dimension=0, tiled=T...  491 us
    reduce_scatter x1, waiting for transfers between devices, on_device(): lax.psum_scatter(gate_term, ('seq', 'fsdp'), scatter_dimension=0, tiled=T...  489 us
    dot_general x115, matrix products, precise_einsum(): return jnp.einsum(form, left, right, precision=lax.Precision.HIGHEST)  211 us
    all_gather x2, waiting for transfers between devices, entering(): everything = jax.tree.map(lambda part: lax.all_gather(part, axis), shard)  207 us
    reduce_scatter x1, waiting for transfers between devices, on_device(): lax.psum_scatter(output_term, ('seq', 'fsdp'), scatter_dimension=0, tiled...  184 us
    reduce_scatter x1, waiting for transfers between devices, on_device(): lax.psum_scatter(value_term, ('seq', 'fsdp'), scatter_dimension=0, tiled=...  180 us
    reduce_scatter x1, waiting for transfers between devices, on_device(): lax.psum_scatter(query_term, ('seq', 'fsdp'), scatter_dimension=0, tiled=...  154 us
  transfers between devices with their start and end apart: 25, of which 21 were waited for; matrix products, arithmetic and copies ran while one was open for 7% of the time, Pallas kernels for 0%

commit v1 on v0

v1 whole, which is shorter than its diff:
```python
import jax
import jax.numpy as jnp
from jax import lax
from jax.sharding import PartitionSpec as P

SPAN = 64
HK = 256
HV = 512
HEADS = 4
EPS = 1e-06
GATE_SCALE = 16.0
BOTH = ("seq", "fsdp")
F32 = jnp.float32
BF16 = jnp.bfloat16


def dot(left, right):
    return jnp.dot(left, right, preferred_element_type=F32)


def dot_rows(left, right):
    return lax.dot_general(left, right, (((0,), (0,)), ((), ())), preferred_element_type=F32)


def dot_cols(left, right):
    return lax.dot_general(left, right, (((1,), (1,)), ((), ())), preferred_element_type=F32)


def ein(form, left, right):
    return jnp.einsum(form, left, right, preferred_element_type=F32)


class Place:
    def __init__(self):
        self.fsdp = lax.axis_size("fsdp")
        self.line_size = self.fsdp // 4
        index = lax.axis_index("fsdp")
        self.seq = lax.axis_index("seq")
        self.core = index % 2
        self.side = (index // 2) % 2
        self.line = index // 4
        self.groups = [
            [4 * a + 2 * b + c for a in range(self.line_size) for c in range(2)] for b in range(2)
        ]

    def send(self, value, move):
        pairs = []
        for s in range(2):
            for a in range(self.line_size):
                for b in range(2):
                    for c in range(2):
                        to = move(s, a, b, c)
                        if 0 <= to[1] < self.line_size:
                            source = s * self.fsdp + 4 * a + 2 * b + c
                            target = to[0] * self.fsdp + 4 * to[1] + 2 * to[2] + to[3]
                            pairs.append((source, target))
        return lax.ppermute(value, BOTH, pairs)

    def over_side(self, value):
        return self.send(value, lambda s, a, b, c: (s, a, 1 - b, c))

    def over_seq(self, value):
        return self.send(value, lambda s, a, b, c: (1 - s, a, b, c))

    def over_both(self, value):
        return self.send(value, lambda s, a, b, c: (1 - s, a, 1 - b, c))

    def over_core(self, value):
        return self.send(value, lambda s, a, b, c: (s, a, b, 1 - c))

    def along(self, value, step):
        return self.send(value, lambda s, a, b, c: (s, a + step, b, c))

    def swap_top(self, value):
        half = self.line_size // 2
        return self.send(value, lambda s, a, b, c: (s, b * half + a % half, a // half, c))


def pair(which, own, other):
    first = which == 0
    return jnp.stack([jnp.where(first, own, other), jnp.where(first, other, own)])


def exchange_quarters(here, blocks):
    me = 2 * here.seq + here.side
    take = lambda i: lax.dynamic_index_in_dim(blocks, i, 0, keepdims=False)
    own = take(me)
    side = here.over_side(take(me ^ 1))
    seq = here.over_seq(take(me ^ 2))
    both = here.over_both(take(me ^ 3))
    rows = pair(here.seq, pair(here.side, own, side), pair(here.side, seq, both))
    return rows.reshape((4,) + own.shape)


def gather_tokens(here, rows):
    half = rows.shape[0] // 2
    top, low = rows[:half], rows[half:]
    top_side = here.over_side(top)
    low_seq = here.over_seq(low)
    top_pair = jnp.stack([top, top_side])
    low_pair = jnp.stack([low, low_seq])
    top_far = here.over_seq(top_pair)
    low_far = here.over_side(low_pair)
    own = jnp.concatenate([top, low])
    side = jnp.concatenate([top_side, low_far[0]])
    seq = jnp.concatenate([top_far[0], low_seq])
    both = jnp.concatenate([top_far[1], low_far[1]])
    out = pair(here.side, pair(here.seq, own, seq), pair(here.seq, side, both))
    return out.reshape((4 * rows.shape[0],) + rows.shape[1:])


def scatter_tokens(here, rows):
    tok, width = rows.shape[0] // 4, rows.shape[1]
    half = tok // 2
    blocks = rows.reshape(2, 2, 2, half, width)
    top, low = blocks[:, :, 0], blocks[:, :, 1]
    pick = lambda a, i, axis: lax.dynamic_index_in_dim(a, i, axis, keepdims=False)
    top_in = here.over_side(pick(top, 1 - here.side, 0))
    low_in = here.over_seq(pick(low, 1 - here.seq, 1))
    top_sum = pick(top, here.side, 0).astype(F32) + top_in.astype(F32)
    low_sum = pick(low, here.seq, 1).astype(F32) + low_in.astype(F32)
    top_far = here.over_seq(pick(top_sum, 1 - here.seq, 0).astype(BF16))
    low_far = here.over_side(pick(low_sum, 1 - here.side, 0).astype(BF16))
    return jnp.concatenate(
        [
            pick(top_sum, here.seq, 0) + top_far.astype(F32),
            pick(low_sum, here.side, 0) + low_far.astype(F32),
        ]
    )


def gather_line(here, rows):
    return lax.all_gather(rows, "fsdp", axis=0, tiled=True, axis_index_groups=here.groups)


def scatter_line(here, rows):
    return lax.psum_scatter(
        rows, "fsdp", scatter_dimension=0, tiled=True, axis_index_groups=here.groups
    )


def carry_states(here, states, decays, backward):
    other_states, other_decays = here.over_core(states), here.over_core(decays)
    first = here.core == 0
    state_at = [jnp.where(first, states, other_states), jnp.where(first, other_states, states)]
    decay_at = [jnp.where(first, decays, other_decays), jnp.where(first, other_decays, decays)]
    order = [(j, c) for j in range(2) for c in range(2)]
    if backward:
        order = order[::-1]
    parts = [(state_at[c][j], decay_at[c][j]) for j, c in order]
    total, through = parts[0]
    for state, decay in parts[1:]:
        total = decay[:, None] * total + state
        through = through * decay
    half = total.shape[0] // 2
    mine = lax.dynamic_slice_in_dim(total, here.core * half, half, 0)
    mine_through = lax.dynamic_slice_in_dim(through, here.core * half, half, 0)
    row = jnp.pad(mine_through[None, :], ((0, 15), (0, total.shape[1] - half)))
    packed = jnp.concatenate([mine, row]).astype(BF16)
    entering = jnp.zeros_like(mine)
    for step in range(here.line_size - 1, 0, -1):
        came = here.along(packed, -step if backward else step).astype(F32)
        entering = came[half, :half][:, None] * entering + came[:half]
    entering = pair(here.core, entering, here.over_core(entering)).reshape(total.shape)
    at = {}
    for (j, c), (state, decay) in zip(order, parts):
        at[j, c] = entering
        entering = decay[:, None] * entering + state
    return jnp.where(
        first, jnp.stack([at[0, 0], at[1, 0]]), jnp.stack([at[0, 1], at[1, 1]])
    )


def on_device(
    tokens,
    attn_gain,
    w_query,
    w_key,
    w_value,
    w_down_rank,
    w_up_rank,
    gate_bias,
    w_outgate,
    head_gain,
    w_output,
    ffn_gain,
    w_gate,
    w_up,
    w_down,
    doc_starts,
    cotangent,
):
    here = Place()
    line = here.line_size
    tok, model = tokens.shape
    rows_d = w_query.shape[0]
    rows_f = w_down.shape[0]
    rank = w_up_rank.shape[0]
    cols_k = w_up_rank.shape[1]
    group = 4 * tok
    spans = group // SPAN
    per_seg = spans // 2
    me = 2 * here.seq + here.side

    def to_gathered(x):
        n = x.shape[0]
        return x.reshape(n, 2, line, 2, 2, rows_d).transpose(0, 2, 4, 1, 3, 5).reshape(n, model)

    def from_gathered(x):
        n = x.shape[0]
        return x.reshape(n, line, 2, 2, 2, rows_d).transpose(0, 3, 1, 4, 2, 5).reshape(n, model)

    small = jnp.concatenate(
        [
            attn_gain,
            ffn_gain,
            head_gain,
            gate_bias,
            w_up_rank.reshape(-1),
            w_down_rank.reshape(-1),
        ]
    )
    small_all = lax.all_gather(small, BOTH, axis=0)
    cuts = []
    at = 0
    for size in (rows_d, rows_d, head_gain.shape[0], cols_k, rank * cols_k, rows_d * rank):
        cuts.append(small_all[:, at : at + size])
        at += size
    devices = small_all.shape[0]
    full_attn_gain = cuts[0].reshape(model).astype(F32)
    full_ffn_gain = cuts[1].reshape(model).astype(F32)
    full_head_gain = cuts[2].reshape(HV).astype(F32)
    full_bias = cuts[3].reshape(HEADS * HK)
    full_up_rank = cuts[4].reshape(devices, rank, cols_k).transpose(1, 0, 2).reshape(rank, -1)
    full_down_rank = cuts[5].reshape(model, rank)
    my_bias = lax.dynamic_slice_in_dim(full_bias, me * HK, HK, 0).astype(F32)
    my_up_rank = lax.dynamic_slice_in_dim(full_up_rank, me * HK, HK, 1)
    down_rank_rows = (
        full_down_rank.reshape(2, line, 2, 2, rows_d, rank)
        .transpose(1, 3, 0, 2, 4, 5)
        .reshape(model, rank)
    )

    def heads_first(w, width):
        return w.reshape(rows_d, HEADS, width).transpose(1, 0, 2)

    mixer_cols = jnp.concatenate(
        [
            heads_first(w_query, HK),
            heads_first(w_key, HK),
            heads_first(w_value, HV),
            heads_first(w_outgate, HV),
        ],
        axis=2,
    )
    mixer_piece = exchange_quarters(here, mixer_cols)
    w_mixer = gather_line(here, mixer_piece.reshape(4 * rows_d, -1))

    def hidden_first(w):
        return (
            w.reshape(rows_d, 2, line, 2, 2, rows_f)
            .transpose(1, 3, 0, 2, 4, 5)
            .reshape(4, rows_d, -1)
        )

    quarter = 2 * line * rows_f
    ffn_cols = jnp.concatenate([hidden_first(w_gate), hidden_first(w_up)], axis=2)
    ffn_piece = exchange_quarters(here, ffn_cols)
    w_out = gather_line(here, here.swap_top(w_output))
    w_out = (
        w_out.reshape(2, line // 2, 2 * rows_d, model).transpose(1, 0, 2, 3).reshape(HV, model)
    )
    w_ffn = gather_line(here, ffn_piece.reshape(4 * rows_d, -1))
    w_dn = gather_line(here, w_down)

    inputs = tokens.astype(F32)
    scale_in = lax.rsqrt(jnp.mean(inputs * inputs, axis=-1, keepdims=True) + EPS)
    normed_in = (inputs * scale_in * full_attn_gain).astype(BF16)
    x_in = gather_tokens(here, to_gathered(normed_in))
    cot = gather_tokens(here, cotangent)
    other_docs = here.over_side(doc_starts)
    docs = pair(here.side, doc_starts, other_docs)
    flags = (jnp.arange(tok, dtype=jnp.int32) == docs[:, :, None]).astype(F32)
    flags = flags.reshape(spans, SPAN)

    projected = dot(x_in, w_mixer)
    queries = projected[:, :HK].astype(BF16)
    keys_in = projected[:, HK : 2 * HK].astype(BF16)
    values = projected[:, 2 * HK : 2 * HK + HV].astype(BF16)
    outgate = projected[:, 2 * HK + HV :]
    rank_low = dot(x_in, down_rank_rows).astype(BF16)
    logits = (dot(rank_low, my_up_rank) + my_bias).astype(BF16).astype(F32)

    decays = (jax.nn.log_sigmoid(logits) / GATE_SCALE).reshape(spans, SPAN, HK)
    causal = jnp.tril(jnp.ones((SPAN, SPAN), F32))
    running = jnp.einsum("ts,nsk->ntk", causal, decays, precision=lax.Precision.HIGHEST)
    count = jnp.einsum("ts,ns->nt", causal, flags, precision=lax.Precision.HIGHEST)
    closing = running[:, -1, :]
    unfinished = (count == 0.0)[:, :, None]
    tail = (count == count[:, -1:])[:, :, None]
    unbroken = count[:, -1:] == 0.0
    mask = (count[:, :, None] == count[:, None, :]) & (causal > 0)[None]
    q_s = queries.reshape(spans, SPAN, HK).astype(F32) * HK ** (-0.5)
    k_s = keys_in.reshape(spans, SPAN, HK).astype(F32)
    v_s = values.reshape(spans, SPAN, HV)
    grow = jnp.exp(running)
    shrink = jnp.exp(-running)
    to_end = jnp.where(tail, jnp.exp(closing[:, None, :] - running), 0.0)
    expanded = q_s * grow
    shrunk = k_s * shrink
    ending = k_s * to_end
    expanded_low = expanded.astype(BF16)
    shrunk_low = shrunk.astype(BF16)
    ending_low = ending.astype(BF16)
    reach_low = jnp.where(unfinished, expanded, 0.0).astype(BF16)
    scores = jnp.where(mask, ein("ntk,nsk->nts", expanded_low, shrunk_low), 0.0).astype(BF16)
    span_decay = jnp.where(unbroken, jnp.exp(closing), 0.0).reshape(2, per_seg, HK)
    updates = ein("ntk,ntv->nkv", ending_low, v_s).reshape(2, per_seg, HK, HV)

    before = [jnp.ones((2, HK), F32)]
    for c in range(per_seg):
        before.append(before[-1] * span_decay[:, c])
    through = before[-1]
    before = jnp.stack(before[:-1], axis=1)
    after = [jnp.ones((2, HK), F32)]
    for c in range(per_seg - 1, 0, -1):
        after.append(after[-1] * span_decay[:, c])
    after = jnp.stack(after[::-1], axis=1)
    seg_ending = (ending.reshape(2, per_seg, SPAN, HK) * after[:, :, None, :]).astype(BF16)
    seg_ending = seg_ending.reshape(2, per_seg * SPAN, HK)
    seg_values = values.reshape(2, per_seg * SPAN, HV)
    seg_end = ein("jtk,jtv->jkv", seg_ending, seg_values)
    entering = carry_states(here, seg_end, through, False)
    states = [entering]
    for c in range(per_seg - 1):
        states.append(span_decay[:, c, :, None] * states[-1] + updates[:, c])
    states = jnp.stack(states, axis=1).reshape(spans, HK, HV)
    states_low = states.astype(BF16)
    raw = ein("nts,nsv->ntv", scores, v_s) + ein("ntk,nkv->ntv", reach_low, states_low)
    mixed = raw.reshape(group, HV).astype(BF16).astype(F32)

    head_scale = lax.rsqrt(jnp.mean(mixed * mixed, axis=-1, keepdims=True) + EPS)
    normed_mix = mixed * head_scale * full_head_gain
    outgate_sig = jax.nn.sigmoid(outgate)
    gate_act = outgate * outgate_sig
    gated = (normed_mix * gate_act).astype(BF16)
    resid = inputs + scatter_tokens(here, dot(gated, w_out).astype(BF16))
    scale_mid = lax.rsqrt(jnp.mean(resid * resid, axis=-1, keepdims=True) + EPS)
    normed_mid = (resid * scale_mid * full_ffn_gain).astype(BF16)
    x_mid = gather_tokens(here, to_gathered(normed_mid))
    gate_up = dot(x_mid, w_ffn)
    gate_pre, up_pre = gate_up[:, :quarter], gate_up[:, quarter:]
    gate_sig = jax.nn.sigmoid(gate_pre)
    silu_gate = gate_pre * gate_sig
    hidden = (silu_gate * up_pre).astype(BF16)

    hidden_grad = dot_cols(cot, w_dn)
    gate_grad = (hidden_grad * up_pre * (gate_sig * (1.0 + gate_pre * (1.0 - gate_sig)))).astype(
        BF16
    )
    up_grad = (hidden_grad * silu_gate).astype(BF16)
    gate_up_grad = jnp.concatenate([gate_grad, up_grad], axis=1)
    mid_grad = scatter_tokens(here, dot_cols(gate_up_grad, w_ffn).astype(BF16))
    mid_grad = from_gathered(mid_grad)
    down_term = scatter_line(here, dot_rows(hidden, cot).astype(BF16))
    ffn_term = scatter_line(here, dot_rows(x_mid, gate_up_grad).astype(BF16))
    layer_output = (resid + scatter_tokens(here, dot(hidden, w_dn).astype(BF16))).astype(BF16)

    cot_here = cotangent.astype(F32)
    ffn_gain_term = jnp.sum(mid_grad * resid * scale_mid, axis=0)
    scaled_mid = full_ffn_gain * mid_grad
    resid_grad = (
        cot_here
        + scale_mid * scaled_mid
        - resid * scale_mid**3 * jnp.mean(scaled_mid * resid, axis=-1, keepdims=True)
    )
    branch = gather_tokens(here, resid_grad.astype(BF16))

    gated_grad = dot_cols(branch, w_out)
    outgate_grad = (
        gated_grad * normed_mix * outgate_sig * (1.0 + outgate * (1.0 - outgate_sig))
    ).astype(BF16)
    normed_grad = gated_grad * gate_act
    head_gain_term = jnp.sum(normed_grad * mixed * head_scale, axis=0)
    scaled_head = full_head_gain * normed_grad
    mixed_grad = (
        head_scale * scaled_head
        - mixed * head_scale**3 * jnp.mean(scaled_head * mixed, axis=-1, keepdims=True)
    ).astype(BF16)
    seg_reach = jnp.where(unfinished, expanded, 0.0).reshape(2, per_seg, SPAN, HK)
    seg_reach = (seg_reach * before[:, :, None, :]).astype(BF16)
    seg_reach = seg_reach.reshape(2, per_seg * SPAN, HK)
    start_grad = ein("jtk,jtv->jkv", seg_reach, mixed_grad.reshape(2, per_seg * SPAN, HV))
    leaving = carry_states(here, start_grad, through, True)
    out_term = dot_rows(gated, branch).astype(BF16)
    out_term = out_term.reshape(line // 2, 2, 2 * rows_d, model).transpose(1, 0, 2, 3)
    out_term = scatter_line(here, out_term.reshape(HV, model))

    o_g = mixed_grad.reshape(spans, SPAN, HV)
    reach_terms = ein("ntk,ntv->nkv", reach_low, o_g).reshape(2, per_seg, HK, HV)
    state_grads = [leaving]
    for c in range(per_seg - 1, 0, -1):
        state_grads.append(span_decay[:, c, :, None] * state_grads[-1] + reach_terms[:, c])
    state_grads = jnp.stack(state_grads[::-1], axis=1).reshape(spans, HK, HV)
    state_grads_low = state_grads.astype(BF16)
    score_grad = jnp.where(mask, ein("ntv,nsv->nts", o_g, v_s), 0.0).astype(BF16)
    expanded_grad = ein("nts,nsk->ntk", score_grad, shrunk_low) + jnp.where(
        unfinished, ein("ntv,nkv->ntk", o_g, states_low), 0.0
    )
    shrunk_grad = ein("nts,ntk->nsk", score_grad, expanded_low)
    ending_grad = ein("ntv,nkv->ntk", v_s, state_grads_low)
    value_grad = ein("nts,ntv->nsv", scores, o_g) + ein("ntk,nkv->ntv", ending_low, state_grads_low)
    query_grad = expanded_grad * grow * HK ** (-0.5)
    key_grad = shrunk_grad * shrink + ending_grad * to_end
    from_here = expanded * expanded_grad - shrunk * shrunk_grad
    from_past = ending * ending_grad
    carried = span_decay.reshape(spans, HK) * jnp.sum(states * state_grads, axis=-1)
    decay_grad = (
        jnp.einsum("ut,nuk->ntk", causal, from_here, precision=lax.Precision.HIGHEST)
        + jnp.einsum(
            "tu,nuk->ntk", causal - jnp.eye(SPAN), from_past, precision=lax.Precision.HIGHEST
        )
        + carried[:, None, :]
    )
    decay_grad = decay_grad * (1.0 - flags[:, :, None])
    logit_grad = (decay_grad.reshape(group, HK) * jax.nn.sigmoid(-logits) / GATE_SCALE).astype(BF16)
    grads = jnp.concatenate(
        [
            query_grad.reshape(group, HK).astype(BF16),
            key_grad.reshape(group, HK).astype(BF16),
            value_grad.reshape(group, HV).astype(BF16),
            outgate_grad,
        ],
        axis=1,
    )
    mixer_term = scatter_line(here, dot_rows(x_in, grads).astype(BF16))
    in_grad = scatter_tokens(here, dot_cols(grads, w_mixer).astype(BF16))
    in_grad = from_gathered(in_grad)

    bias_term = jnp.sum(logit_grad.astype(F32), axis=0)
    up_rank_term = dot_rows(rank_low, logit_grad)
    rank_part = dot_cols(logit_grad, my_up_rank)
    rank_part = rank_part + here.over_side(rank_part)
    rank_part = rank_part + here.over_seq(rank_part)
    position = (2 * here.side + here.seq) * tok
    rank_grad = lax.dynamic_slice_in_dim(rank_part, position, tok, 0).astype(BF16)
    down_rank_term = dot_rows(normed_in, rank_grad)
    in_grad = in_grad + dot_cols(rank_grad, full_down_rank)

    attn_gain_term = jnp.sum(in_grad * inputs * scale_in, axis=0)
    scaled_in = full_attn_gain * in_grad
    input_grad = (
        resid_grad
        + scale_in * scaled_in
        - inputs * scale_in**3 * jnp.mean(scaled_in * inputs, axis=-1, keepdims=True)
    ).astype(BF16)

    zero_bias = jnp.zeros((HEADS * HK,), F32)
    zero_up = jnp.zeros((rank, HEADS * HK), F32)
    bias_all = lax.dynamic_update_slice_in_dim(zero_bias, bias_term, me * HK, 0)
    up_all = lax.dynamic_update_slice_in_dim(zero_up, up_rank_term, me * HK, 1)
    small_terms = jnp.concatenate(
        [
            attn_gain_term.reshape(devices, -1),
            ffn_gain_term.reshape(devices, -1),
            head_gain_term.reshape(devices, -1),
            bias_all.reshape(devices, -1),
            up_all.reshape(rank, devices, cols_k).transpose(1, 0, 2).reshape(devices, -1),
            down_rank_term.reshape(devices, -1),
        ],
        axis=1,
    )
    small_sum = lax.psum_scatter(small_terms, BOTH, scatter_dimension=0, tiled=True)[0]
    pieces = []
    at = 0
    for size in (rows_d, rows_d, head_gain.shape[0], cols_k, rank * cols_k, rows_d * rank):
        pieces.append(small_sum[at : at + size])
        at += size

    down_grad = down_term.astype(F32)
    out_grad = here.swap_top(out_term).astype(F32)
    ffn_back = exchange_quarters(here, ffn_term.reshape(4, rows_d, 2 * quarter)).astype(F32)

    def hidden_last(g):
        return (
            g.reshape(2, 2, rows_d, line, 2, rows_f)
            .transpose(2, 0, 3, 1, 4, 5)
            .reshape(rows_d, 4 * quarter)
        )

    gate_out = hidden_last(ffn_back[:, :, :quarter])
    up_out = hidden_last(ffn_back[:, :, quarter:])
    mixer_back = exchange_quarters(here, mixer_term.reshape(4, rows_d, -1)).astype(F32)

    def heads_last(g):
        return g.transpose(1, 0, 2).reshape(rows_d, -1)

    query_out = heads_last(mixer_back[:, :, :HK])
    key_out = heads_last(mixer_back[:, :, HK : 2 * HK])
    value_out = heads_last(mixer_back[:, :, 2 * HK : 2 * HK + HV])
    outgate_out = heads_last(mixer_back[:, :, 2 * HK + HV :])
    return (
        layer_output,
        input_grad,
        pieces[0],
        query_out,
        key_out,
        value_out,
        pieces[5].reshape(rows_d, rank),
        pieces[4].reshape(rank, cols_k),
        pieces[3],
        outgate_out,
        pieces[2],
        out_grad,
        pieces[1],
        gate_out,
        up_out,
        down_grad,
    )


def solution(mesh):
    rows = P(BOTH, None)
    vector = P(BOTH)
    by_tokens = P(("fsdp", "seq"), None)
    by_cols = P(None, BOTH)
    in_specs = (
        by_tokens,
        vector,
        rows,
        rows,
        rows,
        rows,
        by_cols,
        vector,
        rows,
        vector,
        rows,
        vector,
        rows,
        rows,
        rows,
        P("fsdp"),
        by_tokens,
    )
    out_specs = (
        by_tokens,
        by_tokens,
        vector,
        rows,
        rows,
        rows,
        rows,
        by_cols,
        vector,
        rows,
        vector,
        rows,
        vector,
        rows,
        rows,
        rows,
    )
    return jax.shard_map(
        on_device, mesh=mesh, in_specs=in_specs, out_specs=out_specs, check_vma=False
    )
```

time: 4270 us -> 1170 us (0.27)
  waiting for transfers between devices: 3130 us -> 595 us
  matrix products: 458 us -> 177 us
  blocking collectives: 248 us -> 0 us
  starting transfers between devices: 20.3 us -> 100 us
  other arithmetic: 167 us -> 111 us
    reduce_scatter x8 -> x4, waiting for transfers between devices: 2270 us -> 81 us  [scatter_line(): lax.psum_scatter(rows, 'fsdp', scatter_dimension=0, tiled=True, axis_inde...]
    all_gather x10 -> x4, waiting for transfers between devices: 723 us -> 0.03 us  [gather_line(): lax.all_gather(rows, 'fsdp', axis=0, tiled=True, axis_index_groups=here.g...]
    dot_general x151 -> x36, matrix products: 455 us -> 177 us  [the longest x6 53.4 us: dot_cols(): lax.dot_general(left, right, (((1,), (1,)), ((), ())), preferred_element_...]
    ppermute x0 -> x60, waiting for transfers between devices: none -> 240 us  [send(): return lax.ppermute(value, BOTH, pairs)]
    unnamed x22 -> x12, waiting for transfers between devices: 97 us -> 274 us
    all_gather x3 -> x0, blocking collectives: 107 us -> none  [the longest x1 44.1 us: on_device(): lax.all_gather(w_down_rank, ('seq', 'fsdp'), axis=0, tiled=True)]
    ppermute x0 -> x60, starting transfers between devices: none -> 99.9 us  [send(): return lax.ppermute(value, BOTH, pairs)]
    unnamed x2 -> x0, blocking collectives: 78.2 us -> none
  transfers between devices with their start and end apart: 25 -> 70, of which waited for: 21 -> 35; matrix products, arithmetic and copies ran while one was open for 7% -> 25% of each run, Pallas kernels for 0% -> 0%
where the time goes in v1:
time: 1170 us
  waiting for transfers between devices  595 us (51%)
  matrix products  177 us (15%)
  local copies, waits for them, and re-layouts  164 us (14%)
  other arithmetic  111 us (9%)
  starting transfers between devices  100 us (9%)
  between operations  18.9 us (2%)
    unnamed x12, waiting for transfers between devices  274 us
    ppermute x60, waiting for transfers between devices, send(): return lax.ppermute(value, BOTH, pairs)  240 us
    ppermute x60, starting transfers between devices, send(): return lax.ppermute(value, BOTH, pairs)  99.9 us
    reduce_scatter x4, waiting for transfers between devices, scatter_line(): lax.psum_scatter(rows, 'fsdp', scatter_dimension=0, tiled=True, axis_inde...  81 us
    dot_general x6, matrix products, dot_cols(): lax.dot_general(left, right, (((1,), (1,)), ((), ())), preferred_element_...  53.4 us
    dot_general x6, matrix products, dot_rows(): lax.dot_general(left, right, (((0,), (0,)), ((), ())), preferred_element_...  46 us
    dot_general x6, matrix products, dot(): return jnp.dot(left, right, preferred_element_type=F32)  44.1 us
    unnamed x327, local copies, waits for them, and re-layouts  40.5 us
  transfers between devices with their start and end apart: 70, of which 35 were waited for; matrix products, arithmetic and copies ran while one was open for 25% of the time, Pallas kernels for 0%

profile of v1, /device:TPU:0, one launch (start us, length us, event | category | flops | bytes accessed | tf_op | source)
XLA Modules:
  0.0 1166.3 jit_solution(16299926164093801296)
XLA Ops:
  20.6 6.0 collective-permute-done.6
  56.0 147.4 %all-reduce.7.cloned.1.call-done = bf16[54784]{0:T(1024)(128)(2,1)} async-done(((bf16[54784]{0:T(1024)(128)(2,1)}), bf16[54784]{0:T(1024)(128)(2,1)}) %all-reduce.7.cloned.1.call-update) | async-done | bytes 109584
  215.4 8.1 collective-permute-done.1
  234.5 15.2 %collective-permute-done.2 = bf16[2,128,2048]{2,1,0:T(8,128)(2,1)} collective-permute-done((bf16[2,128,2048]{2,1,0:T(8,128)(2,1)}, bf16[2,128,2048]{2,1,0:T(8,128)(2,1)}, u32[]{:S(2)}, u32[]{:S(2)}) %collective-permute-start.2) | collective-permute-done | bytes 1048608 | tf_op jit(solution)/shard_map/ppermute | solution.py:57
  263.8 11.7 %fusion.160 = (bf16[1024,1536]{1,0:T(8,128)(2,1)S(1)}, f32[1024,1536]{1,0:T(8,128)}) fusion(bf16[1024,2048]{1,0:T(8,128)(2,1)} %bitcast.603, bf16[2048,1536]{1,0:T(8,128)(2,1)} %all-gather.6.cloned.1.call-done), kind=kOutput, calls=%fused_computation.530 | convolution fusion | flops 6444023808 | bytes 19922944 | tf_op jit(solution)/shard_map/dot_general | solution.py:18
  298.7 6.3 collective-permute-done.11
  305.1 6.1 collective-permute-done.10
  335.1 18.8 %collective-permute-done.15 = bf16[2,128,2048]{2,1,0:T(8,128)(2,1)} collective-permute-done((bf16[2,128,2048]{2,1,0:T(8,128)(2,1)}, bf16[2,128,2048]{2,1,0:T(8,128)(2,1)}, u32[]{:S(2)}, u32[]{:S(2)}) %collective-permute-start.15) | collective-permute-done | bytes 1048608 | tf_op jit(solution)/shard_map/ppermute | solution.py:57
  357.0 22.2 %collective-permute-done.17 = bf16[2,128,2048]{2,1,0:T(8,128)(2,1)S(1)} collective-permute-done((bf16[2,128,2048]{2,1,0:T(8,128)(2,1)S(1)}, bf16[2,128,2048]{2,1,0:T(8,128)(2,1)S(1)}, u32[]{:S(2)}, u32[]{:S(2)}) %collective-permute-start.17) | collective-permute-done | bytes 1048608 | tf_op jit(solution)/shard_map/ppermute | solution.py:57
  382.1 7.2 collective-permute-done.16
  430.5 12.3 %collective-permute-done.20 = bf16[2,128,2048]{2,1,0:T(8,128)(2,1)} collective-permute-done((bf16[2,128,2048]{2,1,0:T(8,128)(2,1)}, bf16[2,128,2048]{2,1,0:T(8,128)(2,1)}, u32[]{:S(2)}, u32[]{:S(2)}) %collective-permute-start.20) | collective-permute-done | bytes 1048608 | tf_op jit(solution)/shard_map/ppermute | solution.py:57
  450.1 18.7 %fusion.163 = f32[1024,2816]{1,0:T(8,128)} fusion(bf16[1024,2048]{1,0:T(8,128)(2,1)} %bitcast.636, bf16[2048,2816]{1,0:T(8,128)(2,1)} %all-gather.10.cloned.1.call-done), kind=kOutput, calls=%fused_computation.533 | convolution fusion | flops 11811160064 | bytes 27262976 | tf_op jit(solution)/shard_map/dot_general | solution.py:18
  468.8 17.2 %multiply_convert_fusion.1 = (bf16[1024,1408]{1,0:T(8,128)(2,1)}, bf16[1024,1408]{1,0:T(8,128)(2,1)}, bf16[1024,1408]{1,0:T(8,128)(2,1)}) fusion(f32[1024,2816]{1,0:T(8,128)} %fusion.163, bf16[1024,2048]{1,0:T(8,128)(2,1)} %bitcast.634, bf16[1408,2048]{1,0:T(8,128)(2,1)} %all-gather.12.cloned.1.call-done), kind=kOutput, calls=%fused_computation.6 | convolution fusion | flops 5927206912 | bytes 30146560 | tf_op jit(solution)/shard_map/dot_general | solution.py:26
  486.0 8.6 convolution_convert_fusion.5
  499.7 15.8 %convolution_convert_fusion.3 = bf16[1024,2048]{1,0:T(8,128)(2,1)S(1)} fusion(bf16[2048,2816]{1,0:T(8,128)(2,1)} %all-gather.10.cloned.1.call-done, bf16[1024,1408]{1,0:T(8,128)(2,1)} %get-tuple-element.132, bf16[1024,1408]{1,0:T(8,128)(2,1)S(1)} %copy-done.148), kind=kOutput, calls=%fused_computation.20 | convolution fusion | flops 11824791552 | bytes 21495808 | tf_op jit(solution)/shard_map/dot_general | solution.py:26
  545.9 27.6 %collective-permute-done.36 = bf16[2,128,2048]{1,2,0:T(8,128)(2,1)} collective-permute-done((bf16[2,128,2048]{1,2,0:T(8,128)(2,1)}, bf16[2,128,2048]{1,2,0:T(8,128)(2,1)}, u32[]{:S(2)}, u32[]{:S(2)}) %collective-permute-start.36) | collective-permute-done | bytes 1048608 | tf_op jit(solution)/shard_map/ppermute | solution.py:57
  579.7 10.4 collective-permute-done.35
  606.2 6.4 collective-permute-done.38
  622.1 14.0 %collective-permute-done.39 = bf16[2,128,2048]{2,1,0:T(8,128)(2,1)S(1)} collective-permute-done((bf16[2,128,2048]{2,1,0:T(8,128)(2,1)}, bf16[2,128,2048]{2,1,0:T(8,128)(2,1)S(1)}, u32[]{:S(2)}, u32[]{:S(2)}) %collective-permute-start.39) | collective-permute-done | bytes 1048608 | tf_op jit(solution)/shard_map/ppermute | solution.py:57
  642.8 6.5 fusion.24
  669.8 14.2 %collective-permute-done.44 = bf16[144,512]{1,0:T(8,128)(2,1)S(1)} collective-permute-done((bf16[144,512]{1,0:T(8,128)(2,1)}, bf16[144,512]{1,0:T(8,128)(2,1)S(1)}, u32[]{:S(2)}, u32[]{:S(2)}) %collective-permute-start.44) | collective-permute-done | bytes 147488 | tf_op jit(solution)/shard_map/ppermute | solution.py:57
  703.2 11.8 %multiply_reduce_fusion = (f32[2,8,256]{2,1,0:T(8,128)S(1)}, bf16[2,8,256,512]{3,2,1,0:T(8,128)(2,1)}) fusion(f32[2,8,256,512]{3,2,1,0:T(8,128)} %copy-done.2, f32[2,8,256,512]{3,2,1,0:T(8,128)} %constant_dynamic-update-slice_fusion.22), kind=kLoop, calls=%fused_computation.1 | loop fusion | flops 6287360 | bytes 20987904 | tf_op jit(solution)/shard_map/reduce_sum | solution.py:417
  730.2 8.8 convolution_convert_fusion.4
  755.0 16.2 %collective-permute-done.51 = f32[1024,16]{0,1:T(8,128)S(1)} collective-permute-done((f32[1024,16]{0,1:T(8,128)S(1)}, f32[1024,16]{0,1:T(8,128)S(1)}, u32[]{:S(2)}, u32[]{:S(2)}) %collective-permute-start.51) | collective-permute-done | bytes 65568 | tf_op jit(solution)/shard_map/ppermute | solution.py:57
  790.1 5.6 collective-permute-done.48
  816.1 11.6 convolution_convert_fusion.2
  827.7 10.8 convolution_convert_fusion.1
  838.6 18.4 %convolution_convert_fusion = bf16[2048,2816]{1,0:T(8,128)(2,1)} fusion(bf16[1024,2048]{1,0:T(8,128)(2,1)} %bitcast.637, bf16[1024,1408]{1,0:T(8,128)(2,1)} %get-tuple-element.132, bf16[1024,1408]{1,0:T(8,128)(2,1)} %get-tuple-element.131), kind=kOutput, calls=%fused_computation | convolution fusion | flops 11828461568 | bytes 21495808 | tf_op jit(solution)/shard_map/dot_general | solution.py:22
  862.0 126.2 %all-reduce.9.cloned.1.call-done = f32[32,1712]{1,0:T(8,128)} async-done(((f32[32,1712]{1,0:T(8,128)}), f32[32,1712]{1,0:T(8,128)}) %all-reduce.9.cloned.1.call-update) | async-done | bytes 219152
  1007.6 20.1 %collective-permute-start.55 = (bf16[64,1536]{1,0:T(8,128)(2,1)S(1)}, bf16[64,1536]{1,0:T(8,128)(2,1)S(1)}, u32[]{:S(2)}, u32[]{:S(2)}) collective-permute-start(bf16[64,1536]{1,0:T(8,128)(2,1)S(1)} %get-tuple-element.249), channel_id=1, source_target_pairs={{0,18},{1,19},{2,16},{3,17},{4,22},{5,23},{6,20},{7,21},{8,26},{9,... | collective-permute-start | bytes 589832 | tf_op jit(solution)/shard_map/ppermute | solution.py:57
  1032.5 81.0 %reduce-scatter.9.cloned.1.call-done = bf16[256,2816]{1,0:T(8,128)(2,1)} async-done(((bf16[2048,2816]{1,0:T(8,128)(2,1)}), bf16[256,2816]{1,0:T(8,128)(2,1)}) %reduce-scatter.9.cloned.1.call-update) | async-done | bytes 1441808 | tf_op jit(solution)/shard_map/reduce_scatter | solution.py:137
  1127.2 7.0 collective-permute-done.58
  (771 shorter events, 429.2 us)
Async XLA Ops:
  8.0 195.4 %all-reduce.7.cloned.1.call-start = ((), (), s32[]{:S(2)}) async-start(), calls=%async_computation.12 | async-start | bytes 221184
  20.6 243.2 %all-gather.6.cloned.1.call-start = ((), (), s32[]{:S(2)}) async-start(), calls=%async_computation.4 | async-start | bytes 7077888 | tf_op jit(solution)/shard_map/all_gather | solution.py:133
  29.1 250.9 %all-gather.8.cloned.1.call-start = ((), (), s32[]{:S(2)}) async-start(), calls=%async_computation.5 | async-start | bytes 2359296 | tf_op jit(solution)/shard_map/all_gather | solution.py:133
  45.1 163.8 %collective-permute-start.23 = (bf16[64,2816]{1,0:T(8,128)(2,1)}, bf16[64,2816]{1,0:T(8,128)(2,1)}, u32[]{:S(2)}, u32[]{:S(2)}) collective-permute-start(bf16[64,2816]{1,0:T(8,128)(2,1)} %get-tuple-element.199), channel_id=1, source_target_pairs={{0,2},{1,3},{2,0},{3,1},{4,6},{5,7},{6,4},{7,5},{8,10},{9,11},{10,... | collective-permute-start | bytes 1081352 | tf_op jit(solution)/shard_map/ppermute | solution.py:57
  47.5 164.1 %collective-permute-start.24 = (bf16[64,2816]{1,0:T(8,128)(2,1)}, bf16[64,2816]{1,0:T(8,128)(2,1)}, u32[]{:S(2)}, u32[]{:S(2)}) collective-permute-start(bf16[64,2816]{1,0:T(8,128)(2,1)} %get-tuple-element.201), channel_id=1, source_target_pairs={{0,16},{1,17},{2,18},{3,19},{4,20},{5,21},{6,22},{7,23},{8,24},{9,... | collective-permute-start | bytes 1081352 | tf_op jit(solution)/shard_map/ppermute | solution.py:57
  49.1 163.5 %collective-permute-start.25 = (bf16[64,2816]{1,0:T(8,128)(2,1)}, bf16[64,2816]{1,0:T(8,128)(2,1)}, u32[]{:S(2)}, u32[]{:S(2)}) collective-permute-start(bf16[64,2816]{1,0:T(8,128)(2,1)} %get-tuple-element.200), channel_id=1, source_target_pairs={{0,18},{1,19},{2,16},{3,17},{4,22},{5,23},{6,20},{7,21},{8,26},{9,... | collective-permute-start | bytes 1081352 | tf_op jit(solution)/shard_map/ppermute | solution.py:57
  51.4 277.8 %collective-permute-start.30 = (bf16[128,2048]{1,0:T(8,128)(2,1)}, bf16[128,2048]{1,0:T(8,128)(2,1)}, u32[]{:S(2)}, u32[]{:S(2)}) collective-permute-start(bf16[128,2048]{1,0:T(8,128)(2,1)} %get-tuple-element.223), channel_id=1, source_target_pairs={{0,2},{1,3},{2,0},{3,1},{4,6},{5,7},{6,4},{7,5},{8,10},{9,11},{10,... | collective-permute-start | bytes 1572872 | tf_op jit(solution)/shard_map/ppermute | solution.py:57
  53.4 177.4 %collective-permute-start.32 = (bf16[128,2048]{1,0:T(8,128)(2,1)}, bf16[128,2048]{1,0:T(8,128)(2,1)}, u32[]{:S(2)}, u32[]{:S(2)}) collective-permute-start(bf16[128,2048]{1,0:T(8,128)(2,1)} %get-tuple-element.222), channel_id=1, source_target_pairs={{0,16},{1,17},{2,18},{3,19},{4,20},{5,21},{6,22},{7,23},{8,24},{9,... | collective-permute-start | bytes 1572872 | tf_op jit(solution)/shard_map/ppermute | solution.py:57
  55.0 395.1 %all-gather.10.cloned.1.call-start = ((), (), s32[]{:S(2)}) async-start(), calls=%async_computation.6 | async-start | bytes 12976128 | tf_op jit(solution)/shard_map/all_gather | solution.py:133
  215.1 253.7 %all-gather.12.cloned.1.call-start = ((), (), s32[]{:S(2)}) async-start(), calls=%async_computation.7 | async-start | bytes 6488064 | tf_op jit(solution)/shard_map/all_gather | solution.py:133
  224.5 25.2 %collective-permute-start.2 = (bf16[2,128,2048]{2,1,0:T(8,128)(2,1)}, bf16[2,128,2048]{2,1,0:T(8,128)(2,1)}, u32[]{:S(2)}, u32[]{:S(2)}) collective-permute-start(bf16[2,128,2048]{2,1,0:T(8,128)(2,1)} %pad_maximum_fusion.21), channel_id=1, source_target_pairs={{0,16},{1,17},{2,18},{3,19},{4,20},{5,21},{6,22},{7,23},{8,24},{9,... | collective-permute-start | bytes 3145736 | tf_op jit(solution)/shard_map/ppermute | solution.py:57
  228.6 26.4 %collective-permute-start.4 = (bf16[2,128,2048]{2,1,0:T(8,128)(2,1)}, bf16[2,128,2048]{2,1,0:T(8,128)(2,1)}, u32[]{:S(2)}, u32[]{:S(2)}) collective-permute-start(bf16[2,128,2048]{2,1,0:T(8,128)(2,1)} %pad_maximum_fusion.23), channel_id=1, source_target_pairs={{0,2},{1,3},{2,0},{3,1},{4,6},{5,7},{6,4},{7,5},{8,10},{9,11},{10,... | collective-permute-start | bytes 3145736 | tf_op jit(solution)/shard_map/ppermute | solution.py:57
  233.1 99.7 %collective-permute-start.33 = (bf16[2,128,2048]{2,1,0:T(8,128)(2,1)}, bf16[2,128,2048]{2,1,0:T(8,128)(2,1)}, u32[]{:S(2)}, u32[]{:S(2)}) collective-permute-start(bf16[2,128,2048]{2,1,0:T(8,128)(2,1)} %pad_maximum_fusion.34), channel_id=1, source_target_pairs={{0,2},{1,3},{2,0},{3,1},{4,6},{5,7},{6,4},{7,5},{8,10},{9,11},{10,... | collective-permute-start | bytes 3145736 | tf_op jit(solution)/shard_map/ppermute | solution.py:57
  328.4 25.5 %collective-permute-start.15 = (bf16[2,128,2048]{2,1,0:T(8,128)(2,1)}, bf16[2,128,2048]{2,1,0:T(8,128)(2,1)}, u32[]{:S(2)}, u32[]{:S(2)}) collective-permute-start(bf16[2,128,2048]{2,1,0:T(8,128)(2,1)} %dynamic-slice_bitcast_fusion.3), channel_id=1, source_target_pairs={{0,2},{1,3},{2,0},{3,1},{4,6},{5,7},{6,4},{7,5},{8,10},{9,11},{10,... | collective-permute-start | bytes 3145736 | tf_op jit(solution)/shard_map/ppermute | solution.py:57
  329.1 659.0 %all-reduce.9.cloned.1.call-start = ((), (), s32[]{:S(2)}) async-start(), calls=%async_computation.13 | async-start | bytes 458752
  330.6 50.4 %collective-permute-start.31 = (bf16[2,128,2048]{2,1,0:T(8,128)(2,1)S(1)}, bf16[2,128,2048]{2,1,0:T(8,128)(2,1)S(1)}, u32[]{:S(2)}, u32[]{:S(2)}) collective-permute-start(bf16[2,128,2048]{2,1,0:T(8,128)(2,1)S(1)} %pad_maximum_fusion.32), channel_id=1, source_target_pairs={{0,16},{1,17},{2,18},{3,19},{4,20},{5,21},{6,22},{7,23},{8,24},{9,... | collective-permute-start | bytes 3145736 | tf_op jit(solution)/shard_map/ppermute | solution.py:57
  331.5 47.7 %collective-permute-start.17 = (bf16[2,128,2048]{2,1,0:T(8,128)(2,1)S(1)}, bf16[2,128,2048]{2,1,0:T(8,128)(2,1)S(1)}, u32[]{:S(2)}, u32[]{:S(2)}) collective-permute-start(bf16[2,128,2048]{2,1,0:T(8,128)(2,1)S(1)} %dynamic-slice_bitcast_fusion.2), channel_id=1, source_target_pairs={{0,16},{1,17},{2,18},{3,19},{4,20},{5,21},{6,22},{7,23},{8,24},{9,... | collective-permute-start | bytes 3145736 | tf_op jit(solution)/shard_map/ppermute | solution.py:57
  355.6 33.7 %collective-permute-start.16 = (bf16[128,2048]{1,0:T(8,128)(2,1)S(1)}, bf16[128,2048]{1,0:T(8,128)(2,1)S(1)}, u32[]{:S(2)}, u32[]{:S(2)}) collective-permute-start(bf16[128,2048]{1,0:T(8,128)(2,1)S(1)} %fusion.55), channel_id=1, source_target_pairs={{0,16},{1,17},{2,18},{3,19},{4,20},{5,21},{6,22},{7,23},{8,24},{9,... | collective-permute-start | bytes 1572872 | tf_op jit(solution)/shard_map/ppermute | solution.py:57
  413.0 29.9 %collective-permute-start.20 = (bf16[2,128,2048]{2,1,0:T(8,128)(2,1)}, bf16[2,128,2048]{2,1,0:T(8,128)(2,1)}, u32[]{:S(2)}, u32[]{:S(2)}) collective-permute-start(bf16[2,128,2048]{2,1,0:T(8,128)(2,1)} %pad_maximum_fusion.27), channel_id=1, source_target_pairs={{0,16},{1,17},{2,18},{3,19},{4,20},{5,21},{6,22},{7,23},{8,24},{9,... | collective-permute-start | bytes 3145736 | tf_op jit(solution)/shard_map/ppermute | solution.py:57
  498.9 37.6 %collective-permute-start.26 = (bf16[2,128,2048]{2,1,0:T(8,128)(2,1)}, bf16[2,128,2048]{2,1,0:T(8,128)(2,1)}, u32[]{:S(2)}, u32[]{:S(2)}) collective-permute-start(bf16[2,128,2048]{2,1,0:T(8,128)(2,1)} %dynamic-slice_bitcast_fusion.1), channel_id=1, source_target_pairs={{0,2},{1,3},{2,0},{3,1},{4,6},{5,7},{6,4},{7,5},{8,10},{9,11},{10,... | collective-permute-start | bytes 3145736 | tf_op jit(solution)/shard_map/ppermute | solution.py:57
  524.6 51.2 %collective-permute-start.28 = (bf16[2,128,2048]{2,1,0:T(8,128)(2,1)}, bf16[2,128,2048]{2,1,0:T(8,128)(2,1)}, u32[]{:S(2)}, u32[]{:S(2)}) collective-permute-start(bf16[2,128,2048]{2,1,0:T(8,128)(2,1)} %dynamic-slice_bitcast_fusion), channel_id=1, source_target_pairs={{0,16},{1,17},{2,18},{3,19},{4,20},{5,21},{6,22},{7,23},{8,24},{9,... | collective-permute-start | bytes 3145736 | tf_op jit(solution)/shard_map/ppermute | solution.py:57
  533.6 39.8 %collective-permute-start.36 = (bf16[2,128,2048]{1,2,0:T(8,128)(2,1)}, bf16[2,128,2048]{1,2,0:T(8,128)(2,1)}, u32[]{:S(2)}, u32[]{:S(2)}) collective-permute-start(bf16[2,128,2048]{1,2,0:T(8,128)(2,1)} %bitcast.663), channel_id=1, source_target_pairs={{0,16},{1,17},{2,18},{3,19},{4,20},{5,21},{6,22},{7,23},{8,24},{9,... | collective-permute-start | bytes 3145736 | tf_op jit(solution)/shard_map/ppermute | solution.py:57
  539.5 57.9 %collective-permute-start.27 = (bf16[128,2048]{1,0:T(8,128)(2,1)}, bf16[128,2048]{1,0:T(8,128)(2,1)}, u32[]{:S(2)}, u32[]{:S(2)}) collective-permute-start(bf16[128,2048]{1,0:T(8,128)(2,1)} %fusion.57), channel_id=1, source_target_pairs={{0,16},{1,17},{2,18},{3,19},{4,20},{5,21},{6,22},{7,23},{8,24},{9,... | collective-permute-start | bytes 1572872 | tf_op jit(solution)/shard_map/ppermute | solution.py:57
  544.3 45.9 %collective-permute-start.35 = (bf16[128,2048]{0,1:T(8,128)(2,1)S(1)}, bf16[128,2048]{0,1:T(8,128)(2,1)S(1)}, u32[]{:S(2)}, u32[]{:S(2)}) collective-permute-start(bf16[128,2048]{0,1:T(8,128)(2,1)S(1)} %fusion.59), channel_id=1, source_target_pairs={{0,16},{1,17},{2,18},{3,19},{4,20},{5,21},{6,22},{7,23},{8,24},{9,... | collective-permute-start | bytes 1572872 | tf_op jit(solution)/shard_map/ppermute | solution.py:57
  744.3 35.8 %collective-permute-start.47 = (bf16[2,128,2048]{1,2,0:T(8,128)(2,1)}, bf16[2,128,2048]{1,2,0:T(8,128)(2,1)}, u32[]{:S(2)}, u32[]{:S(2)}) collective-permute-start(bf16[2,128,2048]{1,2,0:T(8,128)(2,1)} %bitcast.660), channel_id=1, source_target_pairs={{0,2},{1,3},{2,0},{3,1},{4,6},{5,7},{6,4},{7,5},{8,10},{9,11},{10,... | collective-permute-start | bytes 3145736 | tf_op jit(solution)/shard_map/ppermute | solution.py:57
  753.8 30.2 %collective-permute-start.49 = (bf16[2,128,2048]{1,2,0:T(8,128)(2,1)}, bf16[2,128,2048]{1,2,0:T(8,128)(2,1)}, u32[]{:S(2)}, u32[]{:S(2)}) collective-permute-start(bf16[2,128,2048]{1,2,0:T(8,128)(2,1)} %bitcast.661), channel_id=1, source_target_pairs={{0,16},{1,17},{2,18},{3,19},{4,20},{5,21},{6,22},{7,23},{8,24},{9,... | collective-permute-start | bytes 3145736 | tf_op jit(solution)/shard_map/ppermute | solution.py:57
  808.5 184.1 %reduce-scatter.7.cloned.1.call-start = ((), (), s32[]{:S(2)}) async-start(), calls=%async_computation.9 | async-start | bytes 2359296 | tf_op jit(solution)/shard_map/reduce_scatter | solution.py:137
  814.6 179.6 %reduce-scatter.5.cloned.1.call-start = ((), (), s32[]{:S(2)}) async-start(), calls=%async_computation.8 | async-start | bytes 7077888 | tf_op jit(solution)/shard_map/reduce_scatter | solution.py:137
  827.7 176.2 %reduce-scatter.11.cloned.1.call-start = ((), (), s32[]{:S(2)}) async-start(), calls=%async_computation.11 | async-start | bytes 6488064 | tf_op jit(solution)/shard_map/reduce_scatter | solution.py:137
  838.5 274.9 %reduce-scatter.9.cloned.1.call-start = ((), (), s32[]{:S(2)}) async-start(), calls=%async_computation.10 | async-start | bytes 12976128 | tf_op jit(solution)/shard_map/reduce_scatter | solution.py:137
  995.6 32.2 %collective-permute-start.53 = (bf16[64,1536]{1,0:T(8,128)(2,1)S(1)}, bf16[64,1536]{1,0:T(8,128)(2,1)S(1)}, u32[]{:S(2)}, u32[]{:S(2)}) collective-permute-start(bf16[64,1536]{1,0:T(8,128)(2,1)S(1)} %get-tuple-element.248), channel_id=1, source_target_pairs={{0,2},{1,3},{2,0},{3,1},{4,6},{5,7},{6,4},{7,5},{8,10},{9,11},{10,... | collective-permute-start | bytes 589832 | tf_op jit(solution)/shard_map/ppermute | solution.py:57
  1007.6 24.4 %collective-permute-start.55 = (bf16[64,1536]{1,0:T(8,128)(2,1)S(1)}, bf16[64,1536]{1,0:T(8,128)(2,1)S(1)}, u32[]{:S(2)}, u32[]{:S(2)}) collective-permute-start(bf16[64,1536]{1,0:T(8,128)(2,1)S(1)} %get-tuple-element.249), channel_id=1, source_target_pairs={{0,18},{1,19},{2,16},{3,17},{4,22},{5,23},{6,20},{7,21},{8,26},{9,... | collective-permute-start | bytes 589832 | tf_op jit(solution)/shard_map/ppermute | solution.py:57
  (187 other events, 2785.6 us)
Sparse Core Ops, SparseCore 0:
  20.7 182.6 all-reduce.6
  808.6 179.5 all-reduce.8
Sparse Core Ops, SparseCore 1:
  29.2 69.9 all-gather.5
  100.6 30.4 all-gather.7
  215.2 112.3 all-gather.9
  329.3 68.7 all-gather.11
  814.7 35.4 reduce-scatter.6
  852.4 69.1 reduce-scatter.4
  923.8 64.2 reduce-scatter.10
  990.2 123.2 reduce-scatter.8

commit v2 on v1

v2 whole, which is shorter than its diff:
```python
import jax
import jax.numpy as jnp
from jax import lax
from jax.experimental import pallas as pl
from jax.experimental.pallas import tpu as pltpu
from jax.sharding import PartitionSpec as P

SPAN = 64
HK = 256
HV = 512
HEADS = 4
EPS = 1e-06
GATE_SCALE = 16.0
BOTH = ("seq", "fsdp")
F32 = jnp.float32
BF16 = jnp.bfloat16


def dot(left, right):
    return jnp.dot(left, right, preferred_element_type=F32)


def dot_rows(left, right):
    return lax.dot_general(left, right, (((0,), (0,)), ((), ())), preferred_element_type=F32)


def dot_cols(left, right):
    return lax.dot_general(left, right, (((1,), (1,)), ((), ())), preferred_element_type=F32)


def ein(form, left, right):
    return jnp.einsum(form, left, right, preferred_element_type=F32)


class Place:
    def __init__(self):
        self.fsdp = lax.axis_size("fsdp")
        self.line_size = self.fsdp // 4
        index = lax.axis_index("fsdp")
        self.seq = lax.axis_index("seq")
        self.core = index % 2
        self.side = (index // 2) % 2
        self.line = index // 4
        self.groups = [
            [4 * a + 2 * b + c for a in range(self.line_size) for c in range(2)] for b in range(2)
        ]

    def send(self, value, move, when=lambda a: True):
        pairs = []
        for s in range(2):
            for a in range(self.line_size):
                for b in range(2):
                    for c in range(2):
                        to = move(s, a, b, c)
                        if 0 <= to[1] < self.line_size and when(a):
                            source = s * self.fsdp + 4 * a + 2 * b + c
                            target = to[0] * self.fsdp + 4 * to[1] + 2 * to[2] + to[3]
                            pairs.append((source, target))
        return lax.ppermute(value, BOTH, pairs)

    def over_side(self, value):
        return self.send(value, lambda s, a, b, c: (s, a, 1 - b, c))

    def over_seq(self, value):
        return self.send(value, lambda s, a, b, c: (1 - s, a, b, c))

    def over_both(self, value):
        return self.send(value, lambda s, a, b, c: (1 - s, a, 1 - b, c))

    def over_core(self, value):
        return self.send(value, lambda s, a, b, c: (s, a, b, 1 - c))

    def along(self, value, step, when=lambda a: True):
        return self.send(value, lambda s, a, b, c: (s, a + step, b, c), when)

    def swap_top(self, value):
        half = self.line_size // 2
        return self.send(value, lambda s, a, b, c: (s, b * half + a % half, a // half, c))


def pair(which, own, other):
    first = which == 0
    return jnp.stack([jnp.where(first, own, other), jnp.where(first, other, own)])


def send_quarters(here, blocks):
    me = 2 * here.seq + here.side
    return (
        take(blocks, me),
        here.over_side(take(blocks, me ^ 1)),
        here.over_seq(take(blocks, me ^ 2)),
        here.over_both(take(blocks, me ^ 3)),
    )


def join_quarters(here, own, side, seq, both):
    rows = pair(here.seq, pair(here.side, own, side), pair(here.side, seq, both))
    return rows.reshape((4,) + own.shape)


def phase(*values):
    return lax.optimization_barrier(values)


def after(value, *others):
    return lax.optimization_barrier((value,) + others)[0]


def take(array, index, axis=0):
    return lax.dynamic_index_in_dim(array, index, axis, keepdims=False)


def near_halves(here, rows):
    half = rows.shape[0] // 2
    top, low = rows[:half], rows[half:]
    return jnp.stack([top, here.over_side(top)]), jnp.stack([low, here.over_seq(low)])


def far_halves(here, top_pair, low_pair):
    return here.over_seq(top_pair), here.over_side(low_pair)


def in_stream(here, top_pair, low_pair, top_far, low_far):
    own = jnp.stack([top_pair[0], low_pair[0]])
    side = jnp.stack([top_pair[1], low_far[0]])
    seq = jnp.stack([top_far[0], low_pair[1]])
    both = jnp.stack([top_far[1], low_far[1]])
    out = jnp.concatenate([pair(here.seq, own, seq), pair(here.seq, side, both)])
    return out.reshape(-1, out.shape[-1])


def gather_loose(here, rows):
    top_pair, low_pair = near_halves(here, rows)
    top_far, low_far = far_halves(here, top_pair, low_pair)
    parts = (top_pair, top_far, low_pair, low_far)
    return jnp.concatenate([p.reshape(-1, rows.shape[1]) for p in parts])


def in_loose(rows, side, seq, both):
    half = rows.shape[0] // 2
    top = [rows[:half], side[:half], seq[:half], both[:half]]
    low = [rows[half:], seq[half:], side[half:], both[half:]]
    return jnp.concatenate(top + low)


def near_sums(here, top, low):
    return top[:, 0], here.over_side(top[:, 1]), low[:, 0], here.over_seq(low[:, 1])


def far_sums(here, top, top_in, low, low_in):
    top_sum = top.astype(F32) + top_in.astype(F32)
    low_sum = low.astype(F32) + low_in.astype(F32)
    top_far = here.over_seq(top_sum[1].astype(BF16))
    low_far = here.over_side(low_sum[1].astype(BF16))
    return jnp.concatenate(
        [top_sum[0] + top_far.astype(F32), low_sum[0] + low_far.astype(F32)]
    )


def loose_parts(rows):
    parts = rows.reshape(2, 2, 2, -1, rows.shape[1])
    return parts[0], parts[1]


def stream_parts(here, rows):
    parts = rows.reshape(2, 2, 2, -1, rows.shape[1])
    own, other = take(parts, here.seq, 1), take(parts, 1 - here.seq, 1)
    top = jnp.stack([own[:, 0], other[:, 0]])
    low = jnp.stack([own[:, 1], other[:, 1]], axis=1)
    return top, low


def gather_line(here, rows):
    return lax.all_gather(rows, "fsdp", axis=0, tiled=True, axis_index_groups=here.groups)


def scatter_line(here, rows):
    return lax.psum_scatter(
        rows, "fsdp", scatter_dimension=0, tiled=True, axis_index_groups=here.groups
    )


def gather_small_plane(here, rows):
    rows = pair(here.side, rows, here.over_side(rows))
    rows = pair(here.seq, rows, here.over_seq(rows))
    return rows.transpose(0, 2, 1, 3, 4).reshape(2 * here.fsdp, -1)


def scatter_small_plane(here, rows):
    parts = rows.reshape(2, here.line_size, 2, 2, -1)
    parts = take(parts, here.seq) + here.over_seq(take(parts, 1 - here.seq))
    return take(parts, here.side, 1) + here.over_side(take(parts, 1 - here.side, 1))


def tile_order(line):
    pairs = []
    for q in range(2):
        for a in range(line):
            first = (q * line + a) * 2
            pairs.append(((first, first + 1), ((2 * a) * 2 + q, (2 * a + 1) * 2 + q)))
    return pairs


def swap_halves(first, second):
    left = lax.broadcasted_iota(jnp.int32, first.shape, 1) < 64
    low = jnp.where(left, first, pltpu.roll(second, 64, 1))
    high = jnp.where(left, pltpu.roll(first, 64, 1), second)
    return low, high


def columns(tile):
    return pl.ds(128 * tile, 128)


def rows_call(kernel, rows, outs, *arrays):
    block = 64
    count = rows // block

    def spec(shape):
        if shape[0] == rows:
            return pl.BlockSpec((block,) + shape[1:], lambda i: (i, 0))
        return pl.BlockSpec(shape, lambda i: (0, 0))

    moved = sum(a.size * a.dtype.itemsize for a in arrays)
    return pl.pallas_call(
        kernel,
        grid=(count,),
        in_specs=[spec(a.shape) for a in arrays],
        out_specs=[spec(shape) for shape, _ in outs],
        out_shape=[jax.ShapeDtypeStruct(*o) for o in outs],
        compiler_params=pltpu.CompilerParams(vmem_limit_bytes=32 * 2**20),
        cost_estimate=pl.CostEstimate(flops=0, bytes_accessed=2 * moved, transcendentals=0),
    )(*arrays)


def to_gathered(x, line):
    rows, model = x.shape
    size = model // (8 * line)
    if size != 64 or rows % 64:
        parts = x.reshape(rows, 2, line, 2, 2, size)
        return parts.transpose(0, 2, 4, 1, 3, 5).reshape(rows, model)

    def kernel(x_ref, out_ref):
        for (one, two), (low, high) in tile_order(line):
            got = swap_halves(
                x_ref[:, columns(one)].astype(F32), x_ref[:, columns(two)].astype(F32)
            )
            out_ref[:, columns(low)] = got[0].astype(out_ref.dtype)
            out_ref[:, columns(high)] = got[1].astype(out_ref.dtype)

    return rows_call(kernel, rows, [(x.shape, x.dtype)], x)[0]


def norm_forward(x, add, gain, line):
    rows, model = x.shape
    size = model // (8 * line)
    if size != 64 or rows % 64:
        total = x.astype(F32) + add
        scale = lax.rsqrt(jnp.mean(total * total, axis=-1, keepdims=True) + EPS)
        return total, to_gathered((total * scale * gain).astype(BF16), line)

    def kernel(x_ref, add_ref, gain_ref, total_ref, out_ref):
        total = x_ref[...].astype(F32) + add_ref[...]
        total_ref[...] = total
        scale = lax.rsqrt(jnp.mean(total * total, axis=-1, keepdims=True) + EPS)
        for (one, two), (low, high) in tile_order(line):
            cut = [
                total_ref[:, columns(t)] * scale * gain_ref[:, columns(t)] for t in (one, two)
            ]
            got = swap_halves(*cut)
            out_ref[:, columns(low)] = got[0].astype(BF16)
            out_ref[:, columns(high)] = got[1].astype(BF16)

    outs = [(x.shape, F32), (x.shape, BF16)]
    return rows_call(kernel, rows, outs, x, add, gain)


def norm_backward(grad, extra, x, base, gain, line, narrow):
    rows, model = x.shape
    size = model // (8 * line)
    plain = size != 64 or rows % 64 != 0
    if plain:
        parts = grad.reshape(rows, line, 2, 2, 2, size)
        grad = parts.transpose(0, 3, 1, 4, 2, 5).reshape(rows, model)

    def whole(grad, x, base, gain):
        x = x.astype(F32)
        scale = lax.rsqrt(jnp.mean(x * x, axis=-1, keepdims=True) + EPS)
        scaled = gain * grad
        mean = jnp.mean(scaled * x, axis=-1, keepdims=True)
        out = base.astype(F32) + scale * scaled - x * (scale * scale * scale * mean)
        return out, jnp.sum(grad * x * scale, axis=0, keepdims=True)

    if plain:
        out, term = whole(grad if extra is None else grad + extra, x, base, gain)
        return (out.astype(BF16), term) if narrow else (out, out.astype(BF16), term)

    def kernel(*refs):
        grad_ref, refs = refs[0], refs[1:]
        extra_ref = None
        if extra is not None:
            extra_ref, refs = refs[0], refs[1:]
        x_ref, base_ref, gain_ref, refs = refs[0], refs[1], refs[2], refs[3:]
        held_ref, term_ref, refs = refs[0], refs[1], refs[2:]
        for (one, two), (low, high) in tile_order(line):
            got = swap_halves(grad_ref[:, columns(low)], grad_ref[:, columns(high)])
            for tile, part in zip((one, two), got):
                if extra_ref is not None:
                    part = part + extra_ref[:, columns(tile)]
                held_ref[:, columns(tile)] = part
        out, term = whole(held_ref[...], x_ref[...], base_ref[...], gain_ref[...])
        held_ref[...] = out
        for ref in refs:
            ref[...] = out.astype(BF16)

        @pl.when(pl.program_id(0) == 0)
        def _():
            term_ref[...] = term

        @pl.when(pl.program_id(0) > 0)
        def _():
            term_ref[...] += term

    arrays = [grad] + ([] if extra is None else [extra]) + [x, base, gain]
    outs = [(x.shape, F32), ((1, model), F32), (x.shape, BF16)]
    wide, term, low = rows_call(kernel, rows, outs, *arrays)
    return (low, term) if narrow else (wide, low, term)


def in_side_order(here, two):
    return jnp.where(here.side == 0, two, two[::-1])


def carry_states(here, states, decays, backward):
    states, decays = in_side_order(here, states), in_side_order(here, decays)
    other_states = here.over_core(states.astype(BF16)).astype(F32)
    other_decays = here.over_core(decays)
    first = here.core == 0
    state_at = [jnp.where(first, states, other_states), jnp.where(first, other_states, states)]
    decay_at = [jnp.where(first, decays, other_decays), jnp.where(first, other_decays, decays)]
    order = [(j, c) for j in range(2) for c in range(2)]
    if backward:
        order = order[::-1]
    parts = [(state_at[c][j], decay_at[c][j]) for j, c in order]
    total, through = parts[0]
    for state, decay in parts[1:]:
        total = decay * total + state
        through = through * decay
    half = total.shape[0] // 2
    mine = lax.dynamic_slice_in_dim(total, here.core * half, half, 0)
    row = jnp.pad(through[None, :], ((0, 15), (0, 0)))
    packed = jnp.concatenate([mine, row]).astype(BF16)
    entering = jnp.zeros_like(mine)
    for step in range(here.line_size - 1, 0, -1):
        came = here.along(packed, -step if backward else step).astype(F32)
        entering = came[half] * entering + came[:half]
    entering = pair(here.core, entering, here.over_core(entering)).reshape(total.shape)
    at = {}
    for (j, c), (state, decay) in zip(order, parts):
        at[j, c] = entering
        entering = decay * entering + state
    out = jnp.where(first, jnp.stack([at[0, 0], at[1, 0]]), jnp.stack([at[0, 1], at[1, 1]]))
    return in_side_order(here, out)


def recurrence_backward(
    leaving, out_grad, values, expanded, shrunk, ending, scores, states, running, logits, decay,
    count, flags,
):
    spans, length, width = running.shape
    value_width = values.shape[-1]
    segments = leaving.shape[0]
    per_seg = spans // segments

    def kernel(
        leaving_ref, o_ref, v_ref, exp_ref, shr_ref, end_ref, score_ref, state_ref, run_ref,
        logit_ref, decay_ref, count_ref, row_ref, flag_ref, grads_ref, logit_grad_ref, carry,
    ):
        @pl.when(pl.program_id(1) == 0)
        def _():
            carry[...] = leaving_ref[0]

        def nt(a, b):
            return lax.dot_general(a, b, (((1,), (1,)), ((), ())), preferred_element_type=F32)

        def tn(a, b):
            return lax.dot_general(a, b, (((0,), (0,)), ((), ())), preferred_element_type=F32)

        o, v = o_ref[0], v_ref[0]
        expanded, shrunk, ending = exp_ref[0], shr_ref[0], end_ref[0]
        state, score = state_ref[0], score_ref[0]
        counts, count_row = count_ref[0], row_ref[0]
        unfinished = counts == 0.0
        tail = counts == counts[length - 1 :]
        above = lax.broadcasted_iota(jnp.int32, (length, length), 0)
        below = lax.broadcasted_iota(jnp.int32, (length, length), 1)
        mask = (counts == count_row) & (above >= below)
        later = carry[...]
        later_low = later.astype(BF16)

        score_grad = jnp.where(mask, nt(o, v), 0.0).astype(BF16)
        expanded_grad = dot(score_grad, shrunk) + jnp.where(unfinished, dot(o, state), 0.0)
        shrunk_grad = tn(score_grad, expanded)
        ending_grad = dot(v, later_low)
        value_grad = tn(score, o) + nt(ending, later_low)
        running = run_ref[0]
        to_end = jnp.where(tail, jnp.exp(running[length - 1 :] - running), 0.0)
        query_grad = expanded_grad * jnp.exp(running) * HK ** (-0.5)
        key_grad = shrunk_grad * jnp.exp(-running) + ending_grad * to_end
        grads_ref[:, :width] = query_grad.astype(BF16)
        grads_ref[:, width : 2 * width] = key_grad.astype(BF16)
        grads_ref[:, 2 * width :] = value_grad.astype(BF16)

        from_here = expanded.astype(F32) * expanded_grad - shrunk.astype(F32) * shrunk_grad
        from_past = ending.astype(F32) * ending_grad
        decay = decay_ref[0]
        carried = decay * jnp.sum(state.astype(F32) * later, axis=0, keepdims=True)
        upper = (below >= above).astype(F32)
        lower = (below < above).astype(F32)
        decay_grad = carried
        for triangle, terms in ((upper, from_here), (lower, from_past)):
            decay_grad = decay_grad + jnp.dot(
                triangle, terms, precision=lax.Precision.HIGHEST, preferred_element_type=F32
            )
        decay_grad = decay_grad * (1.0 - flag_ref[0])
        logits = logit_ref[0]
        logit_grad_ref[...] = (decay_grad * jax.nn.sigmoid(-logits) / GATE_SCALE).astype(BF16)

        reach = jnp.where(unfinished, expanded.astype(F32), 0.0).astype(BF16)
        carry[...] = decay * later + tn(o, reach)

    def at(j, c):
        return j * per_seg + per_seg - 1 - c

    def spec(array):
        return pl.BlockSpec((1,) + array.shape[1:], lambda j, c: (at(j, c), 0, 0))

    arrays = [
        out_grad, values, expanded, shrunk, ending, scores, states, running, logits,
        decay.reshape(spans, 1, width), count.reshape(spans, length, 1),
        count.reshape(spans, 1, length), flags.reshape(spans, length, 1),
    ]
    moved = sum(a.size * a.dtype.itemsize for a in arrays)
    tall = 2 * width + value_width
    return pl.pallas_call(
        kernel,
        grid=(segments, per_seg),
        in_specs=[pl.BlockSpec((1, value_width, width), lambda j, c: (j, 0, 0))]
        + [spec(a) for a in arrays],
        out_specs=[
            pl.BlockSpec((length, tall), lambda j, c: (at(j, c), 0)),
            pl.BlockSpec((length, width), lambda j, c: (at(j, c), 0)),
        ],
        out_shape=[
            jax.ShapeDtypeStruct((spans * length, tall), BF16),
            jax.ShapeDtypeStruct((spans * length, width), BF16),
        ],
        scratch_shapes=[pltpu.VMEM((value_width, width), F32)],
        compiler_params=pltpu.CompilerParams(vmem_limit_bytes=32 * 2**20),
        cost_estimate=pl.CostEstimate(
            flops=10 * spans * length * width * value_width,
            bytes_accessed=moved,
            transcendentals=4 * running.size,
        ),
    )(leaving, *arrays)


def on_device(
    tokens,
    attn_gain,
    w_query,
    w_key,
    w_value,
    w_down_rank,
    w_up_rank,
    gate_bias,
    w_outgate,
    head_gain,
    w_output,
    ffn_gain,
    w_gate,
    w_up,
    w_down,
    doc_starts,
    cotangent,
):
    here = Place()
    line = here.line_size
    tok, model = tokens.shape
    rows_d = w_query.shape[0]
    rows_f = w_down.shape[0]
    rank = w_up_rank.shape[0]
    cols_k = w_up_rank.shape[1]
    group = 4 * tok
    spans = group // SPAN
    per_seg = spans // 2
    me = 2 * here.seq + here.side

    small = jnp.concatenate(
        [
            attn_gain,
            ffn_gain,
            head_gain,
            gate_bias,
            w_up_rank.reshape(-1),
            w_down_rank.reshape(-1),
        ]
    )
    small_size = small.shape[0]
    small_rows = 8 * -(-small_size // (8 * model))
    small = jnp.pad(small, (0, small_rows * model - small_size)).reshape(small_rows, model)
    out_lines = gather_line(here, jnp.concatenate([here.swap_top(w_output), small]))
    out_lines = out_lines.reshape(line, 2, rows_d + small_rows, model)
    small_line = out_lines[:, :, rows_d:].reshape(line, 2, -1)[:, :, :small_size]
    w_out = out_lines[:, :, :rows_d].reshape(2, line // 2, 2 * rows_d, model)
    w_out = w_out.transpose(1, 0, 2, 3).reshape(HV, model)

    def heads_first(w, width):
        return w.reshape(rows_d, HEADS, width).transpose(1, 0, 2)

    def hidden_first(w):
        return (
            w.reshape(rows_d, 2, line, 2, 2, rows_f)
            .transpose(1, 3, 0, 2, 4, 5)
            .reshape(4, rows_d, -1)
        )

    quarter = 2 * line * rows_f
    mixer_cols = jnp.concatenate(
        [
            heads_first(w_query, HK),
            heads_first(w_key, HK),
            heads_first(w_value, HV),
            heads_first(w_outgate, HV),
        ],
        axis=2,
    )
    *mixer_quarters, tokens_in, w_gate, w_up = phase(
        *send_quarters(here, mixer_cols), to_gathered(tokens, line), w_gate, w_up
    )
    mixer_piece = join_quarters(here, *mixer_quarters).reshape(4 * rows_d, -1)
    w_mixer = gather_line(here, mixer_piece)
    other_docs = here.over_side(doc_starts)
    top_pair, low_pair, small_line, gate_cols, other_docs, w_up = phase(
        *near_halves(here, tokens_in), small_line, hidden_first(w_gate), other_docs, w_up
    )
    small_all = gather_small_plane(here, small_line)
    small_all, top_pair, low_pair, up_cols = phase(
        small_all, top_pair, low_pair, hidden_first(w_up)
    )
    ffn_cols = jnp.concatenate([gate_cols, up_cols], axis=2)
    top_far, low_far, ffn_cols, top_pair, low_pair = phase(
        *far_halves(here, top_pair, low_pair), ffn_cols, top_pair, low_pair
    )
    ffn_quarters = send_quarters(here, ffn_cols)
    wide_in = in_stream(here, top_pair, low_pair, top_far, low_far).astype(F32)
    cuts = []
    at = 0
    for size in (rows_d, rows_d, head_gain.shape[0], cols_k, rank * cols_k, rows_d * rank):
        cuts.append(small_all[:, at : at + size])
        at += size
    devices = small_all.shape[0]
    full_attn_gain = cuts[0].reshape(model).astype(F32)
    full_ffn_gain = cuts[1].reshape(model).astype(F32)
    full_head_gain = cuts[2].reshape(HV).astype(F32)
    full_bias = cuts[3].reshape(HEADS * HK)
    full_up_rank = cuts[4].reshape(devices, rank, cols_k).transpose(1, 0, 2).reshape(rank, -1)
    full_down_rank = cuts[5].reshape(model, rank)
    my_bias = lax.dynamic_slice_in_dim(full_bias, me * HK, HK, 0).astype(F32)
    my_up_rank = lax.dynamic_slice_in_dim(full_up_rank, me * HK, HK, 1)
    down_rank_rows = (
        full_down_rank.reshape(2, line, 2, 2, rows_d, rank)
        .transpose(1, 3, 0, 2, 4, 5)
        .reshape(model, rank)
    )

    wide_scale = lax.rsqrt(jnp.mean(wide_in * wide_in, axis=-1, keepdims=True) + EPS)
    x_in = (wide_in * wide_scale * to_gathered(full_attn_gain[None], line)).astype(BF16)
    rank_low = dot(x_in, down_rank_rows).astype(BF16)
    *ffn_quarters, x_in, rank_low, cotangent, w_down = phase(
        *ffn_quarters, x_in, rank_low, cotangent, w_down
    )
    ffn_piece = join_quarters(here, *ffn_quarters).reshape(4 * rows_d, -1)
    w_ffn = gather_line(here, ffn_piece)
    w_dn = gather_line(here, after(w_down, ffn_piece))
    cot_parts = here.over_side(cotangent), here.over_seq(cotangent), here.over_both(cotangent)

    inputs = tokens.astype(F32)
    scale_in = lax.rsqrt(jnp.mean(inputs * inputs, axis=-1, keepdims=True) + EPS)
    normed_in = (inputs * scale_in * full_attn_gain).astype(BF16)
    docs = jnp.stack([doc_starts, other_docs])
    flags = (jnp.arange(tok, dtype=jnp.int32) == docs[:, :, None]).astype(F32)
    flags = flags.reshape(spans, SPAN)

    projected = dot(x_in, w_mixer)
    queries = projected[:, :HK].astype(BF16)
    keys_in = projected[:, HK : 2 * HK].astype(BF16)
    values = projected[:, 2 * HK : 2 * HK + HV].astype(BF16)
    outgate = projected[:, 2 * HK + HV :]
    logits = (dot(rank_low, my_up_rank) + my_bias).astype(BF16).astype(F32)

    decays = (jax.nn.log_sigmoid(logits) / GATE_SCALE).reshape(spans, SPAN, HK)
    causal = jnp.tril(jnp.ones((SPAN, SPAN), F32))
    running = jnp.einsum("ts,nsk->ntk", causal, decays, precision=lax.Precision.HIGHEST)
    count = jnp.einsum("ts,ns->nt", causal, flags, precision=lax.Precision.HIGHEST)
    closing = running[:, -1, :]
    unfinished = (count == 0.0)[:, :, None]
    tail = (count == count[:, -1:])[:, :, None]
    unbroken = count[:, -1:] == 0.0
    mask = (count[:, :, None] == count[:, None, :]) & (causal > 0)[None]
    q_s = queries.reshape(spans, SPAN, HK).astype(F32) * HK ** (-0.5)
    k_s = keys_in.reshape(spans, SPAN, HK).astype(F32)
    v_s = values.reshape(spans, SPAN, HV)
    grow = jnp.exp(running)
    shrink = jnp.exp(-running)
    to_end = jnp.where(tail, jnp.exp(closing[:, None, :] - running), 0.0)
    expanded = q_s * grow
    shrunk = k_s * shrink
    ending = k_s * to_end
    expanded_low = expanded.astype(BF16)
    shrunk_low = shrunk.astype(BF16)
    ending_low = ending.astype(BF16)
    reach_low = jnp.where(unfinished, expanded, 0.0).astype(BF16)
    exact = lax.Precision.HIGHEST
    wide_scores = jnp.einsum("ntk,nsk->nts", expanded, shrunk, precision=exact)
    wide_scores = jnp.where(mask, wide_scores, 0.0)
    scores = wide_scores.astype(BF16)
    span_decay = jnp.where(unbroken, jnp.exp(closing), 0.0).reshape(2, per_seg, HK)
    updates = ein("ntv,ntk->nvk", v_s, ending_low).reshape(2, per_seg, HV, HK)

    before = [jnp.ones((2, HK), F32)]
    for c in range(per_seg):
        before.append(before[-1] * span_decay[:, c])
    through = before[-1]
    before = jnp.stack(before[:-1], axis=1)
    rest = [jnp.ones((2, HK), F32)]
    for c in range(per_seg - 1, 0, -1):
        rest.append(rest[-1] * span_decay[:, c])
    rest = jnp.stack(rest[::-1], axis=1)
    seg_ending = (ending.reshape(2, per_seg, SPAN, HK) * rest[:, :, None, :]).astype(BF16)
    seg_ending = seg_ending.reshape(2, per_seg * SPAN, HK)
    seg_values = values.reshape(2, per_seg * SPAN, HV)
    seg_end = ein("jtv,jtk->jvk", seg_values, seg_ending)
    *cot_parts, seg_end = phase(*cot_parts, seg_end)
    cot = in_loose(cotangent, *cot_parts)
    entering = carry_states(here, seg_end, through, False)
    states = [entering]
    for c in range(per_seg - 1):
        states.append(span_decay[:, c, None, :] * states[-1] + updates[:, c])
    states_low = jnp.stack([s.astype(BF16) for s in states], axis=1).reshape(spans, HV, HK)
    inside = jnp.einsum("nts,nsv->ntv", wide_scores, v_s.astype(F32), precision=exact)
    raw = inside + ein("ntk,nvk->ntv", reach_low, states_low)
    mixed = raw.reshape(group, HV).astype(BF16).astype(F32)

    head_scale = lax.rsqrt(jnp.mean(mixed * mixed, axis=-1, keepdims=True) + EPS)
    normed_mix = mixed * head_scale * full_head_gain
    outgate_sig = jax.nn.sigmoid(outgate)
    gate_act = outgate * outgate_sig
    gated = (normed_mix * gate_act).astype(BF16)
    branch_parts = near_sums(here, *stream_parts(here, dot(gated, w_out).astype(BF16)))
    branch_out = far_sums(here, *branch_parts)
    resid, normed_mid = norm_forward(tokens, branch_out, full_ffn_gain[None], line)
    x_mid = gather_loose(here, normed_mid)
    gate_up = dot(x_mid, w_ffn)
    gate_pre, up_pre = gate_up[:, :quarter], gate_up[:, quarter:]
    gate_sig = jax.nn.sigmoid(gate_pre)
    silu_gate = gate_pre * gate_sig
    hidden = (silu_gate * up_pre).astype(BF16)

    down_part = dot_rows(hidden, cot).astype(BF16)
    down_term = scatter_line(here, down_part)
    hidden_grad = dot_cols(after(cot, down_part), w_dn)
    gate_grad = (hidden_grad * up_pre * (gate_sig * (1.0 + gate_pre * (1.0 - gate_sig)))).astype(
        BF16
    )
    up_grad = (hidden_grad * silu_gate).astype(BF16)
    gate_up_grad = jnp.concatenate([gate_grad, up_grad], axis=1)
    mid_parts = near_sums(here, *loose_parts(dot_cols(gate_up_grad, w_ffn).astype(BF16)))
    ffn_part = dot_rows(x_mid, gate_up_grad).astype(BF16)
    *mid_parts, ffn_part = phase(*mid_parts, ffn_part)
    mid_grad, down_term, ffn_part, hidden = phase(
        far_sums(here, *mid_parts), down_term, ffn_part, hidden
    )
    ffn_term = scatter_line(here, ffn_part)
    resid_grad, branch, ffn_gain_term = norm_backward(
        mid_grad, None, resid, cotangent, full_ffn_gain[None], line, False
    )
    near = near_halves(here, branch)
    *near, hidden = phase(*near, hidden)
    down_out = dot(hidden, w_dn).astype(BF16)
    *far, down_out = phase(*far_halves(here, *near), down_out)
    branch = in_stream(here, *near, *far)

    gated_grad = dot_cols(branch, w_out)
    outgate_grad = (
        gated_grad * normed_mix * outgate_sig * (1.0 + outgate * (1.0 - outgate_sig))
    ).astype(BF16)
    normed_grad = gated_grad * gate_act
    head_gain_term = jnp.sum(normed_grad * mixed * head_scale, axis=0)
    scaled_head = full_head_gain * normed_grad
    mixed_grad = (
        head_scale * scaled_head
        - mixed * head_scale**3 * jnp.mean(scaled_head * mixed, axis=-1, keepdims=True)
    ).astype(BF16)
    seg_reach = jnp.where(unfinished, expanded, 0.0).reshape(2, per_seg, SPAN, HK)
    seg_reach = (seg_reach * before[:, :, None, :]).astype(BF16)
    seg_reach = seg_reach.reshape(2, per_seg * SPAN, HK)
    start_grad = ein("jtv,jtk->jvk", mixed_grad.reshape(2, per_seg * SPAN, HV), seg_reach)
    leaving = carry_states(here, start_grad, through, True)
    down_parts = near_sums(here, *loose_parts(after(down_out, start_grad)))
    out_term = dot_rows(gated, branch).astype(BF16)
    out_term = out_term.reshape(line // 2, 2, 2 * rows_d, model).transpose(1, 0, 2, 3)
    out_part = out_term.reshape(HV, model)
    leaving, out_part, *down_parts = phase(leaving, out_part, *down_parts)
    layer_output = (resid + far_sums(here, *down_parts)).astype(BF16)
    out_term = scatter_line(here, after(out_part, ffn_term))

    mixer_grads, logit_grad = recurrence_backward(
        leaving,
        mixed_grad.reshape(spans, SPAN, HV),
        v_s,
        expanded_low,
        shrunk_low,
        ending_low,
        scores,
        states_low,
        running,
        logits.reshape(spans, SPAN, HK),
        span_decay,
        count,
        flags,
    )
    mixer_grads, layer_output = phase(mixer_grads, layer_output)
    grads = jnp.concatenate([mixer_grads, outgate_grad], axis=1)
    in_part = dot_cols(grads, w_mixer).astype(BF16)

    bias_term = jnp.sum(logit_grad.astype(F32), axis=0)
    up_rank_term = dot_rows(rank_low, logit_grad)
    rank_part = dot_cols(logit_grad, my_up_rank)
    other_side = here.over_side(rank_part[2 * tok :])
    rank_part = rank_part[: 2 * tok] + other_side
    rank_part = rank_part + here.over_seq(rank_part)
    rank_grad = lax.dynamic_slice_in_dim(rank_part, here.seq * tok, tok, 0).astype(BF16)
    down_rank_term = dot_rows(normed_in, rank_grad)
    rank_in_grad = dot_cols(rank_grad, full_down_rank)
    attn_gain_here = jnp.sum(in_part.astype(F32) * (wide_in * wide_scale), axis=0)
    attn_gain_term = jnp.sum(rank_in_grad * (inputs * scale_in), axis=0)

    zero_bias = jnp.zeros((HEADS * HK,), F32)
    zero_up = jnp.zeros((rank, HEADS * HK), F32)
    bias_all = lax.dynamic_update_slice_in_dim(zero_bias, bias_term, me * HK, 0)
    up_all = lax.dynamic_update_slice_in_dim(zero_up, up_rank_term, me * HK, 1)
    small_terms = jnp.concatenate(
        [
            attn_gain_term.reshape(devices, -1)
            + attn_gain_here.reshape(line, 2, 2, 2, rows_d)
            .transpose(2, 0, 3, 1, 4)
            .reshape(devices, -1),
            ffn_gain_term.reshape(devices, -1),
            head_gain_term.reshape(devices, -1),
            bias_all.reshape(devices, -1),
            up_all.reshape(rank, devices, cols_k).transpose(1, 0, 2).reshape(devices, -1),
            down_rank_term.reshape(devices, -1),
        ],
        axis=1,
    )
    small_part = scatter_small_plane(here, small_terms)
    in_parts = near_sums(here, *stream_parts(here, after(in_part, small_part)))
    small_cols = 128 * -(-small_size // (512 * rows_d))
    small_part = jnp.pad(
        small_part.reshape(2 * line, small_size),
        ((0, 0), (0, 4 * rows_d * small_cols - small_size)),
    ).reshape(-1, small_cols)
    wide_grads = jnp.pad(grads, ((0, 0), (0, small_cols)))
    mixer_part = dot_rows(x_in, after(wide_grads, in_part)).astype(BF16)
    mixer_part = lax.dynamic_update_slice(mixer_part, small_part.astype(BF16), (0, grads.shape[1]))
    mixer_part, ffn_term, out_term = phase(mixer_part, ffn_term, out_term)
    mixer_term = scatter_line(here, mixer_part)
    *in_parts, ffn_term = phase(*in_parts, ffn_term)
    in_grad = far_sums(here, *in_parts)
    ffn_back = send_quarters(here, ffn_term.reshape(4, rows_d, 2 * quarter))

    input_grad, _ = norm_backward(
        in_grad,
        rank_in_grad,
        tokens,
        resid_grad,
        full_attn_gain[None],
        line,
        True,
    )

    down_grad = down_term.astype(F32)
    out_grad = here.swap_top(out_term).astype(F32)
    input_grad, out_grad, *ffn_back = phase(input_grad, out_grad, *ffn_back)
    ffn_back = join_quarters(here, *ffn_back).astype(F32)

    def hidden_last(g):
        return (
            g.reshape(2, 2, rows_d, line, 2, rows_f)
            .transpose(2, 0, 3, 1, 4, 5)
            .reshape(rows_d, 4 * quarter)
        )

    gate_out = hidden_last(ffn_back[:, :, :quarter])
    up_out = hidden_last(ffn_back[:, :, quarter:])
    small_sum = mixer_term[:, 2 * HK + 2 * HV :].reshape(-1).astype(F32)
    mixer_term = after(mixer_term[:, : 2 * HK + 2 * HV], gate_out, up_out, out_grad, down_grad)
    mixer_back = send_quarters(here, mixer_term.reshape(4, rows_d, -1))
    mixer_back = join_quarters(here, *mixer_back).astype(F32)

    def heads_last(g):
        return g.transpose(1, 0, 2).reshape(rows_d, -1)

    query_out = heads_last(mixer_back[:, :, :HK])
    key_out = heads_last(mixer_back[:, :, HK : 2 * HK])
    value_out = heads_last(mixer_back[:, :, 2 * HK : 2 * HK + HV])
    outgate_out = heads_last(mixer_back[:, :, 2 * HK + HV :])
    small_sum = after(small_sum, query_out, key_out, value_out, outgate_out)
    pieces = []
    at = 0
    for size in (rows_d, rows_d, head_gain.shape[0], cols_k, rank * cols_k, rows_d * rank):
        pieces.append(small_sum[at : at + size])
        at += size
    return (
        layer_output,
        input_grad,
        pieces[0],
        query_out,
        key_out,
        value_out,
        pieces[5].reshape(rows_d, rank),
        pieces[4].reshape(rank, cols_k),
        pieces[3],
        outgate_out,
        pieces[2],
        out_grad,
        pieces[1],
        gate_out,
        up_out,
        down_grad,
    )


def solution(mesh):
    rows = P(BOTH, None)
    vector = P(BOTH)
    by_tokens = P(("fsdp", "seq"), None)
    by_cols = P(None, BOTH)
    in_specs = (
        by_tokens,
        vector,
        rows,
        rows,
        rows,
        rows,
        by_cols,
        vector,
        rows,
        vector,
        rows,
        vector,
        rows,
        rows,
        rows,
        P("fsdp"),
        by_tokens,
    )
    out_specs = (
        by_tokens,
        by_tokens,
        vector,
        rows,
        rows,
        rows,
        rows,
        by_cols,
        vector,
        rows,
        vector,
        rows,
        vector,
        rows,
        rows,
        rows,
    )
    return jax.shard_map(
        on_device, mesh=mesh, in_specs=in_specs, out_specs=out_specs, check_vma=False
    )
```

time: 1170 us -> 735 us (0.63)
  waiting for transfers between devices: 595 us -> 223 us
  other arithmetic: 111 us -> 67 us
  matrix products: 177 us -> 148 us
  local copies, waits for them, and re-layouts: 164 us -> 141 us
  Pallas kernels: 0 us -> 18.9 us
  starting transfers between devices: 100 us -> 113 us
    unnamed x12 -> x8, waiting for transfers between devices: 274 us -> 0.13 us
    reduce_scatter x4, waiting for transfers between devices: 81 us -> 2.3 us  [scatter_line(): lax.psum_scatter(rows, 'fsdp', scatter_dimension=0, tiled=True, axis_inde...]
    dot_general x14 -> x4, matrix products: 27 us -> 4.71 us  [ein(): return jnp.einsum(form, left, right, preferred_element_type=F32)]
    another operation x30 -> x17, other arithmetic: 25 us -> 4.18 us  [pair(): jnp.stack([jnp.where(first, own, other), jnp.where(first, other, own)])]
    ppermute x60 -> x63, waiting for transfers between devices: 240 us -> 220 us  [send(): return lax.ppermute(value, BOTH, pairs)]
    slice x21 -> x11, local copies, waits for them, and re-layouts: 25.3 us -> 6.37 us  [the longest x1 3.29 us: on_device(): w_out = out_lines[:, :, :rows_d].reshape(2, line // 2, 2 * rows_d, model)]
    pallas_call x0 -> x5, Pallas kernels: none -> 18.9 us  [the longest x1 12 us: recurrence_backward(): pl.pallas_call(kernel, grid=(segments, per_seg), in_specs=[pl.BlockSpec((...]
    reduce_sum x3 -> x1, other arithmetic: 14.4 us -> 0.98 us  [on_device(): jnp.mean(wide_in * wide_in, axis=-1, keepdims=True) + EPS]
  transfers between devices with their start and end apart: 70 -> 71, of which waited for: 35 -> 37; matrix products, arithmetic and copies ran while one was open for 25% -> 44% of each run, Pallas kernels for 0% -> 3%
where the time goes in v2:
time: 735 us; the launch traced here: 727 us
  waiting for transfers between devices  223 us (30%)
  matrix products  148 us (20%)
  local copies, waits for them, and re-layouts  141 us (19%)
  starting transfers between devices  113 us (15%)
  other arithmetic  67 us (9%)
  Pallas kernels  18.9 us (3%)
  between operations  16.8 us (2%)
    ppermute x63, waiting for transfers between devices, send(): return lax.ppermute(value, BOTH, pairs)  220 us
    ppermute x63, starting transfers between devices, send(): return lax.ppermute(value, BOTH, pairs)  112 us
    dot_general x6, matrix products, dot_cols(): lax.dot_general(left, right, (((1,), (1,)), ((), ())), preferred_element_...  53.2 us
    dot_general x6, matrix products, dot(): return jnp.dot(left, right, preferred_element_type=F32)  45.6 us
    dot_general x6, matrix products, dot_rows(): lax.dot_general(left, right, (((0,), (0,)), ((), ())), preferred_element_...  40.4 us
    unnamed x216, local copies, waits for them, and re-layouts  35.5 us
  transfers between devices with their start and end apart: 71, of which 37 were waited for; matrix products, arithmetic and copies ran while one was open for 44% of the time, Pallas kernels for 3%

profile of v2, /device:TPU:0, one launch (start us, length us, event | category | flops | bytes accessed | tf_op | source)
XLA Modules:
  0.0 726.9 jit_solution(7314964441148148690)
XLA Ops:
  20.5 14.5 %collective-permute-start = (bf16[64,1536]{1,0:T(8,128)(2,1)S(1)}, bf16[64,1536]{1,0:T(8,128)(2,1)S(1)}, u32[]{:S(2)}, u32[]{:S(2)}) collective-permute-start(bf16[64,1536]{1,0:T(8,128)(2,1)S(1)} %bitcast.712), channel_id=1, source_target_pairs={{0,2},{1,3},{2,0},{3,1},{4,6},{5,7},{6,4},{7,5},{8,10},{9,11},{10,... | collective-permute-start | bytes 589832 | tf_op jit(solution)/shard_map/ppermute | solution.py:59
  51.6 4.7 reshape.1559
  70.7 4.9 reshape.1562
  84.8 17.0 %collective-permute-done.10 = bf16[2,128,2048]{2,1,0:T(8,128)(2,1)} collective-permute-done((bf16[2,128,2048]{2,1,0:T(8,128)(2,1)}, bf16[2,128,2048]{2,1,0:T(8,128)(2,1)}, u32[]{:S(2)}, u32[]{:S(2)}) %collective-permute-start.10) | collective-permute-done | bytes 1048608 | tf_op jit(solution)/shard_map/ppermute | solution.py:59
  135.0 12.7 %fusion.120 = (bf16[1024,1536]{1,0:T(8,128)(2,1)S(1)}, f32[1024,1536]{1,0:T(8,128)}) fusion(bf16[1024,2048]{1,0:T(8,128)(2,1)} %multiply_convert_fusion.1, bf16[2048,1536]{1,0:T(8,128)(2,1)} %all-gather.7.cloned.1.call-done), kind=kOutput, calls=%fused_computation.476 | convolution fusion | flops 6444023808 | bytes 19922944 | tf_op jit(solution)/shard_map/dot_general | solution.py:20
  153.0 16.0 %collective-permute-done.16 = bf16[256,2048]{1,0:T(8,128)(2,1)} collective-permute-done((bf16[256,2048]{1,0:T(8,128)(2,1)S(1)}, bf16[256,2048]{1,0:T(8,128)(2,1)}, u32[]{:S(2)}, u32[]{:S(2)}) %collective-permute-start.16) | collective-permute-done | bytes 1048608 | tf_op jit(solution)/shard_map/ppermute | solution.py:59
  171.6 9.1 %collective-permute-start.21 = (bf16[272,256]{1,0:T(8,128)(2,1)S(1)}, bf16[272,256]{1,0:T(8,128)(2,1)S(1)}, u32[]{:S(2)}, u32[]{:S(2)}) collective-permute-start(bf16[272,256]{1,0:T(8,128)(2,1)S(1)} %fusion.87), channel_id=1, source_target_pairs={{0,12},{1,13},{2,14},{3,15},{16,28},{17,29},{18,30},{19,31}} | collective-permute-start | bytes 417800 | tf_op jit(solution)/shard_map/ppermute | solution.py:59
  186.4 7.3 %collective-permute-done.19 = bf16[272,256]{1,0:T(8,128)(2,1)S(1)} collective-permute-done((bf16[272,256]{1,0:T(8,128)(2,1)S(1)}, bf16[272,256]{1,0:T(8,128)(2,1)S(1)}, u32[]{:S(2)}, u32[]{:S(2)}) %collective-permute-start.19) | collective-permute-done | bytes 139296 | tf_op jit(solution)/shard_map/ppermute | solution.py:59
  193.7 5.8 collective-permute-done.20
  219.0 21.7 %collective-permute-done.23 = bf16[2,128,2048]{2,1,0:T(8,128)(2,1)} collective-permute-done((bf16[2,128,2048]{2,1,0:T(8,128)(2,1)}, bf16[2,128,2048]{2,1,0:T(8,128)(2,1)}, u32[]{:S(2)}, u32[]{:S(2)}) %collective-permute-start.23) | collective-permute-done | bytes 1048608 | tf_op jit(solution)/shard_map/ppermute | solution.py:59
  246.3 9.6 %collective-permute-done.24 = bf16[128,2048]{1,0:T(8,128)(2,1)S(1)} collective-permute-done((bf16[128,2048]{1,0:T(8,128)(2,1)S(1)}, bf16[128,2048]{1,0:T(8,128)(2,1)S(1)}, u32[]{:S(2)}, u32[]{:S(2)}) %collective-permute-start.24) | collective-permute-done | bytes 524320 | tf_op jit(solution)/shard_map/ppermute | solution.py:59
  262.9 8.5 %collective-permute-done.27 = bf16[128,2048]{1,0:T(8,128)(2,1)S(1)} collective-permute-done((bf16[128,2048]{1,0:T(8,128)(2,1)S(1)}, bf16[128,2048]{1,0:T(8,128)(2,1)S(1)}, u32[]{:S(2)}, u32[]{:S(2)}) %collective-permute-start.27) | collective-permute-done | bytes 524320 | tf_op jit(solution)/shard_map/ppermute | solution.py:59
  280.0 15.4 %collective-permute-done.28 = bf16[2,128,2048]{2,1,0:T(8,128)(2,1)S(1)} collective-permute-done((bf16[2,128,2048]{2,1,0:T(8,128)(2,1)S(1)}, bf16[2,128,2048]{2,1,0:T(8,128)(2,1)S(1)}, u32[]{:S(2)}, u32[]{:S(2)}) %collective-permute-start.28) | collective-permute-done | bytes 1048608 | tf_op jit(solution)/shard_map/ppermute | solution.py:59
  296.4 18.9 %fusion.57 = f32[1024,2816]{1,0:T(8,128)S(1)} fusion(bf16[2048,2816]{1,0:T(8,128)(2,1)} %all-gather.9.cloned.1.call-done, bf16[256,2048]{1,0:T(8,128)(2,1)} %bitcast.115, bf16[256,2048]{1,0:T(8,128)(2,1)} %bitcast.696, bf16[256,2048]{1,0:T(8,128)(2,1)} %bitcast.740, bf16[256,2048]{1,0:T(8,128)(2,1)} %bitcast.694), kind=kOutput, calls=%fused_computation.211 | convolution fusion | flops 11827937280 | bytes 27262976 | tf_op jit(solution)/shard_map/dot_general | solution.py:20
  322.2 8.1 %convolution_convert_fusion.2 = bf16[1408,2048]{1,0:T(8,128)(2,1)} fusion(bf16[1024,1408]{1,0:T(8,128)(2,1)S(1)} %multiply_convert_fusion.4, bf16[1024,2048]{1,0:T(8,128)(2,1)S(1)} %copy-done.69), kind=kOutput, calls=%fused_computation.7 | convolution fusion | flops 5908463616 | bytes 12845056 | tf_op jit(solution)/shard_map/dot_general | solution.py:24
  330.8 15.4 %multiply_convert_fusion.3 = (bf16[1024,1408]{1,0:T(8,128)(2,1)S(1)}, bf16[1024,1408]{1,0:T(8,128)(2,1)}) fusion(f32[1024,2816]{1,0:T(8,128)} %copy-done.31, bf16[1024,2048]{1,0:T(8,128)(2,1)} %copy-done.68, bf16[1408,2048]{1,0:T(8,128)(2,1)} %all-gather.11.cloned.1.call-done), kind=kOutput, calls=%fused_computation.10 | convolution fusion | flops 5924323328 | bytes 27262976 | tf_op jit(solution)/shard_map/dot_general | solution.py:28
  346.2 16.9 %convolution_convert_fusion.3 = bf16[1024,2048]{1,0:T(8,128)(2,1)S(1)} fusion(bf16[2048,2816]{1,0:T(8,128)(2,1)} %all-gather.9.cloned.1.call-done, bf16[1024,1408]{1,0:T(8,128)(2,1)} %get-tuple-element.245, bf16[1024,1408]{1,0:T(8,128)(2,1)S(1)} %get-tuple-element.244), kind=kOutput, calls=%fused_computation.17 | convolution fusion | flops 11824791552 | bytes 21495808 | tf_op jit(solution)/shard_map/dot_general | solution.py:28
  368.9 18.1 %convolution_convert_fusion = bf16[2048,2816]{1,0:T(8,128)(2,1)} fusion(bf16[1024,1408]{1,0:T(8,128)(2,1)} %get-tuple-element.245, bf16[1024,1408]{1,0:T(8,128)(2,1)} %copy-done.94, bf16[256,2048]{1,0:T(8,128)(2,1)} %bitcast.115, bf16[256,2048]{1,0:T(8,128)(2,1)S(1)} %bitcast.697, bf16[256,2048]{1,0:T(8,128)(2,1)S(1)} %bitcast.741, ...), kind=kOutput, calls=%fused_computation | convolution fusion | flops 11845238784 | bytes 21495808 | tf_op jit(solution)/shard_map/dot_general | solution.py:24
  396.9 6.9 collective-permute-done.33
  430.0 8.7 %convolution_convert_fusion.5 = bf16[1024,2048]{1,0:T(8,128)(2,1)S(1)} fusion(bf16[1024,1408]{1,0:T(8,128)(2,1)S(1)} %copy-done.48, bf16[1408,2048]{1,0:T(8,128)(2,1)} %all-gather.11.cloned.1.call-done), kind=kOutput, calls=%fused_computation.19 | convolution fusion | flops 5907677184 | bytes 12845056 | tf_op jit(solution)/shard_map/dot_general | solution.py:20
  438.8 9.9 %collective-permute-done.37 = bf16[2,128,2048]{2,1,0:T(8,128)(2,1)S(1)} collective-permute-done((bf16[2,128,2048]{2,1,0:T(8,128)(2,1)S(1)}, bf16[2,128,2048]{2,1,0:T(8,128)(2,1)S(1)}, u32[]{:S(2)}, u32[]{:S(2)}) %collective-permute-start.37) | collective-permute-done | bytes 1048608 | tf_op jit(solution)/shard_map/ppermute | solution.py:59
  451.9 5.9 fusion.20
  472.2 13.7 %collective-permute-done.40 = bf16[272,256]{1,0:T(8,128)(2,1)S(1)} collective-permute-done((bf16[272,256]{1,0:T(8,128)(2,1)S(1)}, bf16[272,256]{1,0:T(8,128)(2,1)S(1)}, u32[]{:S(2)}, u32[]{:S(2)}) %collective-permute-start.40) | collective-permute-done | bytes 139296 | tf_op jit(solution)/shard_map/ppermute | solution.py:59
  486.0 11.6 %collective-permute-done.41 = bf16[272,256]{1,0:T(8,128)(2,1)S(1)} collective-permute-done((bf16[272,256]{1,0:T(8,128)(2,1)S(1)}, bf16[272,256]{1,0:T(8,128)(2,1)S(1)}, u32[]{:S(2)}, u32[]{:S(2)}) %collective-permute-start.41) | collective-permute-done | bytes 139296 | tf_op jit(solution)/shard_map/ppermute | solution.py:59
  506.8 19.1 %collective-permute-done.45 = bf16[2,128,2048]{2,1,0:T(8,128)(2,1)} collective-permute-done((bf16[2,128,2048]{2,1,0:T(8,128)(2,1)}, bf16[2,128,2048]{2,1,0:T(8,128)(2,1)}, u32[]{:S(2)}, u32[]{:S(2)}) %collective-permute-start.45) | collective-permute-done | bytes 1048608 | tf_op jit(solution)/shard_map/ppermute | solution.py:59
  537.5 12.0 %shard_map.291 = (bf16[1024,1024]{1,0:T(8,128)(2,1)S(1)}, bf16[1024,256]{1,0:T(8,128)(2,1)S(1)}) custom-call(f32[2,512,256]{2,1,0:T(8,128)S(1)} %copy-done.15, bf16[16,64,512]{2,1,0:T(8,128)(2,1)S(1)} %bitcast.641, bf16[16,64,512]{2,1,0:T(8,128)(2,1)S(1)} %bitcast.639, bf16[16,64,256]{2,1,0:T(8,128)(2,1)S(1)} %copy-done.22, ...), custom_call_target="tpu_custom_call" | custom-call | flops 1342177280 | bytes 10121216 | tf_op jit(solution)/shard_map/pallas_call | solution.py:445
  573.3 12.2 %multiply_reduce_fusion = (f32[2048]{0:T(1024)S(1)}, bf16[1024,2048]{1,0:T(8,128)(2,1)}) fusion(f32[1024]{0:T(1024)S(1)} %bitcast.719, bf16[1,2,128,2048]{3,2,1,0:T(8,128)(2,1)} %copy-done.30, bf16[1,2,128,2048]{3,2,1,0:T(8,128)(2,1)} %copy-done.29, bf16[1,2,128,2048]{3,2,1,0:T(8,128)(2,1)} %copy-done.28, bf16[1,2,128,2048]{3,2,1,0:T(8,128)(2,1)} %copy-done.27, ...), kind=kOutput, calls=%fused_computation.2 | convolution fusion | flops 6467614720 | bytes 17838080 | tf_op jit(solution)/shard_map/dot_general | solution.py:28
  592.5 10.1 %convolution_convert_fusion.1 = bf16[2048,1664]{1,0:T(8,128)(2,1)} fusion(bf16[1024,2048]{1,0:T(8,128)(2,1)S(1)} %copy-done.42, bf16[1024,1664]{1,0:T(8,128)(2,1)S(1)} %pad.25), kind=kOutput, calls=%fused_computation.6 | convolution fusion | flops 6982729728 | bytes 14417920 | tf_op jit(solution)/shard_map/dot_general | solution.py:24
  617.1 17.1 %collective-permute-done.52 = bf16[2,128,2048]{2,1,0:T(8,128)(2,1)} collective-permute-done((bf16[2,128,2048]{2,1,0:T(8,128)(2,1)}, bf16[2,128,2048]{2,1,0:T(8,128)(2,1)}, u32[]{:S(2)}, u32[]{:S(2)}) %collective-permute-start.52) | collective-permute-done | bytes 1048608 | tf_op jit(solution)/shard_map/ppermute | solution.py:59
  645.6 24.0 %collective-permute-start.59 = (bf16[64,2816]{1,0:T(8,128)(2,1)S(1)}, bf16[64,2816]{1,0:T(8,128)(2,1)S(1)}, u32[]{:S(2)}, u32[]{:S(2)}) collective-permute-start(bf16[64,2816]{1,0:T(8,128)(2,1)S(1)} %get-tuple-element.294), channel_id=1, source_target_pairs={{0,18},{1,19},{2,16},{3,17},{4,22},{5,23},{6,20},{7,21},{8,26},{9,... | collective-permute-start | bytes 1081352 | tf_op jit(solution)/shard_map/ppermute | solution.py:59
  678.3 4.7 reshape.1596
  689.9 4.7 reshape.1598
  (644 shorter events, 324.8 us)
Async XLA Ops:
  7.2 57.7 %all-gather.5.cloned.1.call-start = ((), (), s32[]{:S(2)}) async-start(), calls=%async_computation.4 | async-start | bytes 2654208 | tf_op jit(solution)/shard_map/all_gather | solution.py:174
  14.0 120.9 %all-gather.7.cloned.1.call-start = ((), (), s32[]{:S(2)}) async-start(), calls=%async_computation.5 | async-start | bytes 7077888 | tf_op jit(solution)/shard_map/all_gather | solution.py:174
  46.1 250.3 %all-gather.9.cloned.1.call-start = ((), (), s32[]{:S(2)}) async-start(), calls=%async_computation.6 | async-start | bytes 12976128 | tf_op jit(solution)/shard_map/all_gather | solution.py:174
  78.8 23.0 %collective-permute-start.10 = (bf16[2,128,2048]{2,1,0:T(8,128)(2,1)}, bf16[2,128,2048]{2,1,0:T(8,128)(2,1)}, u32[]{:S(2)}, u32[]{:S(2)}) collective-permute-start(bf16[2,128,2048]{2,1,0:T(8,128)(2,1)} %pad_maximum_fusion.16), channel_id=1, source_target_pairs={{0,2},{1,3},{2,0},{3,1},{4,6},{5,7},{6,4},{7,5},{8,10},{9,11},{10,... | collective-permute-start | bytes 3145736 | tf_op jit(solution)/shard_map/ppermute | solution.py:59
  79.9 22.5 %collective-permute-start.9 = (bf16[2,128,2048]{2,1,0:T(8,128)(2,1)}, bf16[2,128,2048]{2,1,0:T(8,128)(2,1)}, u32[]{:S(2)}, u32[]{:S(2)}) collective-permute-start(bf16[2,128,2048]{2,1,0:T(8,128)(2,1)} %pad_maximum_fusion.15), channel_id=1, source_target_pairs={{0,16},{1,17},{2,18},{3,19},{4,20},{5,21},{6,22},{7,23},{8,24},{9,... | collective-permute-start | bytes 3145736 | tf_op jit(solution)/shard_map/ppermute | solution.py:59
  117.9 212.9 %all-gather.11.cloned.1.call-start = ((), (), s32[]{:S(2)}) async-start(), calls=%async_computation.7 | async-start | bytes 6488064 | tf_op jit(solution)/shard_map/all_gather | solution.py:174
  126.8 26.2 %collective-permute-start.15 = (bf16[256,2048]{1,0:T(8,128)(2,1)S(1)}, bf16[256,2048]{1,0:T(8,128)(2,1)}, u32[]{:S(2)}, u32[]{:S(2)}) collective-permute-start(bf16[256,2048]{1,0:T(8,128)(2,1)S(1)} %copy-done.14), channel_id=1, source_target_pairs={{0,2},{1,3},{2,0},{3,1},{4,6},{5,7},{6,4},{7,5},{8,10},{9,11},{10,... | collective-permute-start | bytes 3145736 | tf_op jit(solution)/shard_map/ppermute | solution.py:59
  127.8 41.2 %collective-permute-start.16 = (bf16[256,2048]{1,0:T(8,128)(2,1)S(1)}, bf16[256,2048]{1,0:T(8,128)(2,1)}, u32[]{:S(2)}, u32[]{:S(2)}) collective-permute-start(bf16[256,2048]{1,0:T(8,128)(2,1)S(1)} %copy-done.14), channel_id=1, source_target_pairs={{0,16},{1,17},{2,18},{3,19},{4,20},{5,21},{6,22},{7,23},{8,24},{9,... | collective-permute-start | bytes 3145736 | tf_op jit(solution)/shard_map/ppermute | solution.py:59
  129.2 39.9 %collective-permute-start.17 = (bf16[256,2048]{1,0:T(8,128)(2,1)S(1)}, bf16[256,2048]{1,0:T(8,128)(2,1)}, u32[]{:S(2)}, u32[]{:S(2)}) collective-permute-start(bf16[256,2048]{1,0:T(8,128)(2,1)S(1)} %copy-done.14), channel_id=1, source_target_pairs={{0,18},{1,19},{2,16},{3,17},{4,22},{5,23},{6,20},{7,21},{8,26},{9,... | collective-permute-start | bytes 3145736 | tf_op jit(solution)/shard_map/ppermute | solution.py:59
  171.6 27.9 %collective-permute-start.21 = (bf16[272,256]{1,0:T(8,128)(2,1)S(1)}, bf16[272,256]{1,0:T(8,128)(2,1)S(1)}, u32[]{:S(2)}, u32[]{:S(2)}) collective-permute-start(bf16[272,256]{1,0:T(8,128)(2,1)S(1)} %fusion.87), channel_id=1, source_target_pairs={{0,12},{1,13},{2,14},{3,15},{16,28},{17,29},{18,30},{19,31}} | collective-permute-start | bytes 417800 | tf_op jit(solution)/shard_map/ppermute | solution.py:59
  215.2 25.5 %collective-permute-start.23 = (bf16[2,128,2048]{2,1,0:T(8,128)(2,1)}, bf16[2,128,2048]{2,1,0:T(8,128)(2,1)}, u32[]{:S(2)}, u32[]{:S(2)}) collective-permute-start(bf16[2,128,2048]{2,1,0:T(8,128)(2,1)} %fusion.41), channel_id=1, source_target_pairs={{0,2},{1,3},{2,0},{3,1},{4,6},{5,7},{6,4},{7,5},{8,10},{9,11},{10,... | collective-permute-start | bytes 3145736 | tf_op jit(solution)/shard_map/ppermute | solution.py:59
  217.0 190.7 %reduce-scatter.5.cloned.1.call-start = ((), (), s32[]{:S(2)}) async-start(), calls=%async_computation.8 | async-start | bytes 6488064 | tf_op jit(solution)/shard_map/reduce_scatter | solution.py:178
  217.3 27.0 %collective-permute-start.25 = (bf16[2,128,2048]{2,1,0:T(8,128)(2,1)}, bf16[2,128,2048]{2,1,0:T(8,128)(2,1)S(1)}, u32[]{:S(2)}, u32[]{:S(2)}) collective-permute-start(bf16[2,128,2048]{2,1,0:T(8,128)(2,1)} %get-tuple-element.278), channel_id=1, source_target_pairs={{0,16},{1,17},{2,18},{3,19},{4,20},{5,21},{6,22},{7,23},{8,24},{9,... | collective-permute-start | bytes 3145736 | tf_op jit(solution)/shard_map/ppermute | solution.py:59
  271.5 23.9 %collective-permute-start.28 = (bf16[2,128,2048]{2,1,0:T(8,128)(2,1)S(1)}, bf16[2,128,2048]{2,1,0:T(8,128)(2,1)S(1)}, u32[]{:S(2)}, u32[]{:S(2)}) collective-permute-start(bf16[2,128,2048]{2,1,0:T(8,128)(2,1)S(1)} %pad_maximum_fusion.21), channel_id=1, source_target_pairs={{0,16},{1,17},{2,18},{3,19},{4,20},{5,21},{6,22},{7,23},{8,24},{9,... | collective-permute-start | bytes 3145736 | tf_op jit(solution)/shard_map/ppermute | solution.py:59
  274.5 21.9 %collective-permute-start.30 = (bf16[2,128,2048]{2,1,0:T(8,128)(2,1)S(1)}, bf16[2,128,2048]{2,1,0:T(8,128)(2,1)}, u32[]{:S(2)}, u32[]{:S(2)}) collective-permute-start(bf16[2,128,2048]{2,1,0:T(8,128)(2,1)S(1)} %pad_maximum_fusion.22), channel_id=1, source_target_pairs={{0,2},{1,3},{2,0},{3,1},{4,6},{5,7},{6,4},{7,5},{8,10},{9,11},{10,... | collective-permute-start | bytes 3145736 | tf_op jit(solution)/shard_map/ppermute | solution.py:59
  330.4 242.9 %reduce-scatter.7.cloned.1.call-start = ((), (), s32[]{:S(2)}) async-start(), calls=%async_computation.9 | async-start | bytes 12976128 | tf_op jit(solution)/shard_map/reduce_scatter | solution.py:178
  365.1 23.3 %collective-permute-start.31 = (bf16[2,128,2048]{2,1,0:T(8,128)(2,1)}, bf16[2,128,2048]{2,1,0:T(8,128)(2,1)}, u32[]{:S(2)}, u32[]{:S(2)}) collective-permute-start(bf16[2,128,2048]{2,1,0:T(8,128)(2,1)} %get-tuple-element.275), channel_id=1, source_target_pairs={{0,2},{1,3},{2,0},{3,1},{4,6},{5,7},{6,4},{7,5},{8,10},{9,11},{10,... | collective-permute-start | bytes 3145736 | tf_op jit(solution)/shard_map/ppermute | solution.py:59
  368.0 23.1 %collective-permute-start.32 = (bf16[2,128,2048]{2,1,0:T(8,128)(2,1)}, bf16[2,128,2048]{2,1,0:T(8,128)(2,1)}, u32[]{:S(2)}, u32[]{:S(2)}) collective-permute-start(bf16[2,128,2048]{2,1,0:T(8,128)(2,1)} %get-tuple-element.273), channel_id=1, source_target_pairs={{0,16},{1,17},{2,18},{3,19},{4,20},{5,21},{6,22},{7,23},{8,24},{9,... | collective-permute-start | bytes 3145736 | tf_op jit(solution)/shard_map/ppermute | solution.py:59
  407.7 198.5 %reduce-scatter.9.cloned.1.call-start = ((), (), s32[]{:S(2)}) async-start(), calls=%async_computation.10 | async-start | bytes 2359296 | tf_op jit(solution)/shard_map/reduce_scatter | solution.py:178
  465.6 32.0 %collective-permute-start.42 = (bf16[272,256]{1,0:T(8,128)(2,1)S(1)}, bf16[272,256]{1,0:T(8,128)(2,1)S(1)}, u32[]{:S(2)}, u32[]{:S(2)}) collective-permute-start(bf16[272,256]{1,0:T(8,128)(2,1)S(1)} %fusion.88), channel_id=1, source_target_pairs={{12,0},{13,1},{14,2},{15,3},{28,16},{29,17},{30,18},{31,19}} | collective-permute-start | bytes 417800 | tf_op jit(solution)/shard_map/ppermute | solution.py:59
  468.2 29.4 %collective-permute-start.41 = (bf16[272,256]{1,0:T(8,128)(2,1)S(1)}, bf16[272,256]{1,0:T(8,128)(2,1)S(1)}, u32[]{:S(2)}, u32[]{:S(2)}) collective-permute-start(bf16[272,256]{1,0:T(8,128)(2,1)S(1)} %fusion.88), channel_id=1, source_target_pairs={{8,0},{9,1},{10,2},{11,3},{12,4},{13,5},{14,6},{15,7},{24,16},{25,... | collective-permute-start | bytes 417800 | tf_op jit(solution)/shard_map/ppermute | solution.py:59
  471.5 35.3 %collective-permute-start.44 = (bf16[2,128,2048]{2,1,0:T(8,128)(2,1)}, bf16[2,128,2048]{2,1,0:T(8,128)(2,1)}, u32[]{:S(2)}, u32[]{:S(2)}) collective-permute-start(bf16[2,128,2048]{2,1,0:T(8,128)(2,1)} %get-tuple-element.267), channel_id=1, source_target_pairs={{0,2},{1,3},{2,0},{3,1},{4,6},{5,7},{6,4},{7,5},{8,10},{9,11},{10,... | collective-permute-start | bytes 3145736 | tf_op jit(solution)/shard_map/ppermute | solution.py:59
  500.0 25.9 %collective-permute-start.45 = (bf16[2,128,2048]{2,1,0:T(8,128)(2,1)}, bf16[2,128,2048]{2,1,0:T(8,128)(2,1)}, u32[]{:S(2)}, u32[]{:S(2)}) collective-permute-start(bf16[2,128,2048]{2,1,0:T(8,128)(2,1)} %get-tuple-element.265), channel_id=1, source_target_pairs={{0,16},{1,17},{2,18},{3,19},{4,20},{5,21},{6,22},{7,23},{8,24},{9,... | collective-permute-start | bytes 3145736 | tf_op jit(solution)/shard_map/ppermute | solution.py:59
  528.8 38.3 %collective-permute-start.46 = (bf16[128,2048]{1,0:T(8,128)(2,1)}, bf16[128,2048]{1,0:T(8,128)(2,1)}, u32[]{:S(2)}, u32[]{:S(2)}) collective-permute-start(bf16[128,2048]{1,0:T(8,128)(2,1)} %fusion.67), channel_id=1, source_target_pairs={{0,16},{1,17},{2,18},{3,19},{4,20},{5,21},{6,22},{7,23},{8,24},{9,... | collective-permute-start | bytes 1572872 | tf_op jit(solution)/shard_map/ppermute | solution.py:59
  573.2 128.5 %reduce-scatter.11.cloned.1.call-start = ((), (), s32[]{:S(2)}) async-start(), calls=%async_computation.11 | async-start | bytes 7667712 | tf_op jit(solution)/shard_map/reduce_scatter | solution.py:178
  611.7 22.5 %collective-permute-start.52 = (bf16[2,128,2048]{2,1,0:T(8,128)(2,1)}, bf16[2,128,2048]{2,1,0:T(8,128)(2,1)}, u32[]{:S(2)}, u32[]{:S(2)}) collective-permute-start(bf16[2,128,2048]{2,1,0:T(8,128)(2,1)} %get-tuple-element.261), channel_id=1, source_target_pairs={{0,2},{1,3},{2,0},{3,1},{4,6},{5,7},{6,4},{7,5},{8,10},{9,11},{10,... | collective-permute-start | bytes 3145736 | tf_op jit(solution)/shard_map/ppermute | solution.py:59
  613.2 22.1 %collective-permute-start.53 = (bf16[2,128,2048]{2,1,0:T(8,128)(2,1)}, bf16[2,128,2048]{2,1,0:T(8,128)(2,1)}, u32[]{:S(2)}, u32[]{:S(2)}) collective-permute-start(bf16[2,128,2048]{2,1,0:T(8,128)(2,1)} %get-tuple-element.257), channel_id=1, source_target_pairs={{0,16},{1,17},{2,18},{3,19},{4,20},{5,21},{6,22},{7,23},{8,24},{9,... | collective-permute-start | bytes 3145736 | tf_op jit(solution)/shard_map/ppermute | solution.py:59
  637.0 33.3 %collective-permute-start.54 = (bf16[128,2048]{1,0:T(8,128)(2,1)S(1)}, bf16[128,2048]{1,0:T(8,128)(2,1)S(1)}, u32[]{:S(2)}, u32[]{:S(2)}) collective-permute-start(bf16[128,2048]{1,0:T(8,128)(2,1)S(1)} %fusion.69), channel_id=1, source_target_pairs={{0,16},{1,17},{2,18},{3,19},{4,20},{5,21},{6,22},{7,23},{8,24},{9,... | collective-permute-start | bytes 1572872 | tf_op jit(solution)/shard_map/ppermute | solution.py:59
  640.1 30.4 %collective-permute-start.55 = (bf16[128,2048]{1,0:T(8,128)(2,1)S(1)}, bf16[128,2048]{1,0:T(8,128)(2,1)S(1)}, u32[]{:S(2)}, u32[]{:S(2)}) collective-permute-start(bf16[128,2048]{1,0:T(8,128)(2,1)S(1)} %fusion.70), channel_id=1, source_target_pairs={{0,2},{1,3},{2,0},{3,1},{4,6},{5,7},{6,4},{7,5},{8,10},{9,11},{10,... | collective-permute-start | bytes 1572872 | tf_op jit(solution)/shard_map/ppermute | solution.py:59
  641.9 33.9 %collective-permute-start.57 = (bf16[64,2816]{1,0:T(8,128)(2,1)S(1)}, bf16[64,2816]{1,0:T(8,128)(2,1)S(1)}, u32[]{:S(2)}, u32[]{:S(2)}) collective-permute-start(bf16[64,2816]{1,0:T(8,128)(2,1)S(1)} %get-tuple-element.296), channel_id=1, source_target_pairs={{0,2},{1,3},{2,0},{3,1},{4,6},{5,7},{6,4},{7,5},{8,10},{9,11},{10,... | collective-permute-start | bytes 1081352 | tf_op jit(solution)/shard_map/ppermute | solution.py:59
  644.8 31.0 %collective-permute-start.58 = (bf16[64,2816]{1,0:T(8,128)(2,1)S(1)}, bf16[64,2816]{1,0:T(8,128)(2,1)S(1)}, u32[]{:S(2)}, u32[]{:S(2)}) collective-permute-start(bf16[64,2816]{1,0:T(8,128)(2,1)S(1)} %get-tuple-element.295), channel_id=1, source_target_pairs={{0,16},{1,17},{2,18},{3,19},{4,20},{5,21},{6,22},{7,23},{8,24},{9,... | collective-permute-start | bytes 1081352 | tf_op jit(solution)/shard_map/ppermute | solution.py:59
  645.6 30.2 %collective-permute-start.59 = (bf16[64,2816]{1,0:T(8,128)(2,1)S(1)}, bf16[64,2816]{1,0:T(8,128)(2,1)S(1)}, u32[]{:S(2)}, u32[]{:S(2)}) collective-permute-start(bf16[64,2816]{1,0:T(8,128)(2,1)S(1)} %get-tuple-element.294), channel_id=1, source_target_pairs={{0,18},{1,19},{2,16},{3,17},{4,22},{5,23},{6,20},{7,21},{8,26},{9,... | collective-permute-start | bytes 1081352 | tf_op jit(solution)/shard_map/ppermute | solution.py:59
  (134 other events, 1295.7 us)
Sparse Core Ops, SparseCore 0:
  14.2 44.7 all-gather.4
  61.2 63.8 all-gather.6
  127.3 110.1 all-gather.8
  239.0 67.0 all-gather.10
  330.5 70.5 reduce-scatter.4
  407.8 134.5 reduce-scatter.6
  573.4 32.7 reduce-scatter.8
  608.5 78.9 reduce-scatter.10

commit v3 on v2

--- a/solution.py
+++ b/solution.py
@@ -456,7 +456,7 @@
             jax.ShapeDtypeStruct((spans * length, width), BF16),
         ],
         scratch_shapes=[pltpu.VMEM((value_width, width), F32)],
-        compiler_params=pltpu.CompilerParams(vmem_limit_bytes=32 * 2**20),
+        compiler_params=pltpu.CompilerParams(vmem_limit_bytes=56 * 2**20),
         cost_estimate=pl.CostEstimate(
             flops=10 * spans * length * width * value_width,
             bytes_accessed=moved,
@@ -675,7 +675,14 @@
     )
     up_grad = (hidden_grad * silu_gate).astype(BF16)
     gate_up_grad = jnp.concatenate([gate_grad, up_grad], axis=1)
-    mid_parts = near_sums(here, *loose_parts(dot_cols(gate_up_grad, w_ffn).astype(BF16)))
+    rows_by_step = gate_up_grad.reshape(2, 2, 2, tok // 2, 2 * quarter)
+
+    def mid_of(rows):
+        return dot_cols(rows.reshape(2 * tok, -1), w_ffn).astype(BF16).reshape(2, 2, -1, model)
+
+    to_send = mid_of(rows_by_step[:, :, 1])
+    to_keep = mid_of(after(rows_by_step[:, :, 0], to_send))
+    mid_parts = (to_keep[0], here.over_side(to_send[0]), to_keep[1], here.over_seq(to_send[1]))
     ffn_part = dot_rows(x_mid, gate_up_grad).astype(BF16)
     *mid_parts, ffn_part = phase(*mid_parts, ffn_part)
     mid_grad, down_term, ffn_part, hidden = phase(
@@ -707,12 +714,11 @@
     seg_reach = seg_reach.reshape(2, per_seg * SPAN, HK)
     start_grad = ein("jtv,jtk->jvk", mixed_grad.reshape(2, per_seg * SPAN, HV), seg_reach)
     leaving = carry_states(here, start_grad, through, True)
-    down_parts = near_sums(here, *loose_parts(after(down_out, start_grad)))
     out_term = dot_rows(gated, branch).astype(BF16)
     out_term = out_term.reshape(line // 2, 2, 2 * rows_d, model).transpose(1, 0, 2, 3)
     out_part = out_term.reshape(HV, model)
-    leaving, out_part, *down_parts = phase(leaving, out_part, *down_parts)
-    layer_output = (resid + far_sums(here, *down_parts)).astype(BF16)
+    leaving, out_part, down_out = phase(leaving, out_part, down_out)
+    down_parts = near_sums(here, *loose_parts(down_out))
     out_term = scatter_line(here, after(out_part, ffn_term))
 
     mixer_grads, logit_grad = recurrence_backward(
@@ -730,9 +736,15 @@
         count,
         flags,
     )
-    mixer_grads, layer_output = phase(mixer_grads, layer_output)
     grads = jnp.concatenate([mixer_grads, outgate_grad], axis=1)
     in_part = dot_cols(grads, w_mixer).astype(BF16)
+    attn_gain_here = jnp.sum(in_part.astype(F32) * (wide_in * wide_scale), axis=0)
+    ffn_back = send_quarters(here, ffn_term.reshape(4, rows_d, 2 * quarter))
+    in_part, out_term, down_top, down_top_in, down_low, down_low_in, *ffn_back = phase(
+        in_part, out_term, *down_parts, *ffn_back
+    )
+    down_parts = down_top, down_top_in, down_low, down_low_in
+    layer_output = (resid + far_sums(here, *down_parts)).astype(BF16)
 
     bias_term = jnp.sum(logit_grad.astype(F32), axis=0)
     up_rank_term = dot_rows(rank_low, logit_grad)
@@ -743,7 +755,6 @@
     rank_grad = lax.dynamic_slice_in_dim(rank_part, here.seq * tok, tok, 0).astype(BF16)
     down_rank_term = dot_rows(normed_in, rank_grad)
     rank_in_grad = dot_cols(rank_grad, full_down_rank)
-    attn_gain_here = jnp.sum(in_part.astype(F32) * (wide_in * wide_scale), axis=0)
     attn_gain_term = jnp.sum(rank_in_grad * (inputs * scale_in), axis=0)
 
     zero_bias = jnp.zeros((HEADS * HK,), F32)
@@ -772,13 +783,12 @@
         ((0, 0), (0, 4 * rows_d * small_cols - small_size)),
     ).reshape(-1, small_cols)
     wide_grads = jnp.pad(grads, ((0, 0), (0, small_cols)))
-    mixer_part = dot_rows(x_in, after(wide_grads, in_part)).astype(BF16)
+    mixer_part = dot_rows(x_in, wide_grads).astype(BF16)
     mixer_part = lax.dynamic_update_slice(mixer_part, small_part.astype(BF16), (0, grads.shape[1]))
-    mixer_part, ffn_term, out_term = phase(mixer_part, ffn_term, out_term)
+    mixer_part, out_term = phase(mixer_part, out_term)
     mixer_term = scatter_line(here, mixer_part)
-    *in_parts, ffn_term = phase(*in_parts, ffn_term)
+    *in_parts, layer_output = phase(*in_parts, layer_output)
     in_grad = far_sums(here, *in_parts)
-    ffn_back = send_quarters(here, ffn_term.reshape(4, rows_d, 2 * quarter))
 
     input_grad, _ = norm_backward(
         in_grad,
@@ -792,7 +802,6 @@
 
     down_grad = down_term.astype(F32)
     out_grad = here.swap_top(out_term).astype(F32)
-    input_grad, out_grad, *ffn_back = phase(input_grad, out_grad, *ffn_back)
     ffn_back = join_quarters(here, *ffn_back).astype(F32)
 
     def hidden_last(g):
@@ -805,7 +814,9 @@
     gate_out = hidden_last(ffn_back[:, :, :quarter])
     up_out = hidden_last(ffn_back[:, :, quarter:])
     small_sum = mixer_term[:, 2 * HK + 2 * HV :].reshape(-1).astype(F32)
-    mixer_term = after(mixer_term[:, : 2 * HK + 2 * HV], gate_out, up_out, out_grad, down_grad)
+    mixer_term = after(
+        mixer_term[:, : 2 * HK + 2 * HV], gate_out, up_out, out_grad, down_grad
+    )
     mixer_back = send_quarters(here, mixer_term.reshape(4, rows_d, -1))
     mixer_back = join_quarters(here, *mixer_back).astype(F32)
 

time: 735 us -> 721 us (0.981)
  starting transfers between devices: 113 us -> 92.8 us
  waiting for transfers between devices: 223 us -> 211 us
  matrix products: 148 us -> 158 us
    ppermute x63, starting transfers between devices: 112 us -> 91.7 us  [send(): return lax.ppermute(value, BOTH, pairs)]
    ppermute x63, waiting for transfers between devices: 220 us -> 211 us  [send(): return lax.ppermute(value, BOTH, pairs)]
    unnamed x216 -> x212, local copies, waits for them, and re-layouts: 35.5 us -> 27.6 us
    dot_general x6 -> x7, matrix products: 53.2 us -> 56.8 us  [dot_cols(): lax.dot_general(left, right, (((1,), (1,)), ((), ())), preferred_element_...]
  transfers between devices with their start and end apart: 71 -> 71, of which waited for: 37 -> 35; matrix products, arithmetic and copies ran while one was open for 44% -> 48% of each run, Pallas kernels for 3% -> 3%
where the time goes in v3:
time: 721 us; the launch traced here: 714 us
  waiting for transfers between devices  211 us (29%)
  matrix products  158 us (22%)
  local copies, waits for them, and re-layouts  140 us (19%)
  starting transfers between devices  92.8 us (13%)
  other arithmetic  71.3 us (10%)
  Pallas kernels  23.6 us (3%)
  between operations  16.9 us (2%)
    ppermute x63, waiting for transfers between devices, send(): return lax.ppermute(value, BOTH, pairs)  211 us
    ppermute x63, starting transfers between devices, send(): return lax.ppermute(value, BOTH, pairs)  91.7 us
    dot_general x7, matrix products, dot_cols(): lax.dot_general(left, right, (((1,), (1,)), ((), ())), preferred_element_...  56.8 us
    dot_general x6, matrix products, dot(): return jnp.dot(left, right, preferred_element_type=F32)  47.9 us
    dot_general x6, matrix products, dot_rows(): lax.dot_general(left, right, (((0,), (0,)), ((), ())), preferred_element_...  45.2 us
    unnamed x212, local copies, waits for them, and re-layouts  27.6 us
    pallas_call x1, Pallas kernels, recurrence_backward(): pl.pallas_call(kernel, grid=(segments, per_seg), in_specs=[pl.BlockSpec((...  16.7 us
  transfers between devices with their start and end apart: 71, of which 35 were waited for; matrix products, arithmetic and copies ran while one was open for 48% of the time, Pallas kernels for 3%

profile of v3, /device:TPU:0, one launch (start us, length us, event | category | flops | bytes accessed | tf_op | source)
XLA Modules:
  0.0 714.2 jit_solution(414688456138455256)
XLA Ops:
  20.4 14.5 %collective-permute-start = (bf16[64,1536]{1,0:T(8,128)(2,1)S(1)}, bf16[64,1536]{1,0:T(8,128)(2,1)S(1)}, u32[]{:S(2)}, u32[]{:S(2)}) collective-permute-start(bf16[64,1536]{1,0:T(8,128)(2,1)S(1)} %bitcast.710), channel_id=1, source_target_pairs={{0,2},{1,3},{2,0},{3,1},{4,6},{5,7},{6,4},{7,5},{8,10},{9,11},{10,... | collective-permute-start | bytes 589832 | tf_op jit(solution)/shard_map/ppermute | solution.py:59
  51.0 5.2 reshape.1570
  85.0 13.8 %collective-permute-done.10 = bf16[2,128,2048]{2,1,0:T(8,128)(2,1)} collective-permute-done((bf16[2,128,2048]{2,1,0:T(8,128)(2,1)}, bf16[2,128,2048]{2,1,0:T(8,128)(2,1)}, u32[]{:S(2)}, u32[]{:S(2)}) %collective-permute-start.10) | collective-permute-done | bytes 1048608 | tf_op jit(solution)/shard_map/ppermute | solution.py:59
  133.7 12.9 %fusion.123 = (bf16[1024,1536]{1,0:T(8,128)(2,1)S(1)}, f32[1024,1536]{1,0:T(8,128)}) fusion(bf16[1024,2048]{1,0:T(8,128)(2,1)} %multiply_convert_fusion.1, bf16[2048,1536]{1,0:T(8,128)(2,1)} %all-gather.7.cloned.1.call-done), kind=kOutput, calls=%fused_computation.477 | convolution fusion | flops 6444023808 | bytes 19922944 | tf_op jit(solution)/shard_map/dot_general | solution.py:20
  151.2 16.1 %collective-permute-done.16 = bf16[256,2048]{1,0:T(8,128)(2,1)} collective-permute-done((bf16[256,2048]{1,0:T(8,128)(2,1)S(1)}, bf16[256,2048]{1,0:T(8,128)(2,1)}, u32[]{:S(2)}, u32[]{:S(2)}) %collective-permute-start.16) | collective-permute-done | bytes 1048608 | tf_op jit(solution)/shard_map/ppermute | solution.py:59
  169.9 9.0 %collective-permute-start.21 = (bf16[272,256]{1,0:T(8,128)(2,1)S(1)}, bf16[272,256]{1,0:T(8,128)(2,1)S(1)}, u32[]{:S(2)}, u32[]{:S(2)}) collective-permute-start(bf16[272,256]{1,0:T(8,128)(2,1)S(1)} %fusion.88), channel_id=1, source_target_pairs={{0,12},{1,13},{2,14},{3,15},{16,28},{17,29},{18,30},{19,31}} | collective-permute-start | bytes 417800 | tf_op jit(solution)/shard_map/ppermute | solution.py:59
  184.8 7.0 collective-permute-done.19
  191.9 5.7 collective-permute-done.20
  215.8 21.9 %collective-permute-done.23 = bf16[2,128,2048]{2,1,0:T(8,128)(2,1)} collective-permute-done((bf16[2,128,2048]{2,1,0:T(8,128)(2,1)}, bf16[2,128,2048]{2,1,0:T(8,128)(2,1)}, u32[]{:S(2)}, u32[]{:S(2)}) %collective-permute-start.23) | collective-permute-done | bytes 1048608 | tf_op jit(solution)/shard_map/ppermute | solution.py:59
  243.1 9.6 %collective-permute-done.24 = bf16[128,2048]{1,0:T(8,128)(2,1)S(1)} collective-permute-done((bf16[128,2048]{1,0:T(8,128)(2,1)S(1)}, bf16[128,2048]{1,0:T(8,128)(2,1)S(1)}, u32[]{:S(2)}, u32[]{:S(2)}) %collective-permute-start.24) | collective-permute-done | bytes 524320 | tf_op jit(solution)/shard_map/ppermute | solution.py:59
  259.6 8.5 %collective-permute-done.27 = bf16[128,2048]{1,0:T(8,128)(2,1)S(1)} collective-permute-done((bf16[128,2048]{1,0:T(8,128)(2,1)S(1)}, bf16[128,2048]{1,0:T(8,128)(2,1)S(1)}, u32[]{:S(2)}, u32[]{:S(2)}) %collective-permute-start.27) | collective-permute-done | bytes 524320 | tf_op jit(solution)/shard_map/ppermute | solution.py:59
  276.7 15.5 %collective-permute-done.28 = bf16[2,128,2048]{2,1,0:T(8,128)(2,1)S(1)} collective-permute-done((bf16[2,128,2048]{2,1,0:T(8,128)(2,1)S(1)}, bf16[2,128,2048]{2,1,0:T(8,128)(2,1)S(1)}, u32[]{:S(2)}, u32[]{:S(2)}) %collective-permute-start.28) | collective-permute-done | bytes 1048608 | tf_op jit(solution)/shard_map/ppermute | solution.py:59
  293.2 18.9 %fusion.58 = f32[1024,2816]{1,0:T(8,128)S(1)} fusion(bf16[2048,2816]{1,0:T(8,128)(2,1)} %all-gather.9.cloned.1.call-done, bf16[256,2048]{1,0:T(8,128)(2,1)} %bitcast.115, bf16[256,2048]{1,0:T(8,128)(2,1)} %bitcast.689, bf16[256,2048]{1,0:T(8,128)(2,1)} %bitcast.738, bf16[256,2048]{1,0:T(8,128)(2,1)} %bitcast.687), kind=kOutput, calls=%fused_computation.210 | convolution fusion | flops 11827937280 | bytes 27262976 | tf_op jit(solution)/shard_map/dot_general | solution.py:20
  319.0 8.1 %convolution_convert_fusion.2 = bf16[1408,2048]{1,0:T(8,128)(2,1)} fusion(bf16[1024,1408]{1,0:T(8,128)(2,1)S(1)} %multiply_convert_fusion.4, bf16[1024,2048]{1,0:T(8,128)(2,1)S(1)} %copy-done.73), kind=kOutput, calls=%fused_computation.7 | convolution fusion | flops 5908463616 | bytes 12845056 | tf_op jit(solution)/shard_map/dot_general | solution.py:24
  327.4 14.3 %multiply_convert_fusion.3 = (bf16[1024,1408]{1,0:T(8,128)(2,1)S(1)}, bf16[1024,1408]{1,0:T(8,128)(2,1)S(1)}) fusion(f32[1024,2816]{1,0:T(8,128)} %copy-done.19, bf16[1024,2048]{1,0:T(8,128)(2,1)} %copy-done.72, bf16[1408,2048]{1,0:T(8,128)(2,1)} %all-gather.11.cloned.1.call-done), kind=kOutput, calls=%fused_computation.10 | convolution fusion | flops 5924323328 | bytes 27262976 | tf_op jit(solution)/shard_map/dot_general | solution.py:28
  345.2 9.0 %convolution_convert_fusion.7 = bf16[512,2048]{1,0:T(8,128)(2,1)S(1)} fusion(bf16[512,2816]{1,0:T(8,128)(2,1)S(1)} %bitcast.678, bf16[2048,2816]{1,0:T(8,128)(2,1)} %all-gather.9.cloned.1.call-done), kind=kOutput, calls=%fused_computation.24 | convolution fusion | flops 5906628608 | bytes 16515072 | tf_op jit(solution)/shard_map/dot_general | solution.py:28
  357.6 17.9 %convolution_convert_fusion = bf16[2048,2816]{1,0:T(8,128)(2,1)} fusion(bf16[256,2048]{1,0:T(8,128)(2,1)} %bitcast.115, bf16[256,2048]{1,0:T(8,128)(2,1)} %bitcast.690, bf16[256,2048]{1,0:T(8,128)(2,1)} %bitcast.739, bf16[256,2048]{1,0:T(8,128)(2,1)} %bitcast.688, bf16[1024,1408]{1,0:T(8,128)(2,1)} %copy-done.45, bf16[1024,1408]{1,0:T(8,128)(2,1)S(1)} %get-tuple-element.236), kind=kOutput, calls=%fused_computation | convolution fusion | flops 11845238784 | bytes 21495808 | tf_op jit(solution)/shard_map/dot_general | solution.py:24
  375.5 10.0 %convolution_convert_fusion.8 = bf16[512,2048]{1,0:T(8,128)(2,1)S(1)} fusion(bf16[512,2816]{1,0:T(8,128)(2,1)} %bitcast.677, bf16[2048,2816]{1,0:T(8,128)(2,1)} %all-gather.9.cloned.1.call-done), kind=kOutput, calls=%fused_computation.25 | convolution fusion | flops 5906628608 | bytes 16515072 | tf_op jit(solution)/shard_map/dot_general | solution.py:28
  391.2 7.4 %collective-permute-done.33 = bf16[128,2048]{1,0:T(8,128)(2,1)S(1)} collective-permute-done((bf16[128,2048]{1,0:T(8,128)(2,1)S(1)}, bf16[128,2048]{1,0:T(8,128)(2,1)S(1)}, u32[]{:S(2)}, u32[]{:S(2)}) %collective-permute-start.33) | collective-permute-done | bytes 524320 | tf_op jit(solution)/shard_map/ppermute | solution.py:59
  410.6 9.8 %collective-permute-done.36 = bf16[128,2048]{1,0:T(8,128)(2,1)S(1)} collective-permute-done((bf16[128,2048]{1,0:T(8,128)(2,1)S(1)}, bf16[128,2048]{1,0:T(8,128)(2,1)S(1)}, u32[]{:S(2)}, u32[]{:S(2)}) %collective-permute-start.36) | collective-permute-done | bytes 524320 | tf_op jit(solution)/shard_map/ppermute | solution.py:59
  422.7 10.8 %convolution_convert_fusion.4 = bf16[1024,2048]{1,0:T(8,128)(2,1)} fusion(bf16[1024,1408]{1,0:T(8,128)(2,1)S(1)} %copy-done.43, bf16[1408,2048]{1,0:T(8,128)(2,1)} %all-gather.11.cloned.1.call-done), kind=kOutput, calls=%fused_computation.18 | convolution fusion | flops 5907677184 | bytes 12845056 | tf_op jit(solution)/shard_map/dot_general | solution.py:20
  433.6 7.7 %collective-permute-done.37 = bf16[2,128,2048]{2,1,0:T(8,128)(2,1)S(1)} collective-permute-done((bf16[2,128,2048]{2,1,0:T(8,128)(2,1)S(1)}, bf16[2,128,2048]{2,1,0:T(8,128)(2,1)S(1)}, u32[]{:S(2)}, u32[]{:S(2)}) %collective-permute-start.37) | collective-permute-done | bytes 1048608 | tf_op jit(solution)/shard_map/ppermute | solution.py:59
  444.6 5.9 fusion.21
  469.6 13.2 %collective-permute-done.40 = bf16[272,256]{1,0:T(8,128)(2,1)} collective-permute-done((bf16[272,256]{1,0:T(8,128)(2,1)}, bf16[272,256]{1,0:T(8,128)(2,1)}, u32[]{:S(2)}, u32[]{:S(2)}) %collective-permute-start.40) | collective-permute-done | bytes 139296 | tf_op jit(solution)/shard_map/ppermute | solution.py:59
  484.4 10.0 %collective-permute-done.41 = bf16[272,256]{1,0:T(8,128)(2,1)S(1)} collective-permute-done((bf16[272,256]{1,0:T(8,128)(2,1)}, bf16[272,256]{1,0:T(8,128)(2,1)S(1)}, u32[]{:S(2)}, u32[]{:S(2)}) %collective-permute-start.41) | collective-permute-done | bytes 139296 | tf_op jit(solution)/shard_map/ppermute | solution.py:59
  495.6 5.0 convolution_convert_fusion.6
  515.3 16.7 %shard_map.291 = (bf16[1024,1024]{1,0:T(8,128)(2,1)}, bf16[1024,256]{1,0:T(8,128)(2,1)}) custom-call(f32[2,512,256]{2,1,0:T(8,128)} %reverse_select_fusion.leaving_ref, bf16[16,64,512]{2,1,0:T(8,128)(2,1)} %bitcast.646, bf16[16,64,512]{2,1,0:T(8,128)(2,1)} %bitcast.639, bf16[16,64,256]{2,1,0:T(8,128)(2,1)} %get-tuple-element.259.exp_ref, ...), custom_call_target="tpu_custom_call" | custom-call | flops 1342177280 | bytes 10121216 | tf_op jit(solution)/shard_map/pallas_call | solution.py:445
  537.6 13.3 %multiply_reduce_fusion = (f32[2048]{0:T(1024)S(1)}, bf16[1024,2048]{1,0:T(8,128)(2,1)}) fusion(f32[1024]{0:T(1024)S(1)} %bitcast.717, bf16[1,2,128,2048]{3,2,1,0:T(8,128)(2,1)S(1)} %copy-done.18, bf16[1,2,128,2048]{3,2,1,0:T(8,128)(2,1)S(1)} %copy-done.16, bf16[1,2,128,2048]{3,2,1,0:T(8,128)(2,1)S(1)} %copy-done.14, ...), kind=kOutput, calls=%fused_computation.2 | convolution fusion | flops 6467614720 | bytes 17838080 | tf_op jit(solution)/shard_map/dot_general | solution.py:28
  565.9 12.4 %convolution_convert_fusion.1 = bf16[2048,1664]{1,0:T(8,128)(2,1)} fusion(bf16[1024,2048]{1,0:T(8,128)(2,1)} %multiply_convert_fusion.1, bf16[1024,1536]{1,0:T(8,128)(2,1)} %pad_maximum_fusion.4), kind=kOutput, calls=%fused_computation.6 | convolution fusion | flops 6982729728 | bytes 14155776 | tf_op jit(solution)/shard_map/dot_general | solution.py:24
  592.6 5.8 collective-permute-done.48
  627.8 19.2 %collective-permute-done.53 = bf16[2,128,2048]{2,1,0:T(8,128)(2,1)S(1)} collective-permute-done((bf16[2,128,2048]{2,1,0:T(8,128)(2,1)S(1)}, bf16[2,128,2048]{2,1,0:T(8,128)(2,1)S(1)}, u32[]{:S(2)}, u32[]{:S(2)}) %collective-permute-start.53) | collective-permute-done | bytes 1048608 | tf_op jit(solution)/shard_map/ppermute | solution.py:59
  657.5 4.9 reshape.1609
  (641 shorter events, 337.2 us)
Async XLA Ops:
  7.2 57.1 %all-gather.5.cloned.1.call-start = ((), (), s32[]{:S(2)}) async-start(), calls=%async_computation.4 | async-start | bytes 2654208 | tf_op jit(solution)/shard_map/all_gather | solution.py:174
  14.0 119.7 %all-gather.7.cloned.1.call-start = ((), (), s32[]{:S(2)}) async-start(), calls=%async_computation.5 | async-start | bytes 7077888 | tf_op jit(solution)/shard_map/all_gather | solution.py:174
  20.4 19.9 %collective-permute-start = (bf16[64,1536]{1,0:T(8,128)(2,1)S(1)}, bf16[64,1536]{1,0:T(8,128)(2,1)S(1)}, u32[]{:S(2)}, u32[]{:S(2)}) collective-permute-start(bf16[64,1536]{1,0:T(8,128)(2,1)S(1)} %bitcast.710), channel_id=1, source_target_pairs={{0,2},{1,3},{2,0},{3,1},{4,6},{5,7},{6,4},{7,5},{8,10},{9,11},{10,... | collective-permute-start | bytes 589832 | tf_op jit(solution)/shard_map/ppermute | solution.py:59
  46.1 247.1 %all-gather.9.cloned.1.call-start = ((), (), s32[]{:S(2)}) async-start(), calls=%async_computation.6 | async-start | bytes 12976128 | tf_op jit(solution)/shard_map/all_gather | solution.py:174
  76.0 22.8 %collective-permute-start.10 = (bf16[2,128,2048]{2,1,0:T(8,128)(2,1)}, bf16[2,128,2048]{2,1,0:T(8,128)(2,1)}, u32[]{:S(2)}, u32[]{:S(2)}) collective-permute-start(bf16[2,128,2048]{2,1,0:T(8,128)(2,1)} %pad_maximum_fusion.14), channel_id=1, source_target_pairs={{0,2},{1,3},{2,0},{3,1},{4,6},{5,7},{6,4},{7,5},{8,10},{9,11},{10,... | collective-permute-start | bytes 3145736 | tf_op jit(solution)/shard_map/ppermute | solution.py:59
  77.1 22.6 %collective-permute-start.9 = (bf16[2,128,2048]{2,1,0:T(8,128)(2,1)}, bf16[2,128,2048]{2,1,0:T(8,128)(2,1)}, u32[]{:S(2)}, u32[]{:S(2)}) collective-permute-start(bf16[2,128,2048]{2,1,0:T(8,128)(2,1)} %pad_maximum_fusion.13), channel_id=1, source_target_pairs={{0,16},{1,17},{2,18},{3,19},{4,20},{5,21},{6,22},{7,23},{8,24},{9,... | collective-permute-start | bytes 3145736 | tf_op jit(solution)/shard_map/ppermute | solution.py:59
  115.0 212.3 %all-gather.11.cloned.1.call-start = ((), (), s32[]{:S(2)}) async-start(), calls=%async_computation.7 | async-start | bytes 6488064 | tf_op jit(solution)/shard_map/all_gather | solution.py:174
  125.0 26.2 %collective-permute-start.15 = (bf16[256,2048]{1,0:T(8,128)(2,1)S(1)}, bf16[256,2048]{1,0:T(8,128)(2,1)}, u32[]{:S(2)}, u32[]{:S(2)}) collective-permute-start(bf16[256,2048]{1,0:T(8,128)(2,1)S(1)} %copy-done.3), channel_id=1, source_target_pairs={{0,2},{1,3},{2,0},{3,1},{4,6},{5,7},{6,4},{7,5},{8,10},{9,11},{10,... | collective-permute-start | bytes 3145736 | tf_op jit(solution)/shard_map/ppermute | solution.py:59
  126.1 41.3 %collective-permute-start.16 = (bf16[256,2048]{1,0:T(8,128)(2,1)S(1)}, bf16[256,2048]{1,0:T(8,128)(2,1)}, u32[]{:S(2)}, u32[]{:S(2)}) collective-permute-start(bf16[256,2048]{1,0:T(8,128)(2,1)S(1)} %copy-done.3), channel_id=1, source_target_pairs={{0,16},{1,17},{2,18},{3,19},{4,20},{5,21},{6,22},{7,23},{8,24},{9,... | collective-permute-start | bytes 3145736 | tf_op jit(solution)/shard_map/ppermute | solution.py:59
  127.6 39.8 %collective-permute-start.17 = (bf16[256,2048]{1,0:T(8,128)(2,1)S(1)}, bf16[256,2048]{1,0:T(8,128)(2,1)}, u32[]{:S(2)}, u32[]{:S(2)}) collective-permute-start(bf16[256,2048]{1,0:T(8,128)(2,1)S(1)} %copy-done.3), channel_id=1, source_target_pairs={{0,18},{1,19},{2,16},{3,17},{4,22},{5,23},{6,20},{7,21},{8,26},{9,... | collective-permute-start | bytes 3145736 | tf_op jit(solution)/shard_map/ppermute | solution.py:59
  169.9 27.8 %collective-permute-start.21 = (bf16[272,256]{1,0:T(8,128)(2,1)S(1)}, bf16[272,256]{1,0:T(8,128)(2,1)S(1)}, u32[]{:S(2)}, u32[]{:S(2)}) collective-permute-start(bf16[272,256]{1,0:T(8,128)(2,1)S(1)} %fusion.88), channel_id=1, source_target_pairs={{0,12},{1,13},{2,14},{3,15},{16,28},{17,29},{18,30},{19,31}} | collective-permute-start | bytes 417800 | tf_op jit(solution)/shard_map/ppermute | solution.py:59
  212.2 25.5 %collective-permute-start.23 = (bf16[2,128,2048]{2,1,0:T(8,128)(2,1)}, bf16[2,128,2048]{2,1,0:T(8,128)(2,1)}, u32[]{:S(2)}, u32[]{:S(2)}) collective-permute-start(bf16[2,128,2048]{2,1,0:T(8,128)(2,1)} %fusion.42), channel_id=1, source_target_pairs={{0,2},{1,3},{2,0},{3,1},{4,6},{5,7},{6,4},{7,5},{8,10},{9,11},{10,... | collective-permute-start | bytes 3145736 | tf_op jit(solution)/shard_map/ppermute | solution.py:59
  213.9 189.5 %reduce-scatter.5.cloned.1.call-start = ((), (), s32[]{:S(2)}) async-start(), calls=%async_computation.8 | async-start | bytes 6488064 | tf_op jit(solution)/shard_map/reduce_scatter | solution.py:178
  214.4 26.6 %collective-permute-start.25 = (bf16[2,128,2048]{2,1,0:T(8,128)(2,1)}, bf16[2,128,2048]{2,1,0:T(8,128)(2,1)S(1)}, u32[]{:S(2)}, u32[]{:S(2)}) collective-permute-start(bf16[2,128,2048]{2,1,0:T(8,128)(2,1)} %get-tuple-element.270), channel_id=1, source_target_pairs={{0,16},{1,17},{2,18},{3,19},{4,20},{5,21},{6,22},{7,23},{8,24},{9,... | collective-permute-start | bytes 3145736 | tf_op jit(solution)/shard_map/ppermute | solution.py:59
  268.2 24.0 %collective-permute-start.28 = (bf16[2,128,2048]{2,1,0:T(8,128)(2,1)S(1)}, bf16[2,128,2048]{2,1,0:T(8,128)(2,1)S(1)}, u32[]{:S(2)}, u32[]{:S(2)}) collective-permute-start(bf16[2,128,2048]{2,1,0:T(8,128)(2,1)S(1)} %pad_maximum_fusion.19), channel_id=1, source_target_pairs={{0,16},{1,17},{2,18},{3,19},{4,20},{5,21},{6,22},{7,23},{8,24},{9,... | collective-permute-start | bytes 3145736 | tf_op jit(solution)/shard_map/ppermute | solution.py:59
  271.3 21.8 %collective-permute-start.30 = (bf16[2,128,2048]{2,1,0:T(8,128)(2,1)S(1)}, bf16[2,128,2048]{2,1,0:T(8,128)(2,1)}, u32[]{:S(2)}, u32[]{:S(2)}) collective-permute-start(bf16[2,128,2048]{2,1,0:T(8,128)(2,1)S(1)} %pad_maximum_fusion.20), channel_id=1, source_target_pairs={{0,2},{1,3},{2,0},{3,1},{4,6},{5,7},{6,4},{7,5},{8,10},{9,11},{10,... | collective-permute-start | bytes 3145736 | tf_op jit(solution)/shard_map/ppermute | solution.py:59
  327.1 232.4 %reduce-scatter.7.cloned.1.call-start = ((), (), s32[]{:S(2)}) async-start(), calls=%async_computation.9 | async-start | bytes 12976128 | tf_op jit(solution)/shard_map/reduce_scatter | solution.py:178
  355.7 30.1 %collective-permute-start.31 = (bf16[2,128,2048]{2,1,0:T(8,128)(2,1)}, bf16[2,128,2048]{2,1,0:T(8,128)(2,1)}, u32[]{:S(2)}, u32[]{:S(2)}) collective-permute-start(bf16[2,128,2048]{2,1,0:T(8,128)(2,1)} %bitcast.126), channel_id=1, source_target_pairs={{0,2},{1,3},{2,0},{3,1},{4,6},{5,7},{6,4},{7,5},{8,10},{9,11},{10,... | collective-permute-start | bytes 3145736 | tf_op jit(solution)/shard_map/ppermute | solution.py:59
  357.1 28.7 %collective-permute-start.32 = (bf16[2,128,2048]{2,1,0:T(8,128)(2,1)}, bf16[2,128,2048]{2,1,0:T(8,128)(2,1)}, u32[]{:S(2)}, u32[]{:S(2)}) collective-permute-start(bf16[2,128,2048]{2,1,0:T(8,128)(2,1)} %bitcast.128), channel_id=1, source_target_pairs={{0,16},{1,17},{2,18},{3,19},{4,20},{5,21},{6,22},{7,23},{8,24},{9,... | collective-permute-start | bytes 3145736 | tf_op jit(solution)/shard_map/ppermute | solution.py:59
  403.4 195.0 %reduce-scatter.9.cloned.1.call-start = ((), (), s32[]{:S(2)}) async-start(), calls=%async_computation.10 | async-start | bytes 2359296 | tf_op jit(solution)/shard_map/reduce_scatter | solution.py:178
  420.6 20.7 %collective-permute-start.37 = (bf16[2,128,2048]{2,1,0:T(8,128)(2,1)S(1)}, bf16[2,128,2048]{2,1,0:T(8,128)(2,1)S(1)}, u32[]{:S(2)}, u32[]{:S(2)}) collective-permute-start(bf16[2,128,2048]{2,1,0:T(8,128)(2,1)S(1)} %pad_maximum_fusion.21), channel_id=1, source_target_pairs={{0,16},{1,17},{2,18},{3,19},{4,20},{5,21},{6,22},{7,23},{8,24},{9,... | collective-permute-start | bytes 3145736 | tf_op jit(solution)/shard_map/ppermute | solution.py:59
  459.9 34.5 %collective-permute-start.42 = (bf16[272,256]{1,0:T(8,128)(2,1)}, bf16[272,256]{1,0:T(8,128)(2,1)}, u32[]{:S(2)}, u32[]{:S(2)}) collective-permute-start(bf16[272,256]{1,0:T(8,128)(2,1)} %fusion.89), channel_id=1, source_target_pairs={{12,0},{13,1},{14,2},{15,3},{28,16},{29,17},{30,18},{31,19}} | collective-permute-start | bytes 417800 | tf_op jit(solution)/shard_map/ppermute | solution.py:59
  461.2 21.6 %collective-permute-start.40 = (bf16[272,256]{1,0:T(8,128)(2,1)}, bf16[272,256]{1,0:T(8,128)(2,1)}, u32[]{:S(2)}, u32[]{:S(2)}) collective-permute-start(bf16[272,256]{1,0:T(8,128)(2,1)} %fusion.89), channel_id=1, source_target_pairs={{4,0},{5,1},{6,2},{7,3},{8,4},{9,5},{10,6},{11,7},{12,8},{13,9},{1... | collective-permute-start | bytes 417800 | tf_op jit(solution)/shard_map/ppermute | solution.py:59
  462.5 31.9 %collective-permute-start.41 = (bf16[272,256]{1,0:T(8,128)(2,1)}, bf16[272,256]{1,0:T(8,128)(2,1)S(1)}, u32[]{:S(2)}, u32[]{:S(2)}) collective-permute-start(bf16[272,256]{1,0:T(8,128)(2,1)} %fusion.89), channel_id=1, source_target_pairs={{8,0},{9,1},{10,2},{11,3},{12,4},{13,5},{14,6},{15,7},{24,16},{25,... | collective-permute-start | bytes 417800 | tf_op jit(solution)/shard_map/ppermute | solution.py:59
  511.0 81.1 %collective-permute-start.44 = (bf16[2,128,2048]{2,1,0:T(8,128)(2,1)}, bf16[2,128,2048]{2,1,0:T(8,128)(2,1)}, u32[]{:S(2)}, u32[]{:S(2)}) collective-permute-start(bf16[2,128,2048]{2,1,0:T(8,128)(2,1)} %get-tuple-element.257), channel_id=1, source_target_pairs={{0,2},{1,3},{2,0},{3,1},{4,6},{5,7},{6,4},{7,5},{8,10},{9,11},{10,... | collective-permute-start | bytes 3145736 | tf_op jit(solution)/shard_map/ppermute | solution.py:59
  513.7 78.5 %collective-permute-start.45 = (bf16[2,128,2048]{2,1,0:T(8,128)(2,1)}, bf16[2,128,2048]{2,1,0:T(8,128)(2,1)}, u32[]{:S(2)}, u32[]{:S(2)}) collective-permute-start(bf16[2,128,2048]{2,1,0:T(8,128)(2,1)} %get-tuple-element.255), channel_id=1, source_target_pairs={{0,16},{1,17},{2,18},{3,19},{4,20},{5,21},{6,22},{7,23},{8,24},{9,... | collective-permute-start | bytes 3145736 | tf_op jit(solution)/shard_map/ppermute | solution.py:59
  559.5 130.2 %reduce-scatter.11.cloned.1.call-start = ((), (), s32[]{:S(2)}) async-start(), calls=%async_computation.11 | async-start | bytes 7667712 | tf_op jit(solution)/shard_map/reduce_scatter | solution.py:178
  601.0 80.2 %collective-permute-start.59 = (bf16[64,2048]{1,0:T(8,128)(2,1)}, bf16[64,2048]{1,0:T(8,128)(2,1)}, u32[]{:S(2)}, u32[]{:S(2)}) collective-permute-start(bf16[64,2048]{1,0:T(8,128)(2,1)} %reduce-scatter.9.cloned.1.call-done), channel_id=1, source_target_pairs={{0,0},{1,1},{2,8},{3,9},{4,4},{5,5},{6,12},{7,13},{8,2},{9,3},{10,... | collective-permute-start | bytes 786440 | tf_op jit(solution)/shard_map/ppermute | solution.py:59
  613.9 33.0 %collective-permute-start.53 = (bf16[2,128,2048]{2,1,0:T(8,128)(2,1)S(1)}, bf16[2,128,2048]{2,1,0:T(8,128)(2,1)S(1)}, u32[]{:S(2)}, u32[]{:S(2)}) collective-permute-start(bf16[2,128,2048]{2,1,0:T(8,128)(2,1)S(1)} %get-tuple-element.253), channel_id=1, source_target_pairs={{0,2},{1,3},{2,0},{3,1},{4,6},{5,7},{6,4},{7,5},{8,10},{9,11},{10,... | collective-permute-start | bytes 3145736 | tf_op jit(solution)/shard_map/ppermute | solution.py:59
  616.0 30.9 %collective-permute-start.54 = (bf16[2,128,2048]{2,1,0:T(8,128)(2,1)S(1)}, bf16[2,128,2048]{2,1,0:T(8,128)(2,1)S(1)}, u32[]{:S(2)}, u32[]{:S(2)}) collective-permute-start(bf16[2,128,2048]{2,1,0:T(8,128)(2,1)S(1)} %get-tuple-element.249), channel_id=1, source_target_pairs={{0,16},{1,17},{2,18},{3,19},{4,20},{5,21},{6,22},{7,23},{8,24},{9,... | collective-permute-start | bytes 3145736 | tf_op jit(solution)/shard_map/ppermute | solution.py:59
  649.5 33.7 %collective-permute-start.57 = (bf16[128,2048]{1,0:T(8,128)(2,1)}, bf16[128,2048]{1,0:T(8,128)(2,1)}, u32[]{:S(2)}, u32[]{:S(2)}) collective-permute-start(bf16[128,2048]{1,0:T(8,128)(2,1)} %fusion.70), channel_id=1, source_target_pairs={{0,16},{1,17},{2,18},{3,19},{4,20},{5,21},{6,22},{7,23},{8,24},{9,... | collective-permute-start | bytes 1572872 | tf_op jit(solution)/shard_map/ppermute | solution.py:59
  653.2 31.1 %collective-permute-start.58 = (bf16[128,2048]{1,0:T(8,128)(2,1)}, bf16[128,2048]{1,0:T(8,128)(2,1)}, u32[]{:S(2)}, u32[]{:S(2)}) collective-permute-start(bf16[128,2048]{1,0:T(8,128)(2,1)} %fusion.71), channel_id=1, source_target_pairs={{0,2},{1,3},{2,0},{3,1},{4,6},{5,7},{6,4},{7,5},{8,10},{9,11},{10,... | collective-permute-start | bytes 1572872 | tf_op jit(solution)/shard_map/ppermute | solution.py:59
  (132 other events, 1328.6 us)
Sparse Core Ops, SparseCore 0:
  14.2 44.7 all-gather.4
  61.2 63.9 all-gather.6
  127.4 110.0 all-gather.8
  239.0 66.9 all-gather.10
  327.2 72.2 reduce-scatter.4
  403.6 135.8 reduce-scatter.6
  559.7 33.6 reduce-scatter.8
  598.6 75.0 reduce-scatter.10
